TPU v7x, 256 devices: a whole 4x4x8 slice. The times are simulated.
256 devices in a mesh: dp: 32 (over x, z), tensor: 8 (over y, core).
Axes of the slice: x: 4, y: 4, z: 8, core: 2. Of those that a mesh axis runs over, the one named last changes fastest.
Arguments:
- grads: bfloat16 [32, 2, 512, 8192], P('dp', None, 'tensor'), may hold values from -6 to 6
- errors: bfloat16 [32, 2, 512, 8192], P('dp', None, 'tensor'), may hold values from -3 to 3
- q_init: bfloat16 [2, 8192, 32], replicated, may hold values from -6 to 6
Outputs:
- error_new: bfloat16 [32, 2, 512, 8192], P('dp', None, 'tensor')
- q_new: float32 [2, 8192, 32], replicated
- orthonormal: float32 [2, 512, 32], P(None, 'tensor')
All inputs are finite; a program needn't handle non-finite values.
Results may differ from a plain program's by a relative error of at most 0.012.
Values sent between devices are 32-bit elements; how exact they have to be, the bound alone decides.
No kernel may reach another device: no remote copies, remote signals or barrier semaphores. Data moves between devices by JAX's collectives and lax.ppermute only.
A program may use at most 64 MiB of HBM per device.

v0:
```python
import jax
import jax.numpy as jnp
from jax import lax
from jax.sharding import PartitionSpec as P


def local(grads, errors, q_init):
    merged = (grads[0].astype(jnp.float32) + errors[0].astype(jnp.float32)).astype(jnp.bfloat16)
    partial_value = jnp.einsum("mrc,mck->mrk", merged, q_init, preferred_element_type=jnp.float32)
    summed = lax.psum(partial_value, "dp")
    gram_local = jnp.einsum("mrk,mrl->mkl", summed, summed, precision=lax.Precision.HIGHEST)
    gram_matrix = lax.psum(gram_local, "tensor")
    columns = []
    for matrix_index in range(summed.shape[0]):
        factor = jnp.linalg.cholesky(gram_matrix[matrix_index])
        solved = lax.linalg.triangular_solve(
            factor, summed[matrix_index].T, left_side=True, lower=True
        )
        columns.append(solved.T)
    orthonormal = jnp.stack(columns)
    rounded_p = orthonormal.astype(jnp.bfloat16)
    q_partial = jnp.einsum("mrc,mrk->mck", merged, rounded_p, preferred_element_type=jnp.float32)
    q_total = lax.psum(q_partial, ("dp", "tensor"))
    q_new = q_total / lax.axis_size("dp")
    rounded_q = q_new.astype(jnp.bfloat16)
    approx = jnp.einsum("mrk,mck->mrc", rounded_p, rounded_q, preferred_element_type=jnp.float32)
    error_new = (merged.astype(jnp.float32) - approx).astype(jnp.bfloat16)
    return (error_new[None], q_new, orthonormal)


def solution(mesh):
    placed = (P("dp", None, "tensor", None), P("dp", None, "tensor", None), P())
    return jax.shard_map(
        local,
        mesh=mesh,
        in_specs=placed,
        out_specs=(P("dp", None, "tensor", None), P(), P(None, "tensor", None)),
        check_vma=False,
    )
```

profile of v0, /device:TPU:1, one launch (start us, length us, event | category | flops | bytes accessed | tf_op | source)
XLA Modules:
  0.0 461.1 jit_solution(15442054493076861567)
XLA Ops:
  7.2 0.0 copy-start
  7.2 0.0 copy-start.1
  7.2 0.0 all-reduce.2.cloned.1.call-start
  7.2 1.2 copy-done
  8.4 2.9 fusion.14
  11.3 118.7 %psum.21 = f32[2,64,32]{1,2,0:T(8,128)S(1)} all-reduce(f32[2,64,32]{1,2,0:T(8,128)S(1)} %fusion.14), channel_id=1, replica_groups=mesh['dp'=32,'tensor'=8] {'dp'}, use_global_device_ids=true, to_apply=%region_0.0 | all-reduce | flops 4096 | bytes 32768 | tf_op jit(solution)/shard_map/psum | solution.py:10
  129.9 0.2 fusion.16
  130.1 48.6 %psum.22 = f32[2,32,32]{1,2,0:T(8,128)S(1)} all-reduce(f32[2,32,32]{1,2,0:T(8,128)S(1)} %fusion.16), channel_id=1, replica_groups=mesh['dp'=32,'tensor'=8] {'tensor'}, use_global_device_ids=true, to_apply=%region_1.0 | all-reduce | flops 2048 | bytes 16384 | tf_op jit(solution)/shard_map/psum | solution.py:12
  178.8 0.1 copy.7
  178.8 0.1 copy.8
  178.9 2.9 cholesky.44
  181.9 0.6 compare_reduce_fusion.1
  182.5 0.7 fusion.4
  183.2 2.4 custom-call.6
  185.6 0.2 convolution_bitcast_fusion.1
  185.9 2.9 cholesky.55
  188.8 0.6 compare_reduce_fusion
  189.4 0.7 fusion.5
  190.1 2.4 custom-call.7
  192.5 0.2 convolution_bitcast_fusion
  192.8 0.0 copy-done.1
  192.8 0.0 copy-start.4
  192.8 3.5 fusion.11
  196.4 0.0 all-reduce.2.cloned.1.call-update
  196.4 253.4 %all-reduce.2.cloned.1.call-done = f32[2,8192,32]{1,2,0:T(8,128)} async-done(((f32[2,8192,32]{1,2,0:T(8,128)}), f32[2,8192,32]{1,2,0:T(8,128)}) %all-reduce.2.cloned.1.call-update) | async-done | bytes 2097168 | tf_op jit(solution)/shard_map/psum | solution.py:23
  449.8 0.0 copy-start.2
  449.8 1.9 broadcast_multiply_fusion
  451.7 0.0 copy-done.4
  451.7 0.3 copy-done.2
  452.0 0.0 copy-start.3
  452.0 2.2 fusion.1
  454.3 0.0 copy-done.3
  (5 shorter events, 0.1 us)
Async XLA Ops:
  7.2 1.2 copy-start
  7.2 185.6 %copy-start.1 = (bf16[1,2,64,8192]{3,2,1,0:T(8,128)(2,1)S(1)}, bf16[1,2,64,8192]{3,2,1,0:T(8,128)(2,1)}, u32[]{:S(2)}) copy-start(bf16[1,2,64,8192]{3,2,1,0:T(8,128)(2,1)} %param.7) | copy-start | bytes 6291460
  7.2 442.6 %all-reduce.2.cloned.1.call-start = ((), (), s32[]{:S(2)}) async-start(), calls=%async_computation | async-start | bytes 4194304 | tf_op jit(solution)/shard_map/psum | solution.py:23
  192.8 258.9 %copy-start.4 = (f32[2,64,32]{1,2,0:T(8,128)}, f32[2,64,32]{1,2,0:T(8,128)S(1)}, u32[]{:S(2)}) copy-start(f32[2,64,32]{1,2,0:T(8,128)S(1)} %pad_maximum_fusion) | copy-start | bytes 49156
  449.8 2.2 copy-start.2
  452.0 2.2 copy-start.3
Sparse Core Ops, SparseCore 0:
  196.5 253.2 all-reduce.1
where the time goes:
time: 462 us; the launch traced here: 461 us
  waiting for transfers between devices  253 us (55%)
  blocking collectives  167 us (36%)
  other arithmetic  15.3 us (3%)
  between operations  14.1 us (3%)
  matrix products  9.27 us (2%)
    psum x1, waiting for transfers between devices, local(): q_total = lax.psum(q_partial, ('dp', 'tensor'))  253 us
    psum x1, blocking collectives, local(): summed = lax.psum(partial_value, 'dp')  119 us
    psum x1, blocking collectives, local(): gram_matrix = lax.psum(gram_local, 'tensor')  48.6 us
  transfers between devices with their start and end apart: 1, of which 1 were waited for; matrix products, arithmetic and copies ran while one was open for 0% of the time, Pallas kernels for 0%

commit v1 on v0

v1 whole, which is shorter than its diff:
```python
import jax
import jax.numpy as jnp
from jax import lax
from jax.sharding import Mesh
from jax.sharding import PartitionSpec as P

NX, NZ, NY, NC = 4, 8, 4, 2
COLS, R, MATS, ROWS = 8192, 32, 2, 64
SPAN = COLS // (NX * NZ)


def split3(a):
    high = a.astype(jnp.bfloat16)
    rest = a - high.astype(jnp.float32)
    middle = rest.astype(jnp.bfloat16)
    low = (rest - middle.astype(jnp.float32)).astype(jnp.bfloat16)
    return high, middle, low


def swap(a):
    return lax.ppermute(a, "c", [(0, 1), (1, 0)])


def local(grads, errors, q_init):
    core = lax.axis_index("c")
    merged = (grads[0].astype(jnp.float32) + errors[0].astype(jnp.float32)).astype(jnp.bfloat16)
    terms = jnp.einsum("mck,mrc->kmr", q_init, merged, preferred_element_type=jnp.float32)
    terms = terms.reshape(R, MATS * ROWS)
    summed = jnp.sum(lax.all_gather(terms, "x"), axis=0)
    summed = jnp.sum(lax.all_gather(summed, "z"), axis=0)
    summed = summed.reshape(R, MATS, ROWS).transpose(1, 0, 2)

    pieces = jnp.concatenate(split3(summed), axis=1)
    products = jnp.einsum("mkr,mrc->mkc", pieces, merged, preferred_element_type=jnp.float32)
    products = products.reshape(MATS, 3, R, COLS)
    t_terms = products[:, 0] + (products[:, 1] + products[:, 2])

    gram = jnp.einsum("mkr,mlr->mkl", summed, summed, precision=lax.Precision.HIGHEST)
    gram = gram.reshape(MATS * R * R // 128, 128)
    gram = gram + swap(gram)
    gram = jnp.sum(lax.all_gather(gram, "y"), axis=0).reshape(MATS, R, R)
    factor = jnp.linalg.cholesky(gram)
    eye = jnp.broadcast_to(jnp.eye(R, dtype=jnp.float32), (MATS, R, R))
    inverse = lax.linalg.triangular_solve(factor, eye, left_side=True, lower=True)
    ortho = jnp.einsum("mkl,mlr->mrk", inverse, summed, precision=lax.Precision.HIGHEST)
    rounded_p = ortho.astype(jnp.bfloat16)

    mine = lax.dynamic_index_in_dim(t_terms, core, 0, keepdims=False)
    other = lax.dynamic_index_in_dim(t_terms, 1 - core, 0, keepdims=False)
    half = mine + swap(other)
    rows = jnp.sum(lax.all_to_all(half.reshape(NY, R // NY, COLS), "y", 0, 0), axis=0)
    blocks = rows.reshape(R // NY, NX * NZ, SPAN).transpose(1, 0, 2)
    own = jnp.sum(lax.all_to_all(blocks, ("x", "z"), 0, 0), axis=0)

    blocks = lax.all_to_all(jnp.broadcast_to(own[None], blocks.shape), ("x", "z"), 0, 0)
    rows = blocks.transpose(1, 0, 2).reshape(R // NY, COLS)
    half = lax.all_gather(rows, "y").reshape(R, COLS)
    inverse_mine = lax.dynamic_index_in_dim(inverse, core, 0, keepdims=False)
    q_mine = jnp.dot(inverse_mine, half, precision=lax.Precision.HIGHEST) / (NX * NZ)
    q_other = swap(q_mine)
    q_t = jnp.where(core == 0, jnp.stack([q_mine, q_other]), jnp.stack([q_other, q_mine]))
    rounded_q = q_t.astype(jnp.bfloat16)
    approx = jnp.einsum("mrk,mkc->mrc", rounded_p, rounded_q, preferred_element_type=jnp.float32)
    error_new = (merged.astype(jnp.float32) - approx).astype(jnp.bfloat16)
    return (error_new[None], q_t.transpose(0, 2, 1), ortho)


def solution(mesh):
    fine = Mesh(mesh.devices.reshape(NX, NZ, NY, NC), ("x", "z", "y", "c"))
    big = P(("x", "z"), None, ("y", "c"), None)
    return jax.shard_map(
        local,
        mesh=fine,
        in_specs=(big, big, P()),
        out_specs=(big, P(), P(None, ("y", "c"), None)),
        check_vma=False,
    )
```

time: 462 us -> 167 us (0.36)
  waiting for transfers between devices: 253 us -> 5.91 us
  blocking collectives: 167 us -> 90.7 us
  starting transfers between devices: 0.04 us -> 17.2 us
  other arithmetic: 15.3 us -> 20.5 us
  matrix products: 9.27 us -> 13.9 us
    psum x1 -> x0, waiting for transfers between devices: 253 us -> none  [local(): q_total = lax.psum(q_partial, ('dp', 'tensor'))]
    psum x2 -> x0, blocking collectives: 167 us -> none  [the longest x1 119 us: local(): summed = lax.psum(partial_value, 'dp')]
    all_to_all x0 -> x3, blocking collectives: none -> 49.4 us  [the longest x1 18.3 us: local(): lax.all_to_all(half.reshape(NY, R // NY, COLS), 'y', 0, 0)]
    all_gather x0 -> x3, blocking collectives: none -> 41.3 us  [the longest x1 21.8 us: local(): summed = jnp.sum(lax.all_gather(summed, 'z'), axis=0)]
    ppermute x0 -> x3, starting transfers between devices: none -> 17.2 us  [swap(): return lax.ppermute(a, 'c', [(0, 1), (1, 0)])]
    ppermute x0 -> x3, waiting for transfers between devices: none -> 5.88 us  [swap(): return lax.ppermute(a, 'c', [(0, 1), (1, 0)])]
    dot_general x4 -> x6, matrix products: 8.8 us -> 13.7 us  [the longest x1 4.65 us: local(): jnp.einsum('mrk,mkc->mrc', rounded_p, rounded_q, preferred_element_type=j...]
    another operation x11 -> x7, other arithmetic: 13.4 us -> 11 us  [the longest x4 6.02 us: local(): factor = jnp.linalg.cholesky(gram)]
  transfers between devices with their start and end apart: 1 -> 4, of which waited for: 1 -> 3; matrix products, arithmetic and copies ran while one was open for 0% -> 7% of each run, Pallas kernels for 0% -> 0%
where the time goes in v1:
time: 167 us; the launch traced here: 166 us
  blocking collectives  90.7 us (54%)
  other arithmetic  20.5 us (12%)
  starting transfers between devices  17.2 us (10%)
  between operations  14.2 us (9%)
  matrix products  13.9 us (8%)
  waiting for transfers between devices  5.91 us (4%)
  local copies, waits for them, and re-layouts  3.91 us (2%)
    all_gather x1, blocking collectives, local(): summed = jnp.sum(lax.all_gather(summed, 'z'), axis=0)  21.8 us
    all_to_all x1, blocking collectives, local(): lax.all_to_all(half.reshape(NY, R // NY, COLS), 'y', 0, 0)  18.3 us
    ppermute x3, starting transfers between devices, swap(): return lax.ppermute(a, 'c', [(0, 1), (1, 0)])  17.2 us
    all_to_all x1, blocking collectives, local(): own = jnp.sum(lax.all_to_all(blocks, ('x', 'z'), 0, 0), axis=0)  16.4 us
    all_to_all x1, blocking collectives, local(): lax.all_to_all(jnp.broadcast_to(own[None], blocks.shape), ('x', 'z'), 0, 0)  14.7 us
    all_gather x1, blocking collectives, local(): summed = jnp.sum(lax.all_gather(terms, 'x'), axis=0)  10.1 us
    all_gather x1, blocking collectives, local(): gram = jnp.sum(lax.all_gather(gram, 'y'), axis=0).reshape(MATS, R, R)  9.37 us
    another operation x4, other arithmetic, local(): factor = jnp.linalg.cholesky(gram)  6.02 us
  transfers between devices with their start and end apart: 4, of which 3 were waited for; matrix products, arithmetic and copies ran while one was open for 7% of the time, Pallas kernels for 0%

profile of v1, /device:TPU:1, one launch (start us, length us, event | category | flops | bytes accessed | tf_op | source)
XLA Modules:
  0.0 166.4 jit_solution(4621679228074726690)
XLA Ops:
  7.2 0.0 copy-start
  7.2 0.0 copy-start.1
  7.2 0.0 all-gather.4.cloned.1.call-start
  7.2 1.2 copy-done
  8.4 2.9 %convolution_bitcast_fusion = f32[32,2,64]{2,0,1:T(8,128)S(1)} fusion(bf16[2,8192,32]{1,2,0:T(8,128)(2,1)S(1)} %copy-done, bf16[1,2,64,8192]{3,2,1,0:T(8,128)(2,1)} %param.4, bf16[1,2,64,8192]{3,2,1,0:T(8,128)(2,1)} %param.3), kind=kOutput, calls=%fused_computation.11 | convolution fusion | flops 71303168 | bytes 5259264 | tf_op jit(solution)/shard_map/mck,mrc->kmr/dot_general | solution.py:27
  11.3 0.1 all_gather_reshape.6
  11.4 10.1 %all_gather.18 = f32[4,32,128]{2,1,0:T(8,128)S(1)} all-gather(f32[1,32,128]{2,1,0:T(8,128)S(1)} %all_gather_reshape.6), channel_id=1, replica_groups=mesh['x'=4,'z'=8,'y'=4,'c'=2] {'x'}, dimensions={0}, use_global_device_ids=true | all-gather | bytes 81920 | tf_op jit(solution)/shard_map/all_gather | solution.py:29
  21.6 21.8 %all-gather = f32[256,128]{1,0:T(8,128)S(1)} all-gather(f32[32,128]{1,0:T(8,128)S(1)} %reduce_sum.45), channel_id=2, replica_groups=mesh['x'=4,'z'=8,'y'=4,'c'=2] {'z'}, dimensions={0}, use_global_device_ids=true | all-gather | bytes 147456 | tf_op jit(solution)/shard_map/all_gather | solution.py:30
  43.4 0.1 reshape.48
  43.5 0.0 copy-done.1
  43.6 2.6 %fusion.10 = f32[2,96,8192]{2,1,0:T(8,128)S(1)} fusion(bf16[2,32,64]{2,1,0:T(8,128)(2,1)S(1)} %get-tuple-element.4, bf16[2,32,64]{2,1,0:T(8,128)(2,1)S(1)} %get-tuple-element.3, bf16[2,32,64]{2,1,0:T(8,128)(2,1)S(1)} %bitcast.71, bf16[1,2,64,8192]{3,2,1,0:T(8,128)(2,1)S(1)} %copy-done.1, bf16[1,2,64,8192]{3,2,1,0:T(8,128)(2,1)} %param.3), kind=kOutput, calls=%fused_computation.17 | convolution fusion | flops 205594624 | bytes 10510336 | tf_op jit(solution)/shard_map/mkr,mrc->mkc/dot_general | solution.py:34
  46.1 1.6 fusion.3
  47.8 2.3 %dynamic-slice_bitcast_fusion = f32[32,8192]{1,0:T(8,128)} fusion(f32[2,1,32,8192]{3,2,1,0:T(8,128)} %fusion.3, s32[]{:T(128)S(6)} %select_n.24), kind=kLoop, calls=%fused_computation.15 | loop fusion | bytes 2097156 | tf_op jit(solution)/shard_map/jit(dynamic_index_in_dim)/squeeze | solution.py:49
  50.0 9.9 %collective-permute-start.1 = (f32[32,8192]{1,0:T(8,128)}, f32[32,8192]{1,0:T(8,128)}, u32[]{:S(2)}, u32[]{:S(2)}) collective-permute-start(f32[32,8192]{1,0:T(8,128)} %dynamic-slice_bitcast_fusion), channel_id=1, source_target_pairs={{0,1},{1,0},{2,3},{3,2},{4,5},{5,4},{6,7},{7,6},{8,9},{9,8},{10,11... | collective-permute-start | bytes 3145736 | tf_op jit(solution)/shard_map/ppermute | solution.py:21
  59.9 2.6 %collective-permute-done.1 = f32[32,8192]{1,0:T(8,128)} collective-permute-done((f32[32,8192]{1,0:T(8,128)}, f32[32,8192]{1,0:T(8,128)}, u32[]{:S(2)}, u32[]{:S(2)}) %collective-permute-start.1) | collective-permute-done | bytes 1048608 | tf_op jit(solution)/shard_map/ppermute | solution.py:21
  62.6 1.6 fusion.8
  64.2 18.3 %all_to_all.15 = f32[4,8,8192]{2,1,0:T(8,128)} all-to-all(f32[4,8,8192]{2,1,0:T(8,128)S(1)} %fusion.8), channel_id=1, replica_groups=mesh['x'=4,'z'=8,'y'=4,'c'=2] {'y'}, dimensions={0} | all-to-all | bytes 2097152 | tf_op jit(solution)/shard_map/all_to_all | solution.py:51
  82.5 1.3 reduce_sum.48
  83.9 16.4 %all_to_all.16 = f32[32,8,256]{2,1,0:T(8,128)} all-to-all(f32[32,8,256]{2,1,0:T(8,128)S(1)} %bitcast.67), channel_id=1, replica_groups=mesh['x'=4,'z'=8,'y'=4,'c'=2] {'x','z'}, dimensions={0} | all-to-all | bytes 524288 | tf_op jit(solution)/shard_map/all_to_all | solution.py:53
  100.2 1.0 reduce_sum.49
  101.3 14.7 %all_to_all.17 = f32[32,8,256]{2,1,0:T(8,128)} all-to-all(f32[32,8,256]{2,1,0:T(8,128)S(1)} %broadcast_in_dim.17), channel_id=1, replica_groups=mesh['x'=4,'z'=8,'y'=4,'c'=2] {'x','z'}, dimensions={0} | all-to-all | bytes 524288 | tf_op jit(solution)/shard_map/all_to_all | solution.py:55
  115.9 0.0 all-gather.4.cloned.1.call-update
  115.9 0.2 fusion.21
  116.1 0.1 reshape.49
  116.2 4.4 %collective-permute-start = (f32[16,128]{1,0:T(8,128)S(1)}, f32[16,128]{1,0:T(8,128)S(1)}, u32[]{:S(2)}, u32[]{:S(2)}) collective-permute-start(f32[16,128]{1,0:T(8,128)S(1)} %reshape.49), channel_id=1, source_target_pairs={{0,1},{1,0},{2,3},{3,2},{4,5},{5,4},{6,7},{7,6},{8,9},{9,8},{10,11... | collective-permute-start | bytes 24584 | tf_op jit(solution)/shard_map/ppermute | solution.py:21
  120.6 0.8 collective-permute-done
  121.4 9.4 %all-gather.1 = f32[64,128]{1,0:T(8,128)S(1)} all-gather(f32[16,128]{1,0:T(8,128)S(1)} %add.40), channel_id=3, replica_groups=mesh['x'=4,'z'=8,'y'=4,'c'=2] {'y'}, dimensions={0}, use_global_device_ids=true | all-gather | bytes 40960 | tf_op jit(solution)/shard_map/all_gather | solution.py:41
  130.8 0.1 reshape.50
  130.8 0.1 copy.36
  130.9 5.9 %custom-call.7 = f32[2,32,32]{2,1,0:T(8,128)S(1)} custom-call(f32[2,32,32]{2,1,0:T(8,128)S(1)} %fusion.18), custom_call_target="Cholesky" | custom-call | tf_op jit(solution)/shard_map/jit(cholesky)/cholesky | solution.py:42
  136.8 0.1 compare_reduce_fusion
  136.9 0.1 select_bitcast_fusion
  137.0 4.9 %custom-call.8 = f32[2,1,32,32]{2,3,1,0:T(8,128)S(1)} custom-call(f32[2,1,32,32]{3,2,1,0:T(8,128)S(1)} %select_bitcast_fusion), custom_call_target="InvertDiagBlocksLowerTriangular" | custom-call | tf_op jit(solution)/shard_map/triangular_solve | solution.py:44
  141.9 0.3 fusion.16
  142.2 0.0 all-gather.4.cloned.1.call-done
  142.2 3.3 %convolution_multiply_fusion = f32[32,8192]{1,0:T(8,128)} fusion(f32[4,8,8192]{2,1,0:T(8,128)} %all-gather.4.cloned.1.call-done, f32[2,32,32]{2,1,0:T(8,128)S(1)} %fusion.16, s32[]{:T(128)S(6)} %select_n.23), kind=kOutput, calls=%fused_computation.3 | convolution fusion | flops 100925440 | bytes 2113540 | tf_op jit(solution)/shard_map/dot_general | solution.py:59
  145.5 2.9 %collective-permute-start.2 = (f32[32,8192]{1,0:T(8,128)}, f32[32,8192]{1,0:T(8,128)}, u32[]{:S(2)}, u32[]{:S(2)}) collective-permute-start(f32[32,8192]{1,0:T(8,128)} %convolution_multiply_fusion), channel_id=1, source_target_pairs={{0,1},{1,0},{2,3},{3,2},{4,5},{5,4},{6,7},{7,6},{8,9},{9,8},{10,11... | collective-permute-start | bytes 3145736 | tf_op jit(solution)/shard_map/ppermute | solution.py:21
  148.4 0.2 fusion.19
  148.6 0.0 copy-start.3
  148.6 2.4 %collective-permute-done.2 = f32[32,8192]{1,0:T(8,128)} collective-permute-done((f32[32,8192]{1,0:T(8,128)}, f32[32,8192]{1,0:T(8,128)}, u32[]{:S(2)}, u32[]{:S(2)}) %collective-permute-start.2) | collective-permute-done | bytes 1048608 | tf_op jit(solution)/shard_map/ppermute | solution.py:21
  151.0 0.0 copy-start.2
  151.0 3.9 %fusion.4 = f32[2,8192,32]{1,2,0:T(8,128)} fusion(f32[1,32,8192]{2,1,0:T(8,128)} %bitcast.18, f32[1,32,8192]{2,1,0:T(8,128)} %bitcast.19, pred[]{:T(512)S(6)} %eq.4), kind=kLoop, calls=%fused_computation.9 | loop fusion | flops 1572864 | bytes 4194305 | tf_op jit(solution)/shard_map/transpose | solution.py:65
  154.9 0.0 copy-done.3
  154.9 0.0 copy-done.2
  154.9 4.6 %fusion.1 = bf16[1,2,64,8192]{3,2,1,0:T(8,128)(2,1)} fusion(f32[1,32,8192]{2,1,0:T(8,128)} %bitcast.18, f32[1,32,8192]{2,1,0:T(8,128)} %bitcast.19, pred[]{:T(512)S(6)} %eq.4, f32[2,64,32]{1,2,0:T(8,128)S(1)} %fusion.19, bf16[1,2,64,8192]{3,2,1,0:T(8,128)(2,1)S(1)} %copy-done.1, bf16[1,2,64,8192]{3,2,1,0:T(8,128)(2,1)S(1)} %copy-done.2), kind=kOutput, calls=%fused_computation.2 | convolution fusion | flops 76025856 | bytes 8404993 | tf_op jit(solution)/shard_map/mrk,mkc->mrc/dot_general | solution.py:63
  (13 shorter events, 0.2 us)
Async XLA Ops:
  7.2 1.2 copy-start
  7.2 36.4 %copy-start.1 = (bf16[1,2,64,8192]{3,2,1,0:T(8,128)(2,1)S(1)}, bf16[1,2,64,8192]{3,2,1,0:T(8,128)(2,1)}, u32[]{:S(2)}) copy-start(bf16[1,2,64,8192]{3,2,1,0:T(8,128)(2,1)} %param.4) | copy-start | bytes 6291460
  7.2 135.0 %all-gather.4.cloned.1.call-start = ((), (), s32[]{:S(2)}) async-start(), calls=%async_computation.3 | async-start | bytes 1310720 | tf_op jit(solution)/shard_map/all_gather | solution.py:57
  50.0 12.6 %collective-permute-start.1 = (f32[32,8192]{1,0:T(8,128)}, f32[32,8192]{1,0:T(8,128)}, u32[]{:S(2)}, u32[]{:S(2)}) collective-permute-start(f32[32,8192]{1,0:T(8,128)} %dynamic-slice_bitcast_fusion), channel_id=1, source_target_pairs={{0,1},{1,0},{2,3},{3,2},{4,5},{5,4},{6,7},{7,6},{8,9},{9,8},{10,11... | collective-permute-start | bytes 3145736 | tf_op jit(solution)/shard_map/ppermute | solution.py:21
  116.2 5.2 %collective-permute-start = (f32[16,128]{1,0:T(8,128)S(1)}, f32[16,128]{1,0:T(8,128)S(1)}, u32[]{:S(2)}, u32[]{:S(2)}) collective-permute-start(f32[16,128]{1,0:T(8,128)S(1)} %reshape.49), channel_id=1, source_target_pairs={{0,1},{1,0},{2,3},{3,2},{4,5},{5,4},{6,7},{7,6},{8,9},{9,8},{10,11... | collective-permute-start | bytes 24584 | tf_op jit(solution)/shard_map/ppermute | solution.py:21
  145.5 5.5 %collective-permute-start.2 = (f32[32,8192]{1,0:T(8,128)}, f32[32,8192]{1,0:T(8,128)}, u32[]{:S(2)}, u32[]{:S(2)}) collective-permute-start(f32[32,8192]{1,0:T(8,128)} %convolution_multiply_fusion), channel_id=1, source_target_pairs={{0,1},{1,0},{2,3},{3,2},{4,5},{5,4},{6,7},{7,6},{8,9},{9,8},{10,11... | collective-permute-start | bytes 3145736 | tf_op jit(solution)/shard_map/ppermute | solution.py:21
  148.6 6.3 %copy-start.3 = (f32[2,64,32]{1,2,0:T(8,128)}, f32[2,64,32]{1,2,0:T(8,128)S(1)}, u32[]{:S(2)}) copy-start(f32[2,64,32]{1,2,0:T(8,128)S(1)} %fusion.19) | copy-start | bytes 49156
  151.0 3.9 %copy-start.2 = (bf16[1,2,64,8192]{3,2,1,0:T(8,128)(2,1)S(1)}, bf16[1,2,64,8192]{3,2,1,0:T(8,128)(2,1)}, u32[]{:S(2)}) copy-start(bf16[1,2,64,8192]{3,2,1,0:T(8,128)(2,1)} %param.3) | copy-start | bytes 6291460
Sparse Core Ops, SparseCore 0:
  116.1 23.7 all-gather.3

commit v2 on v0

v2 whole, which is shorter than its diff:
```python
import jax
import jax.numpy as jnp
from jax import lax
from jax.experimental import pallas as pl
from jax.experimental.pallas import tpu as pltpu
from jax.sharding import Mesh
from jax.sharding import PartitionSpec as P

NX, NZ, NY, NC = 4, 8, 4, 2
COLS, R, MATS, ROWS = 8192, 32, 2, 64
WIDE = COLS // NX
SPAN = WIDE // NZ
HIGH = lax.Precision.HIGHEST
VMEM_LIMIT = 32 * 1024 * 1024


def swap(a):
    return lax.ppermute(a, "c", [(0, 1), (1, 0)])


def shifts(a, axis, size):
    return [lax.ppermute(a, axis, [(i, (i + s) % size) for i in range(size)]) for s in range(1, size)]


def copies_to_all(a, axes, count):
    return lax.all_to_all(jnp.broadcast_to(a[None], (count,) + a.shape), axes, 0, 0)


def merge(grads_ref, errors_ref):
    total = grads_ref[...].astype(jnp.float32) + errors_ref[...].astype(jnp.float32)
    return total.astype(jnp.bfloat16).reshape(ROWS, WIDE)


def right_terms(which_ref, summed_ref, grads_ref, errors_ref):
    both = summed_ref[...]
    value = jnp.where(which_ref[0] == 0, both[:, :ROWS], both[:, ROWS:])
    high = value.astype(jnp.bfloat16)
    rest = value - high.astype(jnp.float32)
    middle = rest.astype(jnp.bfloat16)
    low = (rest - middle.astype(jnp.float32)).astype(jnp.bfloat16)
    pieces = jnp.concatenate([high, middle, low], axis=0)
    products = jnp.dot(pieces, merge(grads_ref, errors_ref), preferred_element_type=jnp.float32)
    return products[:R] + (products[R : 2 * R] + products[2 * R :])


def first_half_kernel(which_ref, summed_ref, grads_ref, errors_ref, out_ref):
    out_ref[...] = right_terms(which_ref, summed_ref, grads_ref, errors_ref)


def second_half_kernel(which_ref, summed_ref, grads_ref, errors_ref, received_ref, out_ref):
    terms = right_terms(which_ref, summed_ref, grads_ref, errors_ref) + received_ref[...]
    out_ref[...] = terms.reshape(NY, 1, R // NY, WIDE)


MATRIX_BLOCK = pl.BlockSpec((1, 1, ROWS, WIDE), lambda i, which: (0, which[0], 0, i))
COLUMN_BLOCK = pl.BlockSpec((R, WIDE), lambda i, which: (0, i))
SPREAD_BLOCK = pl.BlockSpec((NY, 1, R // NY, WIDE), lambda i, which: (0, i, 0, 0))


def whole(*shape):
    return pl.BlockSpec(shape, lambda i, which: (0,) * len(shape))


def call(kernel, in_specs, out_specs, out_shape, flops, nbytes, aliases=None):
    return pl.pallas_call(
        kernel,
        grid_spec=pltpu.PrefetchScalarGridSpec(
            num_scalar_prefetch=1, grid=(NX,), in_specs=in_specs, out_specs=out_specs
        ),
        out_shape=out_shape,
        input_output_aliases=aliases or {},
        compiler_params=pltpu.CompilerParams(vmem_limit_bytes=VMEM_LIMIT),
        cost_estimate=pl.CostEstimate(flops=flops, bytes_accessed=nbytes, transcendentals=0),
    )


def right_first(which, summed, grads, errors):
    return call(
        first_half_kernel,
        [whole(R, MATS * ROWS), MATRIX_BLOCK, MATRIX_BLOCK],
        COLUMN_BLOCK,
        jax.ShapeDtypeStruct((R, COLS), jnp.float32),
        6 * ROWS * R * COLS,
        3 << 20,
    )(which, summed, grads, errors)


def right_second(which, summed, grads, errors, received):
    return call(
        second_half_kernel,
        [whole(R, MATS * ROWS), MATRIX_BLOCK, MATRIX_BLOCK, COLUMN_BLOCK],
        SPREAD_BLOCK,
        jax.ShapeDtypeStruct((NY, NX, R // NY, WIDE), jnp.float32),
        6 * ROWS * R * COLS,
        4 << 20,
    )(which, summed, grads, errors, received)


def factor_kernel(gram_ref, summed_ref, inverse_ref, ortho_ref):
    grams = gram_ref[0]
    for part in range(1, NY):
        grams = grams + gram_ref[part]
    row = lax.broadcasted_iota(jnp.int32, (R, 2 * R), 0)
    lane = lax.broadcasted_iota(jnp.int32, (R, 2 * R), 1)
    unit = (lane - R == row).astype(jnp.float32)[:, R:]
    states = [jnp.concatenate([grams[m * R : (m + 1) * R], unit], axis=1) for m in range(MATS)]
    for j in range(R):
        for m in range(MATS):
            x = states[m]
            pivot = x[j : j + 1]
            ratio = x[:, j : j + 1] * (1.0 / x[j : j + 1, j : j + 1])
            states[m] = x - jnp.where(row > j, ratio, 0.0) * pivot
    for m in range(MATS):
        x = states[m]
        diagonal = jnp.sum(jnp.where(row == lane, x, 0.0), axis=1, keepdims=True)
        inverse = x[:, R:] / jnp.sqrt(diagonal)
        inverse_ref[m] = inverse
        ortho_ref[m] = jnp.dot(
            inverse,
            summed_ref[:, m * ROWS : (m + 1) * ROWS],
            precision=HIGH,
            preferred_element_type=jnp.float32,
        )


def factors(grams, summed):
    return pl.pallas_call(
        factor_kernel,
        out_shape=(
            jax.ShapeDtypeStruct((MATS, R, R), jnp.float32),
            jax.ShapeDtypeStruct((MATS, R, ROWS), jnp.float32),
        ),
        cost_estimate=pl.CostEstimate(flops=1 << 20, bytes_accessed=12 << 20, transcendentals=0),
    )(grams, summed)


def finish_kernel(which_ref, inverse_ref, total_ref, out_ref):
    total = total_ref[...].reshape(R, WIDE)
    inverse = inverse_ref[0] * (1.0 / (NX * NZ))
    out_ref[...] = jnp.dot(inverse, total, precision=HIGH, preferred_element_type=jnp.float32)


def finish(which, inverse, total):
    return call(
        finish_kernel,
        [pl.BlockSpec((1, R, R), lambda i, which: (which[0], 0, 0)), SPREAD_BLOCK],
        COLUMN_BLOCK,
        jax.ShapeDtypeStruct((R, COLS), jnp.float32),
        2 * R * R * COLS,
        2 << 20,
    )(which, inverse, total)


def error_kernel(which_ref, ortho_ref, q_ref, grads_ref, errors_ref, *refs):
    error_ref, out_ref = refs[-2:]
    q = q_ref[...]
    approx = lax.dot_general(
        ortho_ref[0].astype(jnp.bfloat16),
        q.astype(jnp.bfloat16),
        (((0,), (0,)), ((), ())),
        preferred_element_type=jnp.float32,
    )
    error = merge(grads_ref, errors_ref).astype(jnp.float32) - approx
    error_ref[...] = error.astype(jnp.bfloat16).reshape(1, 1, ROWS, WIDE)
    out_ref[...] = q.reshape(1, R, WIDE)


def error_step(which, ortho, q, grads, errors, before=()):
    out_spec = pl.BlockSpec((1, R, WIDE), lambda i, which: (which[0], 0, i))
    untouched = pl.BlockSpec(memory_space=pl.ANY)
    ortho_spec = pl.BlockSpec((1, R, ROWS), lambda i, which: (which[0], 0, 0))
    return call(
        error_kernel,
        [ortho_spec, COLUMN_BLOCK, MATRIX_BLOCK, MATRIX_BLOCK] + [untouched] * len(before),
        [MATRIX_BLOCK, out_spec],
        (
            jax.ShapeDtypeStruct((1, MATS, ROWS, COLS), jnp.bfloat16),
            jax.ShapeDtypeStruct((MATS, R, COLS), jnp.float32),
        ),
        2 * ROWS * R * COLS,
        5 << 20,
        {5: 0, 6: 1} if before else None,
    )(which, ortho, q, grads, errors, *before)


def local(grads, errors, q_init):
    core = lax.axis_index("c").astype(jnp.int32)
    own = core.reshape(1)
    other = (1 - core).reshape(1)
    merged = (grads[0].astype(jnp.float32) + errors[0].astype(jnp.float32)).astype(jnp.bfloat16)
    terms = jnp.einsum("mck,mrc->kmr", q_init, merged, preferred_element_type=jnp.float32)
    terms = terms.reshape(R, MATS * ROWS)
    terms = jnp.sum(copies_to_all(terms, "x", NX), axis=0)
    summed = jnp.sum(copies_to_all(terms, "z", NZ), axis=0)

    split = summed.reshape(R, MATS, ROWS)
    gram = jnp.einsum("kmr,lmr->mkl", split, split, precision=HIGH).reshape(MATS * R, R)
    gram = gram + swap(gram)
    grams = jnp.stack([gram] + shifts(gram, "y", NY))

    received = swap(right_first(other, summed, grads, errors))
    half = right_second(own, summed, grads, errors, received)
    half = half.reshape(NY * NX, R // NY, WIDE)
    mine = jnp.sum(lax.all_to_all(half, ("y", "x"), 0, 0), axis=0)
    inverse, ortho = factors(grams, summed)
    mine = mine.reshape(R // NY, NZ, SPAN).transpose(1, 0, 2)
    mine = jnp.sum(lax.all_to_all(mine, "z", 0, 0), axis=0)

    total = copies_to_all(mine, "z", NZ).transpose(1, 0, 2).reshape(R // NY, WIDE)
    total = copies_to_all(total, ("y", "x"), NY * NX).reshape(NY, NX, R // NY, WIDE)
    q_own = finish(own, inverse, total)
    q_other = swap(q_own)
    first = error_step(own, ortho, q_own, grads, errors)
    error_new, q_t = error_step(other, ortho, q_other, grads, errors, first)
    return (error_new, q_t.transpose(0, 2, 1), ortho.transpose(0, 2, 1))


def solution(mesh):
    fine = Mesh(mesh.devices.reshape(NX, NZ, NY, NC), ("x", "z", "y", "c"))
    big = P(("x", "z"), None, ("y", "c"), None)
    return jax.shard_map(
        local,
        mesh=fine,
        in_specs=(big, big, P()),
        out_specs=(big, P(), P(None, ("y", "c"), None)),
        check_vma=False,
    )
```

time: 462 us -> 121 us (0.26)
  waiting for transfers between devices: 253 us -> 19.2 us
  blocking collectives: 167 us -> 49.7 us
  starting transfers between devices: 0.04 us -> 24.2 us
  Pallas kernels: 0 us -> 15.5 us
  between operations: 14.1 us -> 0.77 us
  other arithmetic: 15.3 us -> 1.99 us
  matrix products: 9.27 us -> 3.05 us
    psum x1 -> x0, waiting for transfers between devices: 253 us -> none  [local(): q_total = lax.psum(q_partial, ('dp', 'tensor'))]
    psum x2 -> x0, blocking collectives: 167 us -> none  [the longest x1 119 us: local(): summed = lax.psum(partial_value, 'dp')]
    all_to_all x0 -> x4, blocking collectives: none -> 49.7 us  [the longest x1 21.1 us: local(): mine = jnp.sum(lax.all_to_all(half, ('y', 'x'), 0, 0), axis=0)]
    pallas_call x0 -> x6, Pallas kernels: none -> 15.5 us  [the longest x2 4.94 us: error_step(): call(error_kernel, [ortho_spec, COLUMN_BLOCK, MATRIX_BLOCK, MATRIX_BLOCK]...]
    another operation x11 -> x1, other arithmetic: 13.4 us -> 0.67 us  [local(): grams = jnp.stack([gram] + shifts(gram, 'y', NY))]
    all_to_all x0 -> x2, starting transfers between devices: none -> 12.5 us  [copies_to_all(): lax.all_to_all(jnp.broadcast_to(a[None], (count,) + a.shape), axes, 0, 0)]
    ppermute x0 -> x6, starting transfers between devices: none -> 11.7 us  [the longest x3 7.84 us: swap(): return lax.ppermute(a, 'c', [(0, 1), (1, 0)])]
    ppermute x0 -> x6, waiting for transfers between devices: none -> 11.2 us  [the longest x3 8.01 us: shifts(): lax.ppermute(a, axis, [(i, (i + s) % size) for i in range(size)])]
  transfers between devices with their start and end apart: 1 -> 8, of which waited for: 1 -> 6; matrix products, arithmetic and copies ran while one was open for 0% -> 1% of each run, Pallas kernels for 0% -> 6%
where the time goes in v2:
time: 121 us; the launch traced here: 120 us
  blocking collectives  49.7 us (41%)
  starting transfers between devices  24.2 us (20%)
  waiting for transfers between devices  19.2 us (16%)
  Pallas kernels  15.5 us (13%)
  local copies, waits for them, and re-layouts  5.68 us (5%)
  matrix products  3.05 us (3%)
  other arithmetic  1.99 us (2%)
    all_to_all x1, blocking collectives, local(): mine = jnp.sum(lax.all_to_all(half, ('y', 'x'), 0, 0), axis=0)  21.1 us
    all_to_all x2, blocking collectives, copies_to_all(): lax.all_to_all(jnp.broadcast_to(a[None], (count,) + a.shape), axes, 0, 0)  18.8 us
    all_to_all x2, starting transfers between devices, copies_to_all(): lax.all_to_all(jnp.broadcast_to(a[None], (count,) + a.shape), axes, 0, 0)  12.5 us
    all_to_all x1, blocking collectives, local(): mine = jnp.sum(lax.all_to_all(mine, 'z', 0, 0), axis=0)  9.71 us
    all_to_all x2, waiting for transfers between devices, copies_to_all(): lax.all_to_all(jnp.broadcast_to(a[None], (count,) + a.shape), axes, 0, 0)  8.03 us
    ppermute x3, waiting for transfers between devices, shifts(): lax.ppermute(a, axis, [(i, (i + s) % size) for i in range(size)])  8.01 us
    ppermute x3, starting transfers between devices, swap(): return lax.ppermute(a, 'c', [(0, 1), (1, 0)])  7.84 us
    pallas_call x2, Pallas kernels, error_step(): call(error_kernel, [ortho_spec, COLUMN_BLOCK, MATRIX_BLOCK, MATRIX_BLOCK]...  4.94 us
  transfers between devices with their start and end apart: 8, of which 6 were waited for; matrix products, arithmetic and copies ran while one was open for 1% of the time, Pallas kernels for 6%

profile of v2, /device:TPU:1, one launch (start us, length us, event | category | flops | bytes accessed | tf_op | source)
XLA Modules:
  0.0 120.1 jit_solution(13254172655813822047)
XLA Ops:
  0.6 0.0 copy-start
  0.6 0.0 copy-start.1
  0.7 1.2 %copy-done = bf16[2,8192,32]{1,2,0:T(8,128)(2,1)S(1)} copy-done((bf16[2,8192,32]{1,2,0:T(8,128)(2,1)S(1)}, bf16[2,8192,32]{1,2,0:T(8,128)(2,1)}, u32[]{:S(2)}) %copy-start) | copy-done | bytes 1048600
  1.9 2.9 %fusion.3 = f32[32,2,64]{2,0,1:T(8,128)S(1)} fusion(bf16[2,8192,32]{1,2,0:T(8,128)(2,1)S(1)} %copy-done, bf16[1,2,64,8192]{3,2,1,0:T(8,128)(2,1)} %errors_ref.7, bf16[1,2,64,8192]{3,2,1,0:T(8,128)(2,1)} %grads_ref.7), kind=kOutput, calls=%fused_computation.3 | convolution fusion | flops 71303168 | bytes 5259264 | tf_op jit(solution)/shard_map/mck,mrc->kmr/dot_general | solution.py:191
  4.8 0.1 broadcast_in_dim.12
  4.9 9.1 %all_to_all.30 = f32[4,32,128]{2,1,0:T(8,128)S(1)} all-to-all(f32[4,32,128]{2,1,0:T(8,128)S(1)} %broadcast_in_dim.13), channel_id=1, replica_groups=mesh['x'=4,'z'=8,'y'=4,'c'=2] {'x'}, dimensions={0} | all-to-all | bytes 131072 | tf_op jit(solution)/shard_map/all_to_all | solution.py:26
  14.0 0.7 broadcast_in_dim.28
  14.7 8.2 %all-to-all-start.1 = ((f32[8,32,128]{2,1,0:T(8,128)}), f32[8,32,128]{2,1,0:T(8,128)S(1)}, u32[]{:S(2)}, u32[]{:S(2)}) async-start(f32[8,32,128]{2,1,0:T(8,128)} %broadcast_in_dim.28), calls=%async_computation.1 | async-start | bytes 262144 | tf_op jit(solution)/shard_map/all_to_all | solution.py:26
  22.9 8.0 %all-to-all-done.1 = f32[8,32,128]{2,1,0:T(8,128)S(1)} async-done(((f32[8,32,128]{2,1,0:T(8,128)}), f32[8,32,128]{2,1,0:T(8,128)S(1)}, u32[]{:S(2)}, u32[]{:S(2)}) %all-to-all-start.1) | async-done | bytes 131104 | tf_op jit(solution)/shard_map/all_to_all | solution.py:26
  30.9 0.0 copy-start.4
  30.9 0.0 copy-done.1
  30.9 0.0 copy-start.2
  30.9 1.6 %copy-done.2 = bf16[1,2,64,8192]{3,2,1,0:T(8,128)(2,1)S(1)} copy-done((bf16[1,2,64,8192]{3,2,1,0:T(8,128)(2,1)S(1)}, bf16[1,2,64,8192]{3,2,1,0:T(8,128)(2,1)}, u32[]{:S(2)}) %copy-start.2) | copy-done | bytes 2097176
  32.5 1.5 %shard_map.59 = f32[32,8192]{1,0:T(8,128)S(1)} custom-call(s32[1]{0:T(128)} %bitcast.which_ref, f32[32,128]{1,0:T(8,128)S(1)} %reduce_sum.37.summed_ref, bf16[1,2,64,8192]{3,2,1,0:T(8,128)(2,1)S(1)} %copy-done.2, bf16[1,2,64,8192]{3,2,1,0:T(8,128)(2,1)S(1)} %copy-done.1), custom_call_target="tpu_custom_call" | custom-call | flops 100663296 | bytes 3145728 | tf_op jit(solution)/shard_map/pallas_call | solution.py:78
  34.1 3.5 %collective-permute-start.4 = (f32[32,8192]{1,0:T(8,128)S(1)}, f32[32,8192]{1,0:T(8,128)S(1)}, u32[]{:S(2)}, u32[]{:S(2)}) collective-permute-start(f32[32,8192]{1,0:T(8,128)S(1)} %shard_map.59), channel_id=1, source_target_pairs={{0,1},{1,0},{2,3},{3,2},{4,5},{5,4},{6,7},{7,6},{8,9},{9,8},{10,11... | collective-permute-start | bytes 3145736 | tf_op jit(solution)/shard_map/ppermute | solution.py:18
  37.6 2.3 %collective-permute-done.4.received_ref = f32[32,8192]{1,0:T(8,128)S(1)} collective-permute-done((f32[32,8192]{1,0:T(8,128)S(1)}, f32[32,8192]{1,0:T(8,128)S(1)}, u32[]{:S(2)}, u32[]{:S(2)}) %collective-permute-start.4) | collective-permute-done | bytes 1048608 | tf_op jit(solution)/shard_map/ppermute | solution.py:18
  39.9 1.7 %shard_map.60 = f32[4,4,8,2048]{3,2,1,0:T(8,128)S(1)} custom-call(s32[1]{0:T(128)} %bitcast.8.which_ref, f32[32,128]{1,0:T(8,128)S(1)} %reduce_sum.37.summed_ref, bf16[1,2,64,8192]{3,2,1,0:T(8,128)(2,1)S(1)} %copy-done.2, bf16[1,2,64,8192]{3,2,1,0:T(8,128)(2,1)S(1)} %copy-done.1, f32[32,8192]{1,0:T(8,128)S(1)} %collective-permute-done.4.received_ref), custom_call_target="tpu_custom_call" | custom-call | flops 100663296 | bytes 4194304 | tf_op jit(solution)/shard_map/pallas_call | solution.py:89
  41.5 21.1 %all_to_all.31 = f32[16,8,2048]{2,1,0:T(8,128)} all-to-all(f32[16,8,2048]{2,1,0:T(8,128)S(1)} %bitcast.26), channel_id=1, replica_groups=mesh['x'=4,'z'=8,'y'=4,'c'=2] {'y','x'}, dimensions={0} | all-to-all | bytes 2097152 | tf_op jit(solution)/shard_map/all_to_all | solution.py:204
  62.7 1.3 %reduce_sum.38 = f32[8,2048]{1,0:T(8,128)S(1)} reduce(f32[16,8,2048]{2,1,0:T(8,128)} %all_to_all.31, f32[]{:T(128)} %constant.2.clone.1), dimensions={0}, to_apply=%region_2.0 | reduce | flops 245760 | bytes 1114116 | tf_op jit(solution)/shard_map/reduce_sum | solution.py:204
  64.0 9.7 %all_to_all.32 = f32[8,8,256]{2,1,0:T(8,128)S(1)} all-to-all(f32[8,8,256]{2,1,0:T(8,128)S(1)} %bitcast.29), channel_id=1, replica_groups=mesh['x'=4,'z'=8,'y'=4,'c'=2] {'z'}, dimensions={0} | all-to-all | bytes 131072 | tf_op jit(solution)/shard_map/all_to_all | solution.py:207
  73.7 9.7 %all_to_all.33 = f32[8,8,256]{2,1,0:T(8,128)S(1)} all-to-all(f32[8,8,256]{2,1,0:T(8,128)S(1)} %broadcast_in_dim.29), channel_id=1, replica_groups=mesh['x'=4,'z'=8,'y'=4,'c'=2] {'z'}, dimensions={0} | all-to-all | bytes 131072 | tf_op jit(solution)/shard_map/all_to_all | solution.py:26
  83.4 1.1 broadcast_in_dim.31
  84.5 4.4 %all-to-all-start.5 = ((f32[16,8,2048]{2,1,0:T(8,128)}), f32[16,8,2048]{2,1,0:T(8,128)}, u32[]{:S(2)}, u32[]{:S(2)}) async-start(f32[16,8,2048]{2,1,0:T(8,128)} %broadcast_in_dim.31), calls=%async_computation.5 | async-start | bytes 2097152 | tf_op jit(solution)/shard_map/all_to_all | solution.py:26
  88.8 0.0 copy-done.4
  88.8 0.1 reshape.36
  88.9 0.2 fusion.6
  89.1 3.9 %collective-permute-start = (f32[64,32]{1,0:T(8,128)S(1)}, f32[64,32]{1,0:T(8,128)S(1)}, u32[]{:S(2)}, u32[]{:S(2)}) collective-permute-start(f32[64,32]{1,0:T(8,128)S(1)} %bitcast.31), channel_id=1, source_target_pairs={{0,1},{1,0},{2,3},{3,2},{4,5},{5,4},{6,7},{7,6},{8,9},{9,8},{10,11... | collective-permute-start | bytes 24584 | tf_op jit(solution)/shard_map/ppermute | solution.py:18
  93.0 0.9 collective-permute-done
  93.9 2.7 %collective-permute-start.3 = (f32[64,32]{1,0:T(8,128)S(1)}, f32[64,32]{1,0:T(8,128)S(1)}, u32[]{:S(2)}, u32[]{:S(2)}) collective-permute-start(f32[64,32]{1,0:T(8,128)S(1)} %bitcast_add_fusion), channel_id=1, source_target_pairs={{0,6},{2,0},{4,2},{6,4},{1,7},{3,1},{5,3},{7,5},{8,14},{10,8},{12,... | collective-permute-start | bytes 24584 | tf_op jit(solution)/shard_map/ppermute | solution.py:22
  96.6 0.5 collective-permute-start.2
  97.2 0.6 collective-permute-start.1
  97.8 2.3 %collective-permute-done.3 = f32[64,32]{1,0:T(8,128)S(1)} collective-permute-done((f32[64,32]{1,0:T(8,128)S(1)}, f32[64,32]{1,0:T(8,128)S(1)}, u32[]{:S(2)}, u32[]{:S(2)}) %collective-permute-start.3) | collective-permute-done | bytes 8224 | tf_op jit(solution)/shard_map/ppermute | solution.py:22
  100.1 4.7 %collective-permute-done.2 = f32[64,32]{1,0:T(8,128)S(1)} collective-permute-done((f32[64,32]{1,0:T(8,128)S(1)}, f32[64,32]{1,0:T(8,128)S(1)}, u32[]{:S(2)}, u32[]{:S(2)}) %collective-permute-start.2) | collective-permute-done | bytes 8224 | tf_op jit(solution)/shard_map/ppermute | solution.py:22
  104.8 1.0 collective-permute-done.1
  105.8 0.7 pad_maximum_fusion.gram_ref
  106.5 4.4 %shard_map.58 = (f32[2,32,32]{2,1,0:T(8,128)}, f32[2,32,64]{2,1,0:T(8,128)}) custom-call(f32[4,64,32]{2,1,0:T(8,128)} %pad_maximum_fusion.gram_ref, f32[32,128]{1,0:T(8,128)} %copy-done.4), custom_call_target="tpu_custom_call" | custom-call | flops 1048576 | bytes 12582912 | tf_op jit(solution)/shard_map/pallas_call | solution.py:127
  110.8 0.0 copy-start.5
  110.8 0.0 all-to-all-done.5
  110.9 0.0 copy-start.3
  110.9 0.0 copy-start.6
  110.9 0.9 copy-done.6
  111.8 3.0 %shard_map.61.q_ref = f32[32,8192]{1,0:T(8,128)S(1)} custom-call(s32[1]{0:T(128)} %bitcast.8.which_ref, f32[2,32,32]{2,1,0:T(8,128)S(1)} %copy-done.6, f32[4,4,8,2048]{3,2,1,0:T(8,128)} %bitcast.14.total_ref), custom_call_target="tpu_custom_call" | custom-call | flops 16777216 | bytes 2097152 | tf_op jit(solution)/shard_map/pallas_call | solution.py:144
  114.8 0.4 collective-permute-start.5
  115.2 0.0 copy-done.5
  115.2 0.0 copy-done.3
  115.2 2.5 %shard_map.62 = (bf16[1,2,64,8192]{3,2,1,0:T(8,128)(2,1)}, f32[2,32,8192]{2,1,0:T(8,128)}) custom-call(s32[1]{0:T(128)} %bitcast.8.which_ref, f32[2,32,64]{2,1,0:T(8,128)S(1)} %copy-done.5, f32[32,8192]{1,0:T(8,128)S(1)} %shard_map.61.q_ref, bf16[1,2,64,8192]{3,2,1,0:T(8,128)(2,1)S(1)} %copy-done.3, bf16[1,2,64,8192]{3,2,1,0:T(8,128)(2,1)S(1)} %copy-done.1), custom_call_target="tpu_custom_call" | custom-call | flops 33554432 | bytes 5242880 | tf_op jit(solution)/shard_map/pallas_call | solution.py:172
  117.6 0.0 collective-permute-done.5.q_ref
  117.6 2.5 %shard_map.63 = (bf16[1,2,64,8192]{3,2,1,0:T(8,128)(2,1)}, f32[2,32,8192]{2,1,0:T(8,128)}) custom-call(s32[1]{0:T(128)} %bitcast.which_ref, f32[2,32,64]{2,1,0:T(8,128)S(1)} %copy-done.5, f32[32,8192]{1,0:T(8,128)S(1)} %collective-permute-done.5.q_ref, bf16[1,2,64,8192]{3,2,1,0:T(8,128)(2,1)S(1)} %copy-done.3, ...), custom_call_target="tpu_custom_call", output_to_operand_aliasing={{0}: (5, {}), {1}: (6, {})} | custom-call | flops 33554432 | bytes 5242880 | tf_op jit(solution)/shard_map/pallas_call | solution.py:172
  (7 shorter events, 0.1 us)
Async XLA Ops:
  0.6 1.2 %copy-start = (bf16[2,8192,32]{1,2,0:T(8,128)(2,1)S(1)}, bf16[2,8192,32]{1,2,0:T(8,128)(2,1)}, u32[]{:S(2)}) copy-start(bf16[2,8192,32]{1,2,0:T(8,128)(2,1)} %param.5) | copy-start | bytes 3145732
  0.6 30.3 %copy-start.1 = (bf16[1,2,64,8192]{3,2,1,0:T(8,128)(2,1)S(1)}, bf16[1,2,64,8192]{3,2,1,0:T(8,128)(2,1)}, u32[]{:S(2)}) copy-start(bf16[1,2,64,8192]{3,2,1,0:T(8,128)(2,1)} %errors_ref.7) | copy-start | bytes 6291460
  14.7 16.2 %all-to-all-start.1 = ((f32[8,32,128]{2,1,0:T(8,128)}), f32[8,32,128]{2,1,0:T(8,128)S(1)}, u32[]{:S(2)}, u32[]{:S(2)}) async-start(f32[8,32,128]{2,1,0:T(8,128)} %broadcast_in_dim.28), calls=%async_computation.1 | async-start | bytes 262144 | tf_op jit(solution)/shard_map/all_to_all | solution.py:26
  30.9 57.9 %copy-start.4 = (f32[32,128]{1,0:T(8,128)}, f32[32,128]{1,0:T(8,128)S(1)}, u32[]{:S(2)}) copy-start(f32[32,128]{1,0:T(8,128)S(1)} %reduce_sum.37.summed_ref) | copy-start | bytes 49156
  30.9 1.6 %copy-start.2 = (bf16[1,2,64,8192]{3,2,1,0:T(8,128)(2,1)S(1)}, bf16[1,2,64,8192]{3,2,1,0:T(8,128)(2,1)}, u32[]{:S(2)}) copy-start(bf16[1,2,64,8192]{3,2,1,0:T(8,128)(2,1)} %grads_ref.7) | copy-start | bytes 6291460
  34.1 5.8 %collective-permute-start.4 = (f32[32,8192]{1,0:T(8,128)S(1)}, f32[32,8192]{1,0:T(8,128)S(1)}, u32[]{:S(2)}, u32[]{:S(2)}) collective-permute-start(f32[32,8192]{1,0:T(8,128)S(1)} %shard_map.59), channel_id=1, source_target_pairs={{0,1},{1,0},{2,3},{3,2},{4,5},{5,4},{6,7},{7,6},{8,9},{9,8},{10,11... | collective-permute-start | bytes 3145736 | tf_op jit(solution)/shard_map/ppermute | solution.py:18
  84.5 26.4 %all-to-all-start.5 = ((f32[16,8,2048]{2,1,0:T(8,128)}), f32[16,8,2048]{2,1,0:T(8,128)}, u32[]{:S(2)}, u32[]{:S(2)}) async-start(f32[16,8,2048]{2,1,0:T(8,128)} %broadcast_in_dim.31), calls=%async_computation.5 | async-start | bytes 2097152 | tf_op jit(solution)/shard_map/all_to_all | solution.py:26
  89.1 4.8 %collective-permute-start = (f32[64,32]{1,0:T(8,128)S(1)}, f32[64,32]{1,0:T(8,128)S(1)}, u32[]{:S(2)}, u32[]{:S(2)}) collective-permute-start(f32[64,32]{1,0:T(8,128)S(1)} %bitcast.31), channel_id=1, source_target_pairs={{0,1},{1,0},{2,3},{3,2},{4,5},{5,4},{6,7},{7,6},{8,9},{9,8},{10,11... | collective-permute-start | bytes 24584 | tf_op jit(solution)/shard_map/ppermute | solution.py:18
  93.9 6.2 %collective-permute-start.3 = (f32[64,32]{1,0:T(8,128)S(1)}, f32[64,32]{1,0:T(8,128)S(1)}, u32[]{:S(2)}, u32[]{:S(2)}) collective-permute-start(f32[64,32]{1,0:T(8,128)S(1)} %bitcast_add_fusion), channel_id=1, source_target_pairs={{0,6},{2,0},{4,2},{6,4},{1,7},{3,1},{5,3},{7,5},{8,14},{10,8},{12,... | collective-permute-start | bytes 24584 | tf_op jit(solution)/shard_map/ppermute | solution.py:22
  96.6 8.1 %collective-permute-start.2 = (f32[64,32]{1,0:T(8,128)S(1)}, f32[64,32]{1,0:T(8,128)S(1)}, u32[]{:S(2)}, u32[]{:S(2)}) collective-permute-start(f32[64,32]{1,0:T(8,128)S(1)} %bitcast_add_fusion), channel_id=1, source_target_pairs={{0,4},{2,6},{4,0},{6,2},{1,5},{3,7},{5,1},{7,3},{8,12},{10,14},{12... | collective-permute-start | bytes 24584 | tf_op jit(solution)/shard_map/ppermute | solution.py:22
  97.2 8.6 %collective-permute-start.1 = (f32[64,32]{1,0:T(8,128)S(1)}, f32[64,32]{1,0:T(8,128)S(1)}, u32[]{:S(2)}, u32[]{:S(2)}) collective-permute-start(f32[64,32]{1,0:T(8,128)S(1)} %bitcast_add_fusion), channel_id=1, source_target_pairs={{0,2},{2,4},{4,6},{6,0},{1,3},{3,5},{5,7},{7,1},{8,10},{10,12},{12... | collective-permute-start | bytes 24584 | tf_op jit(solution)/shard_map/ppermute | solution.py:22
  110.8 4.3 %copy-start.5 = (f32[2,32,64]{2,1,0:T(8,128)S(1)}, f32[2,32,64]{2,1,0:T(8,128)}, u32[]{:S(2)}) copy-start(f32[2,32,64]{2,1,0:T(8,128)} %get-tuple-element.9.ortho_ref) | copy-start | bytes 49156
  110.9 4.3 %copy-start.3 = (bf16[1,2,64,8192]{3,2,1,0:T(8,128)(2,1)S(1)}, bf16[1,2,64,8192]{3,2,1,0:T(8,128)(2,1)}, u32[]{:S(2)}) copy-start(bf16[1,2,64,8192]{3,2,1,0:T(8,128)(2,1)} %grads_ref.7) | copy-start | bytes 6291460
  110.9 0.9 copy-start.6
  114.8 2.8 %collective-permute-start.5 = (f32[32,8192]{1,0:T(8,128)S(1)}, f32[32,8192]{1,0:T(8,128)S(1)}, u32[]{:S(2)}, u32[]{:S(2)}) collective-permute-start(f32[32,8192]{1,0:T(8,128)S(1)} %shard_map.61.q_ref), channel_id=1, source_target_pairs={{0,1},{1,0},{2,3},{3,2},{4,5},{5,4},{6,7},{7,6},{8,9},{9,8},{10,11... | collective-permute-start | bytes 3145736 | tf_op jit(solution)/shard_map/ppermute | solution.py:18

commit v3 on v2

v3 whole, which is shorter than its diff:
```python
import jax
import jax.numpy as jnp
from jax import lax
from jax.experimental import pallas as pl
from jax.experimental.pallas import tpu as pltpu
from jax.sharding import Mesh
from jax.sharding import PartitionSpec as P

NX, NV, NW, NY, NC = 4, 4, 2, 4, 2
COLS, R, MATS, ROWS = 8192, 32, 2, 64
DP = NX * NV * NW
WIDE = COLS // NX
SPAN = WIDE // NW
K8 = R // NY
HIGH = lax.Precision.HIGHEST
VMEM_LIMIT = 32 * 1024 * 1024


def swap(a):
    return lax.ppermute(a, "c", [(0, 1), (1, 0)])


def shifts(a, axis, size):
    return [lax.ppermute(a, axis, [(i, (i + s) % size) for i in range(size)]) for s in range(1, size)]


def exchange(a, axes):
    return lax.all_to_all(a, axes, 0, 0)


def split3(value):
    high = value.astype(jnp.bfloat16)
    rest = value - high.astype(jnp.float32)
    middle = rest.astype(jnp.bfloat16)
    low = (rest - middle.astype(jnp.float32)).astype(jnp.bfloat16)
    return high, middle, low


def left_kernel(grads_ref, errors_ref, q_ref, merged_ref, copies_ref, total):
    step = pl.program_id(0)

    @pl.when(step == 0)
    def _():
        total[...] = jnp.zeros_like(total)

    for m in range(MATS):
        added = grads_ref[0, m].astype(jnp.float32) + errors_ref[0, m].astype(jnp.float32)
        merged = added.astype(jnp.bfloat16)
        merged_ref[m] = merged
        total[:, m * ROWS : (m + 1) * ROWS] += lax.dot_general(
            q_ref[m], merged, (((1,), (1,)), ((), ())), preferred_element_type=jnp.float32
        )

    @pl.when(step == NX - 1)
    def _():
        for copy in range(NX):
            copies_ref[copy] = total[...]


def left(grads, errors, q_t):
    block = pl.BlockSpec((1, MATS, ROWS, WIDE), lambda i: (0, 0, 0, i))
    return pl.pallas_call(
        left_kernel,
        grid=(NX,),
        in_specs=[block, block, pl.BlockSpec((MATS, R, WIDE), lambda i: (0, 0, i))],
        out_specs=[
            pl.BlockSpec((MATS, ROWS, WIDE), lambda i: (0, 0, i)),
            pl.BlockSpec((NX, R, MATS * ROWS), lambda i: (0, 0, 0)),
        ],
        out_shape=(
            jax.ShapeDtypeStruct((MATS, ROWS, COLS), jnp.bfloat16),
            jax.ShapeDtypeStruct((NX, R, MATS * ROWS), jnp.float32),
        ),
        scratch_shapes=[pltpu.VMEM((R, MATS * ROWS), jnp.float32)],
        compiler_params=pltpu.CompilerParams(vmem_limit_bytes=VMEM_LIMIT),
        cost_estimate=pl.CostEstimate(flops=1 << 27, bytes_accessed=7 << 20, transcendentals=0),
    )(grads, errors, q_t)


def sum_kernel(parts_ref, *refs):
    out_ref = refs[-1]
    total = parts_ref[0]
    for part in range(1, parts_ref.shape[0]):
        total = total + parts_ref[part]
    if len(out_ref.shape) == len(total.shape):
        out_ref[...] = total
    else:
        for copy in range(out_ref.shape[0]):
            out_ref[copy] = total


def sum_parts(parts, copies=None, after=()):
    shape = parts.shape[1:] if copies is None else (copies,) + parts.shape[1:]
    return pl.pallas_call(
        sum_kernel,
        in_specs=[pl.BlockSpec(memory_space=pltpu.VMEM)] + [pl.BlockSpec(memory_space=pl.ANY)] * len(after),
        out_specs=pl.BlockSpec(memory_space=pltpu.VMEM),
        out_shape=jax.ShapeDtypeStruct(shape, jnp.float32),
        compiler_params=pltpu.CompilerParams(vmem_limit_bytes=VMEM_LIMIT),
        cost_estimate=pl.CostEstimate(flops=1 << 18, bytes_accessed=1 << 20, transcendentals=0),
    )(parts, *after)


def right_terms(which_ref, summed_ref, merged_ref):
    both = summed_ref[...]
    value = jnp.where(which_ref[0] == 0, both[:, :ROWS], both[:, ROWS:])
    pieces = jnp.concatenate(split3(value), axis=0)
    products = jnp.dot(pieces, merged_ref[0], preferred_element_type=jnp.float32)
    return products[:R] + (products[R : 2 * R] + products[2 * R :])


def first_half_kernel(which_ref, summed_ref, merged_ref, gram_ref, out_ref):
    out_ref[...] = right_terms(which_ref, summed_ref, merged_ref)


def second_half_kernel(which_ref, summed_ref, merged_ref, received_ref, out_ref):
    terms = right_terms(which_ref, summed_ref, merged_ref) + received_ref[...]
    for w in range(NW):
        out_ref[0, w] = terms[:, w * SPAN : (w + 1) * SPAN].reshape(NY, K8, SPAN)


MATRIX_BLOCK = pl.BlockSpec((1, ROWS, WIDE), lambda i, which: (which[0], 0, i))
ERROR_BLOCK = pl.BlockSpec((1, 1, ROWS, WIDE), lambda i, which: (0, which[0], 0, i))
COLUMN_BLOCK = pl.BlockSpec((R, WIDE), lambda i, which: (0, i))
SPREAD_BLOCK = pl.BlockSpec((1, NW, NY, K8, SPAN), lambda i, which: (i, 0, 0, 0, 0))
UNTOUCHED = pl.BlockSpec(memory_space=pl.ANY)


def whole(*shape):
    return pl.BlockSpec(shape, lambda i, which: (0,) * len(shape))


def call(kernel, in_specs, out_specs, out_shape, flops, nbytes, aliases=None):
    return pl.pallas_call(
        kernel,
        grid_spec=pltpu.PrefetchScalarGridSpec(
            num_scalar_prefetch=1, grid=(NX,), in_specs=in_specs, out_specs=out_specs
        ),
        out_shape=out_shape,
        input_output_aliases=aliases or {},
        compiler_params=pltpu.CompilerParams(vmem_limit_bytes=VMEM_LIMIT),
        cost_estimate=pl.CostEstimate(flops=flops, bytes_accessed=nbytes, transcendentals=0),
    )


def right_first(which, summed, merged, gram):
    return call(
        first_half_kernel,
        [whole(R, MATS * ROWS), MATRIX_BLOCK, UNTOUCHED],
        COLUMN_BLOCK,
        jax.ShapeDtypeStruct((R, COLS), jnp.float32),
        6 * ROWS * R * COLS,
        2 << 20,
    )(which, summed, merged, gram)


def right_second(which, summed, merged, received):
    return call(
        second_half_kernel,
        [whole(R, MATS * ROWS), MATRIX_BLOCK, COLUMN_BLOCK],
        SPREAD_BLOCK,
        jax.ShapeDtypeStruct((NX, NW, NY, K8, SPAN), jnp.float32),
        6 * ROWS * R * COLS,
        3 << 20,
    )(which, summed, merged, received)


def factor_kernel(first_ref, second_ref, third_ref, fourth_ref, summed_ref, inverse_ref, ortho_ref):
    grams = (first_ref[...] + second_ref[...]) + (third_ref[...] + fourth_ref[...])
    row = lax.broadcasted_iota(jnp.int32, (R, 2 * R), 0)
    lane = lax.broadcasted_iota(jnp.int32, (R, 2 * R), 1)
    unit = (lane - R == row).astype(jnp.float32)[:, R:]
    states = [jnp.concatenate([grams[m * R : (m + 1) * R], unit], axis=1) for m in range(MATS)]
    for j in range(R):
        for m in range(MATS):
            x = states[m]
            pivot = x[j : j + 1]
            ratio = x[:, j : j + 1] * (1.0 / x[j : j + 1, j : j + 1])
            states[m] = x - jnp.where(row > j, ratio, 0.0) * pivot
    for m in range(MATS):
        x = states[m]
        diagonal = jnp.sum(jnp.where(row == lane, x, 0.0), axis=1, keepdims=True)
        inverse = x[:, R:] / jnp.sqrt(diagonal)
        inverse_ref[m] = inverse
        ortho_ref[m] = jnp.dot(
            inverse,
            summed_ref[:, m * ROWS : (m + 1) * ROWS],
            precision=HIGH,
            preferred_element_type=jnp.float32,
        )


def factors(grams, summed):
    return pl.pallas_call(
        factor_kernel,
        out_shape=(
            jax.ShapeDtypeStruct((MATS, R, R), jnp.float32),
            jax.ShapeDtypeStruct((MATS, R, ROWS), jnp.float32),
        ),
        cost_estimate=pl.CostEstimate(flops=1 << 20, bytes_accessed=12 << 20, transcendentals=0),
    )(*grams, summed)


def finish_kernel(which_ref, inverse_ref, total_ref, out_ref):
    a, b, c = split3(inverse_ref[0] * (1.0 / DP))
    left_pieces = jnp.concatenate([a, a, a, b, b, c], axis=1)
    for w in range(NW):
        high, middle, low = split3(total_ref[0, w].reshape(R, SPAN))
        right_pieces = jnp.concatenate([high, middle, low, high, middle, high], axis=0)
        out_ref[:, w * SPAN : (w + 1) * SPAN] = jnp.dot(
            left_pieces, right_pieces, preferred_element_type=jnp.float32
        )


def finish(which, inverse, total):
    return call(
        finish_kernel,
        [pl.BlockSpec((1, R, R), lambda i, which: (which[0], 0, 0)), SPREAD_BLOCK],
        COLUMN_BLOCK,
        jax.ShapeDtypeStruct((R, COLS), jnp.float32),
        2 * R * R * COLS,
        2 << 20,
    )(which, inverse, total)


def error_kernel(which_ref, ortho_ref, q_ref, merged_ref, *refs):
    error_ref, out_ref = refs[-2:]
    q = q_ref[...]
    approx = lax.dot_general(
        ortho_ref[0].astype(jnp.bfloat16),
        q.astype(jnp.bfloat16),
        (((0,), (0,)), ((), ())),
        preferred_element_type=jnp.float32,
    )
    error = merged_ref[0].astype(jnp.float32) - approx
    error_ref[...] = error.astype(jnp.bfloat16).reshape(1, 1, ROWS, WIDE)
    out_ref[...] = q.reshape(1, R, WIDE)


def error_step(which, ortho, q, merged, before=()):
    out_spec = pl.BlockSpec((1, R, WIDE), lambda i, which: (which[0], 0, i))
    ortho_spec = pl.BlockSpec((1, R, ROWS), lambda i, which: (which[0], 0, 0))
    return call(
        error_kernel,
        [ortho_spec, COLUMN_BLOCK, MATRIX_BLOCK] + [UNTOUCHED] * len(before),
        [ERROR_BLOCK, out_spec],
        (
            jax.ShapeDtypeStruct((1, MATS, ROWS, COLS), jnp.bfloat16),
            jax.ShapeDtypeStruct((MATS, R, COLS), jnp.float32),
        ),
        2 * ROWS * R * COLS,
        5 << 20,
        {4: 0, 5: 1} if before else None,
    )(which, ortho, q, merged, *before)


def local(grads, errors, q_init):
    core = lax.axis_index("c").astype(jnp.int32)
    own = core.reshape(1)
    other = (1 - core).reshape(1)
    merged, terms = left(grads, errors, q_init.transpose(0, 2, 1))
    terms = sum_parts(exchange(terms, "x"), NV * NW)
    summed = sum_parts(exchange(terms, ("v", "w")))

    split = summed.reshape(R, MATS, ROWS)
    gram = jnp.einsum("kmr,lmr->mkl", split, split, precision=HIGH).reshape(MATS * R, R)
    gram_pair = gram + swap(gram)
    grams = [gram_pair] + shifts(gram_pair, "y", NY)

    received = swap(right_first(other, summed, merged, gram))
    half = right_second(own, summed, merged, received)
    half = exchange(half.reshape(NX * NW * NY, K8, SPAN), ("x", "w", "y"))
    mine = sum_parts(half, NV, after=grams)
    inverse, ortho = factors(grams, summed)
    mine = sum_parts(exchange(mine, "v"), NX * NW * NY)

    total = exchange(mine, ("x", "w", "y")).reshape(NX, NW, NY, K8, SPAN)
    q_own = finish(own, inverse, total)
    q_other = swap(q_own)
    first = error_step(own, ortho, q_own, merged)
    error_new, q_t = error_step(other, ortho, q_other, merged, first)
    return (error_new, q_t.transpose(0, 2, 1), ortho.transpose(0, 2, 1))


def solution(mesh):
    fine = Mesh(mesh.devices.reshape(NX, NV, NW, NY, NC), ("x", "v", "w", "y", "c"))
    big = P(("x", "v", "w"), None, ("y", "c"), None)
    return jax.shard_map(
        local,
        mesh=fine,
        in_specs=(big, big, P()),
        out_specs=(big, P(), P(None, ("y", "c"), None)),
        check_vma=False,
    )
```

time: 121 us -> 106 us (0.88)
  blocking collectives: 49.7 us -> 18.8 us
  waiting for transfers between devices: 19.2 us -> 33.6 us
  starting transfers between devices: 24.2 us -> 28.8 us
  matrix products: 3.05 us -> 0.16 us
  other arithmetic: 1.99 us -> 0.01 us
  Pallas kernels: 15.5 us -> 17.1 us
    all_to_all x4 -> x2, blocking collectives: 49.7 us -> 18.8 us  [exchange(): return lax.all_to_all(a, axes, 0, 0)]
    all_to_all x2 -> x3, waiting for transfers between devices: 8.03 us -> 18.1 us  [exchange(): return lax.all_to_all(a, axes, 0, 0)]
    all_to_all x2 -> x3, starting transfers between devices: 12.5 us -> 17.5 us  [exchange(): return lax.all_to_all(a, axes, 0, 0)]
    ppermute x3, waiting for transfers between devices: 8.01 us -> 12.4 us  [shifts(): lax.ppermute(a, axis, [(i, (i + s) % size) for i in range(size)])]
    pallas_call x4 -> x9, Pallas kernels: 8.12 us -> 11.5 us  [the longest x2 4.74 us: error_step(): call(error_kernel, [ortho_spec, COLUMN_BLOCK, MATRIX_BLOCK] + [UNTOUCHED]...]
    dot_general x1 -> x0, matrix products: 2.89 us -> none  [local(): jnp.einsum('mck,mrc->kmr', q_init, merged, preferred_element_type=jnp.flo...]
    unnamed x14 -> x22, local copies, waits for them, and re-layouts: 3.72 us -> 6.15 us
    broadcast_in_dim x5 -> x0, local copies, waits for them, and re-layouts: 1.84 us -> none  [copies_to_all(): jnp.broadcast_to(a[None], (count,) + a.shape)]
  transfers between devices with their start and end apart: 8 -> 9, of which waited for: 6 -> 6; matrix products, arithmetic and copies ran while one was open for 1% -> 0% of each run, Pallas kernels for 6% -> 6%
where the time goes in v3:
time: 106 us; the launch traced here: 105 us
  waiting for transfers between devices  33.6 us (32%)
  starting transfers between devices  28.8 us (27%)
  blocking collectives  18.8 us (18%)
  Pallas kernels  17.1 us (16%)
  local copies, waits for them, and re-layouts  6.23 us (6%)
    all_to_all x2, blocking collectives, exchange(): return lax.all_to_all(a, axes, 0, 0)  18.8 us
    all_to_all x3, waiting for transfers between devices, exchange(): return lax.all_to_all(a, axes, 0, 0)  18.1 us
    all_to_all x3, starting transfers between devices, exchange(): return lax.all_to_all(a, axes, 0, 0)  17.5 us
    ppermute x3, waiting for transfers between devices, shifts(): lax.ppermute(a, axis, [(i, (i + s) % size) for i in range(size)])  12.4 us
    ppermute x3, starting transfers between devices, swap(): return lax.ppermute(a, 'c', [(0, 1), (1, 0)])  7.33 us
    unnamed x22, local copies, waits for them, and re-layouts  6.15 us
    pallas_call x2, Pallas kernels, error_step(): call(error_kernel, [ortho_spec, COLUMN_BLOCK, MATRIX_BLOCK] + [UNTOUCHED]...  4.74 us
    pallas_call x1, Pallas kernels, factors(): pl.pallas_call(factor_kernel, out_shape=(jax.ShapeDtypeStruct((MATS, R, R...  4.3 us
  transfers between devices with their start and end apart: 9, of which 6 were waited for; matrix products, arithmetic and copies ran while one was open for 0% of the time, Pallas kernels for 6%

profile of v3, /device:TPU:1, one launch (start us, length us, event | category | flops | bytes accessed | tf_op | source)
XLA Modules:
  0.0 105.4 jit_solution(9922422146187151300)
XLA Ops:
  0.6 0.0 copy-start.1
  0.6 1.6 %copy-done.1 = bf16[1,2,64,8192]{3,2,1,0:T(8,128)(2,1)S(1)} copy-done((bf16[1,2,64,8192]{3,2,1,0:T(8,128)(2,1)S(1)}, bf16[1,2,64,8192]{3,2,1,0:T(8,128)(2,1)}, u32[]{:S(2)}) %copy-start.1) | copy-done | bytes 2097176
  2.2 0.0 copy-start.2
  2.2 1.6 %copy-done.2 = bf16[1,2,64,8192]{3,2,1,0:T(8,128)(2,1)S(1)} copy-done((bf16[1,2,64,8192]{3,2,1,0:T(8,128)(2,1)S(1)}, bf16[1,2,64,8192]{3,2,1,0:T(8,128)(2,1)}, u32[]{:S(2)}) %copy-start.2) | copy-done | bytes 2097176
  3.8 0.0 copy-start.3
  3.8 1.2 %copy-done.3 = bf16[2,8192,32]{1,2,0:T(8,128)(2,1)S(1)} copy-done((bf16[2,8192,32]{1,2,0:T(8,128)(2,1)S(1)}, bf16[2,8192,32]{1,2,0:T(8,128)(2,1)}, u32[]{:S(2)}) %copy-start.3) | copy-done | bytes 1048600
  5.0 2.0 %shard_map.58 = (bf16[2,64,8192]{2,1,0:T(8,128)(2,1)S(1)}, f32[4,32,128]{2,1,0:T(8,128)S(1)}) custom-call(bf16[1,2,64,8192]{3,2,1,0:T(8,128)(2,1)S(1)} %copy-done.1, bf16[1,2,64,8192]{3,2,1,0:T(8,128)(2,1)S(1)} %copy-done.2, bf16[2,32,8192]{2,1,0:T(8,128)(2,1)S(1)} %bitcast.10), custom_call_target="tpu_custom_call" | custom-call | flops 134217728 | bytes 7340032 | tf_op jit(solution)/shard_map/pallas_call | solution.py:62
  7.0 9.1 %all_to_all.25.parts_ref = f32[4,32,128]{2,1,0:T(8,128)S(1)} all-to-all(f32[4,32,128]{2,1,0:T(8,128)S(1)} %get-tuple-element.11), channel_id=1, replica_groups=mesh['x'=4,'v'=4,'w'=2,'y'=4,'c'=2] {'x'}, dimensions={0} | all-to-all | bytes 131072 | tf_op jit(solution)/shard_map/all_to_all | solution.py:28
  16.1 0.7 shard_map.59
  16.8 8.2 %all-to-all-start.1 = ((f32[8,32,128]{2,1,0:T(8,128)}), f32[8,32,128]{2,1,0:T(8,128)S(1)}, u32[]{:S(2)}, u32[]{:S(2)}) async-start(f32[8,32,128]{2,1,0:T(8,128)} %shard_map.59), calls=%async_computation.1 | async-start | bytes 262144 | tf_op jit(solution)/shard_map/all_to_all | solution.py:28
  25.0 8.0 %all-to-all-done.1.parts_ref = f32[8,32,128]{2,1,0:T(8,128)S(1)} async-done(((f32[8,32,128]{2,1,0:T(8,128)}), f32[8,32,128]{2,1,0:T(8,128)S(1)}, u32[]{:S(2)}, u32[]{:S(2)}) %all-to-all-start.1) | async-done | bytes 131104 | tf_op jit(solution)/shard_map/all_to_all | solution.py:28
  33.0 0.0 copy-start.4
  33.0 0.1 reshape.25
  33.1 0.2 fusion
  33.3 1.4 %shard_map.62 = f32[32,8192]{1,0:T(8,128)S(1)} custom-call(s32[1]{0:T(128)} %bitcast.which_ref, f32[32,128]{1,0:T(8,128)S(1)} %shard_map.60.summed_ref, bf16[2,64,8192]{2,1,0:T(8,128)(2,1)S(1)} %get-tuple-element.14.merged_ref, f32[64,32]{1,0:T(8,128)S(1)} %bitcast.11), custom_call_target="tpu_custom_call" | custom-call | flops 100663296 | bytes 2097152 | tf_op jit(solution)/shard_map/pallas_call | solution.py:147
  34.7 3.5 %collective-permute-start.4 = (f32[32,8192]{1,0:T(8,128)S(1)}, f32[32,8192]{1,0:T(8,128)S(1)}, u32[]{:S(2)}, u32[]{:S(2)}) collective-permute-start(f32[32,8192]{1,0:T(8,128)S(1)} %shard_map.62), channel_id=1, source_target_pairs={{0,1},{1,0},{2,3},{3,2},{4,5},{5,4},{6,7},{7,6},{8,9},{9,8},{10,11... | collective-permute-start | bytes 3145736 | tf_op jit(solution)/shard_map/ppermute | solution.py:20
  38.3 2.3 %collective-permute-done.4.received_ref = f32[32,8192]{1,0:T(8,128)S(1)} collective-permute-done((f32[32,8192]{1,0:T(8,128)S(1)}, f32[32,8192]{1,0:T(8,128)S(1)}, u32[]{:S(2)}, u32[]{:S(2)}) %collective-permute-start.4) | collective-permute-done | bytes 1048608 | tf_op jit(solution)/shard_map/ppermute | solution.py:20
  40.5 2.5 %shard_map.63 = f32[4,2,4,8,1024]{4,3,2,1,0:T(8,128)} custom-call(s32[1]{0:T(128)} %bitcast.3.which_ref, f32[32,128]{1,0:T(8,128)S(1)} %shard_map.60.summed_ref, bf16[2,64,8192]{2,1,0:T(8,128)(2,1)S(1)} %get-tuple-element.14.merged_ref, f32[32,8192]{1,0:T(8,128)S(1)} %collective-permute-done.4.received_ref), custom_call_target="tpu_custom_call" | custom-call | flops 100663296 | bytes 3145728 | tf_op jit(solution)/shard_map/pallas_call | solution.py:158
  43.0 0.0 copy-done.4
  43.0 5.2 %all-to-all-start.2 = ((f32[32,8,1024]{2,1,0:T(8,128)}), f32[32,8,1024]{2,1,0:T(8,128)S(1)}, u32[]{:S(2)}, u32[]{:S(2)}) async-start(f32[32,8,1024]{2,1,0:T(8,128)} %bitcast.4), calls=%async_computation.2 | async-start | bytes 2097152 | tf_op jit(solution)/shard_map/all_to_all | solution.py:28
  48.2 0.7 collective-permute-start
  48.9 0.9 collective-permute-done
  49.8 2.8 %collective-permute-start.3 = (f32[64,32]{1,0:T(8,128)S(1)}, f32[64,32]{1,0:T(8,128)S(1)}, u32[]{:S(2)}, u32[]{:S(2)}) collective-permute-start(f32[64,32]{1,0:T(8,128)S(1)} %bitcast_add_fusion.first_ref.refs_0_), channel_id=1, source_target_pairs={{0,6},{2,0},{4,2},{6,4},{1,7},{3,1},{5,3},{7,5},{8,14},{10,8},{12,... | collective-permute-start | bytes 24584 | tf_op jit(solution)/shard_map/ppermute | solution.py:24
  52.6 0.6 collective-permute-start.2
  53.2 0.6 collective-permute-start.1
  53.8 0.0 collective-permute-done.3.fourth_ref.refs_3_
  53.8 4.6 %collective-permute-done.2.third_ref.refs_2_ = f32[64,32]{1,0:T(8,128)S(1)} collective-permute-done((f32[64,32]{1,0:T(8,128)S(1)}, f32[64,32]{1,0:T(8,128)S(1)}, u32[]{:S(2)}, u32[]{:S(2)}) %collective-permute-start.2) | collective-permute-done | bytes 8224 | tf_op jit(solution)/shard_map/ppermute | solution.py:24
  58.4 7.7 %collective-permute-done.1.second_ref.refs_1_ = f32[64,32]{1,0:T(8,128)S(1)} collective-permute-done((f32[64,32]{1,0:T(8,128)S(1)}, f32[64,32]{1,0:T(8,128)S(1)}, u32[]{:S(2)}, u32[]{:S(2)}) %collective-permute-start.1) | collective-permute-done | bytes 8224 | tf_op jit(solution)/shard_map/ppermute | solution.py:24
  66.2 0.0 all-to-all-done.2.parts_ref
  66.2 0.1 shard_map.64
  66.2 9.7 %all_to_all.26.parts_ref = f32[4,8,1024]{2,1,0:T(8,128)S(1)} all-to-all(f32[4,8,1024]{2,1,0:T(8,128)S(1)} %shard_map.64), channel_id=1, replica_groups=mesh['x'=4,'v'=4,'w'=2,'y'=4,'c'=2] {'v'}, dimensions={0} | all-to-all | bytes 262144 | tf_op jit(solution)/shard_map/all_to_all | solution.py:28
  75.9 0.1 shard_map.65
  76.1 0.0 copy-start
  76.1 1.0 copy-done
  77.0 0.0 copy-done.5
  77.0 0.0 copy-done.7
  77.0 0.0 copy-done.8
  77.0 0.0 copy-done.9
  77.0 4.1 %all-to-all-start.4 = ((f32[32,8,1024]{2,1,0:T(8,128)}), f32[32,8,1024]{2,1,0:T(8,128)S(1)}, u32[]{:S(2)}, u32[]{:S(2)}) async-start(f32[32,8,1024]{2,1,0:T(8,128)} %copy-done), calls=%async_computation.4 | async-start | bytes 2097152 | tf_op jit(solution)/shard_map/all_to_all | solution.py:28
  81.2 4.3 %shard_map.61 = (f32[2,32,32]{2,1,0:T(8,128)}, f32[2,32,64]{2,1,0:T(8,128)}) custom-call(f32[64,32]{1,0:T(8,128)} %copy-done.5, f32[64,32]{1,0:T(8,128)} %copy-done.9, f32[64,32]{1,0:T(8,128)} %copy-done.8, f32[64,32]{1,0:T(8,128)} %copy-done.7, f32[32,128]{1,0:T(8,128)} %copy-done.4), custom_call_target="tpu_custom_call" | custom-call | flops 1048576 | bytes 12582912 | tf_op jit(solution)/shard_map/pallas_call | solution.py:194
  85.5 10.0 %all-to-all-done.4 = f32[32,8,1024]{2,1,0:T(8,128)S(1)} async-done(((f32[32,8,1024]{2,1,0:T(8,128)}), f32[32,8,1024]{2,1,0:T(8,128)S(1)}, u32[]{:S(2)}, u32[]{:S(2)}) %all-to-all-start.4) | async-done | bytes 1048608 | tf_op jit(solution)/shard_map/all_to_all | solution.py:28
  95.5 0.8 copy-done.10
  96.3 1.3 %shard_map.66.q_ref = f32[32,8192]{1,0:T(8,128)S(1)} custom-call(s32[1]{0:T(128)} %bitcast.3.which_ref, f32[2,32,32]{2,1,0:T(8,128)S(1)} %copy-done.10, f32[4,2,4,8,1024]{4,3,2,1,0:T(8,128)S(1)} %bitcast.9), custom_call_target="tpu_custom_call" | custom-call | flops 16777216 | bytes 2097152 | tf_op jit(solution)/shard_map/pallas_call | solution.py:216
  97.6 3.1 %collective-permute-start.5 = (f32[32,8192]{1,0:T(8,128)S(1)}, f32[32,8192]{1,0:T(8,128)S(1)}, u32[]{:S(2)}, u32[]{:S(2)}) collective-permute-start(f32[32,8192]{1,0:T(8,128)S(1)} %shard_map.66.q_ref), channel_id=1, source_target_pairs={{0,1},{1,0},{2,3},{3,2},{4,5},{5,4},{6,7},{7,6},{8,9},{9,8},{10,11... | collective-permute-start | bytes 3145736 | tf_op jit(solution)/shard_map/ppermute | solution.py:20
  100.7 0.0 copy-done.6
  100.7 2.4 %shard_map.67 = (bf16[1,2,64,8192]{3,2,1,0:T(8,128)(2,1)}, f32[2,32,8192]{2,1,0:T(8,128)}) custom-call(s32[1]{0:T(128)} %bitcast.3.which_ref, f32[2,32,64]{2,1,0:T(8,128)S(1)} %copy-done.6, f32[32,8192]{1,0:T(8,128)S(1)} %shard_map.66.q_ref, bf16[2,64,8192]{2,1,0:T(8,128)(2,1)S(1)} %get-tuple-element.14.merged_ref), custom_call_target="tpu_custom_call" | custom-call | flops 33554432 | bytes 5242880 | tf_op jit(solution)/shard_map/pallas_call | solution.py:243
  103.0 0.0 collective-permute-done.5.q_ref
  103.0 2.4 %shard_map.68 = (bf16[1,2,64,8192]{3,2,1,0:T(8,128)(2,1)}, f32[2,32,8192]{2,1,0:T(8,128)}) custom-call(s32[1]{0:T(128)} %bitcast.which_ref, f32[2,32,64]{2,1,0:T(8,128)S(1)} %copy-done.6, f32[32,8192]{1,0:T(8,128)S(1)} %collective-permute-done.5.q_ref, ...), custom_call_target="tpu_custom_call", output_to_operand_aliasing={{0}: (4, {}), {1}: (5, {})} | custom-call | flops 33554432 | bytes 5242880 | tf_op jit(solution)/shard_map/pallas_call | solution.py:243
  (8 shorter events, 0.0 us)
Async XLA Ops:
  0.6 1.6 %copy-start.1 = (bf16[1,2,64,8192]{3,2,1,0:T(8,128)(2,1)S(1)}, bf16[1,2,64,8192]{3,2,1,0:T(8,128)(2,1)}, u32[]{:S(2)}) copy-start(bf16[1,2,64,8192]{3,2,1,0:T(8,128)(2,1)} %grads_ref.1) | copy-start | bytes 6291460
  2.2 1.6 %copy-start.2 = (bf16[1,2,64,8192]{3,2,1,0:T(8,128)(2,1)S(1)}, bf16[1,2,64,8192]{3,2,1,0:T(8,128)(2,1)}, u32[]{:S(2)}) copy-start(bf16[1,2,64,8192]{3,2,1,0:T(8,128)(2,1)} %errors_ref.1) | copy-start | bytes 6291460
  3.8 1.2 %copy-start.3 = (bf16[2,8192,32]{1,2,0:T(8,128)(2,1)S(1)}, bf16[2,8192,32]{1,2,0:T(8,128)(2,1)}, u32[]{:S(2)}) copy-start(bf16[2,8192,32]{1,2,0:T(8,128)(2,1)} %param.5) | copy-start | bytes 3145732
  16.8 16.2 %all-to-all-start.1 = ((f32[8,32,128]{2,1,0:T(8,128)}), f32[8,32,128]{2,1,0:T(8,128)S(1)}, u32[]{:S(2)}, u32[]{:S(2)}) async-start(f32[8,32,128]{2,1,0:T(8,128)} %shard_map.59), calls=%async_computation.1 | async-start | bytes 262144 | tf_op jit(solution)/shard_map/all_to_all | solution.py:28
  33.0 10.0 %copy-start.4 = (f32[32,128]{1,0:T(8,128)}, f32[32,128]{1,0:T(8,128)S(1)}, u32[]{:S(2)}) copy-start(f32[32,128]{1,0:T(8,128)S(1)} %shard_map.60.summed_ref) | copy-start | bytes 49156
  34.7 5.8 %collective-permute-start.4 = (f32[32,8192]{1,0:T(8,128)S(1)}, f32[32,8192]{1,0:T(8,128)S(1)}, u32[]{:S(2)}, u32[]{:S(2)}) collective-permute-start(f32[32,8192]{1,0:T(8,128)S(1)} %shard_map.62), channel_id=1, source_target_pairs={{0,1},{1,0},{2,3},{3,2},{4,5},{5,4},{6,7},{7,6},{8,9},{9,8},{10,11... | collective-permute-start | bytes 3145736 | tf_op jit(solution)/shard_map/ppermute | solution.py:20
  43.0 23.2 %all-to-all-start.2 = ((f32[32,8,1024]{2,1,0:T(8,128)}), f32[32,8,1024]{2,1,0:T(8,128)S(1)}, u32[]{:S(2)}, u32[]{:S(2)}) async-start(f32[32,8,1024]{2,1,0:T(8,128)} %bitcast.4), calls=%async_computation.2 | async-start | bytes 2097152 | tf_op jit(solution)/shard_map/all_to_all | solution.py:28
  48.2 1.6 %collective-permute-start = (f32[64,32]{1,0:T(8,128)S(1)}, f32[64,32]{1,0:T(8,128)S(1)}, u32[]{:S(2)}, u32[]{:S(2)}) collective-permute-start(f32[64,32]{1,0:T(8,128)S(1)} %bitcast.12), channel_id=1, source_target_pairs={{0,1},{1,0},{2,3},{3,2},{4,5},{5,4},{6,7},{7,6},{8,9},{9,8},{10,11... | collective-permute-start | bytes 24584 | tf_op jit(solution)/shard_map/ppermute | solution.py:20
  49.8 27.2 %copy-start.5 = (f32[64,32]{1,0:T(8,128)}, f32[64,32]{1,0:T(8,128)S(1)}, u32[]{:S(2)}) copy-start(f32[64,32]{1,0:T(8,128)S(1)} %bitcast_add_fusion.first_ref.refs_0_) | copy-start | bytes 24580
  49.8 4.0 %collective-permute-start.3 = (f32[64,32]{1,0:T(8,128)S(1)}, f32[64,32]{1,0:T(8,128)S(1)}, u32[]{:S(2)}, u32[]{:S(2)}) collective-permute-start(f32[64,32]{1,0:T(8,128)S(1)} %bitcast_add_fusion.first_ref.refs_0_), channel_id=1, source_target_pairs={{0,6},{2,0},{4,2},{6,4},{1,7},{3,1},{5,3},{7,5},{8,14},{10,8},{12,... | collective-permute-start | bytes 24584 | tf_op jit(solution)/shard_map/ppermute | solution.py:24
  52.6 5.8 %collective-permute-start.2 = (f32[64,32]{1,0:T(8,128)S(1)}, f32[64,32]{1,0:T(8,128)S(1)}, u32[]{:S(2)}, u32[]{:S(2)}) collective-permute-start(f32[64,32]{1,0:T(8,128)S(1)} %bitcast_add_fusion.first_ref.refs_0_), channel_id=1, source_target_pairs={{0,4},{2,6},{4,0},{6,2},{1,5},{3,7},{5,1},{7,3},{8,12},{10,14},{12... | collective-permute-start | bytes 24584 | tf_op jit(solution)/shard_map/ppermute | solution.py:24
  53.2 13.0 %collective-permute-start.1 = (f32[64,32]{1,0:T(8,128)S(1)}, f32[64,32]{1,0:T(8,128)S(1)}, u32[]{:S(2)}, u32[]{:S(2)}) collective-permute-start(f32[64,32]{1,0:T(8,128)S(1)} %bitcast_add_fusion.first_ref.refs_0_), channel_id=1, source_target_pairs={{0,2},{2,4},{4,6},{6,0},{1,3},{3,5},{5,7},{7,1},{8,10},{10,12},{12... | collective-permute-start | bytes 24584 | tf_op jit(solution)/shard_map/ppermute | solution.py:24
  53.8 23.2 %copy-start.7 = (f32[64,32]{1,0:T(8,128)}, f32[64,32]{1,0:T(8,128)S(1)}, u32[]{:S(2)}) copy-start(f32[64,32]{1,0:T(8,128)S(1)} %collective-permute-done.3.fourth_ref.refs_3_) | copy-start | bytes 24580
  58.4 18.6 %copy-start.8 = (f32[64,32]{1,0:T(8,128)}, f32[64,32]{1,0:T(8,128)S(1)}, u32[]{:S(2)}) copy-start(f32[64,32]{1,0:T(8,128)S(1)} %collective-permute-done.2.third_ref.refs_2_) | copy-start | bytes 24580
  66.2 10.9 %copy-start.9 = (f32[64,32]{1,0:T(8,128)}, f32[64,32]{1,0:T(8,128)S(1)}, u32[]{:S(2)}) copy-start(f32[64,32]{1,0:T(8,128)S(1)} %collective-permute-done.1.second_ref.refs_1_) | copy-start | bytes 24580
  76.1 1.0 copy-start
  77.0 18.5 %all-to-all-start.4 = ((f32[32,8,1024]{2,1,0:T(8,128)}), f32[32,8,1024]{2,1,0:T(8,128)S(1)}, u32[]{:S(2)}, u32[]{:S(2)}) async-start(f32[32,8,1024]{2,1,0:T(8,128)} %copy-done), calls=%async_computation.4 | async-start | bytes 2097152 | tf_op jit(solution)/shard_map/all_to_all | solution.py:28
  85.5 15.2 %copy-start.6 = (f32[2,32,64]{2,1,0:T(8,128)S(1)}, f32[2,32,64]{2,1,0:T(8,128)}, u32[]{:S(2)}) copy-start(f32[2,32,64]{2,1,0:T(8,128)} %get-tuple-element.12.ortho_ref) | copy-start | bytes 49156
  95.5 0.8 copy-start.10
  97.6 5.4 %collective-permute-start.5 = (f32[32,8192]{1,0:T(8,128)S(1)}, f32[32,8192]{1,0:T(8,128)S(1)}, u32[]{:S(2)}, u32[]{:S(2)}) collective-permute-start(f32[32,8192]{1,0:T(8,128)S(1)} %shard_map.66.q_ref), channel_id=1, source_target_pairs={{0,1},{1,0},{2,3},{3,2},{4,5},{5,4},{6,7},{7,6},{8,9},{9,8},{10,11... | collective-permute-start | bytes 3145736 | tf_op jit(solution)/shard_map/ppermute | solution.py:20

commit v4 on v0

v4 whole, which is shorter than its diff:
```python
import jax
import jax.numpy as jnp
from jax import lax
from jax.experimental import pallas as pl
from jax.experimental.pallas import tpu as pltpu
from jax.sharding import Mesh
from jax.sharding import PartitionSpec as P

NX, NV, NW, NY, NC = 4, 4, 2, 4, 2
COLS, R, MATS, ROWS = 8192, 32, 2, 64
DP = NX * NV * NW
GROUP = NX * NW * NY
BLOCK = COLS // GROUP
CHUNKS = 8
SPAN = COLS // CHUNKS
PER = GROUP // CHUNKS
AHEAD = 8
HIGH = lax.Precision.HIGHEST

IN_VMEM = pl.BlockSpec(memory_space=pltpu.VMEM)
IN_SMEM = pl.BlockSpec(memory_space=pltpu.SMEM)
IN_HBM = pl.BlockSpec(memory_space=pltpu.HBM)
ANYWHERE = pl.BlockSpec(memory_space=pl.ANY)
PARAMS = pltpu.CompilerParams(vmem_limit_bytes=16 * 1024 * 1024)


def cost(flops, nbytes):
    return pl.CostEstimate(flops=flops, bytes_accessed=nbytes, transcendentals=0)


def f32(*shape):
    return jax.ShapeDtypeStruct(shape, jnp.float32)


def vmem(*shape, dtype=jnp.float32):
    return pltpu.VMEM(shape, dtype)


def hbm(*shape, dtype=jnp.float32):
    return pltpu.HBM(shape, dtype)


def keep(a, space):
    return pltpu.with_memory_space_constraint(a, space)


def swap(a):
    return lax.ppermute(a, "c", [(0, 1), (1, 0)])


def shifts(a, axis, size):
    return [lax.ppermute(a, axis, [(i, (i + s) % size) for i in range(size)]) for s in range(1, size)]


def exchange(a, axes):
    return lax.all_to_all(a, axes, 0, 0)


def chunk(j):
    return pl.ds(j * SPAN, SPAN)


def split3(value):
    high = value.astype(jnp.bfloat16)
    rest = value - high.astype(jnp.float32)
    middle = rest.astype(jnp.bfloat16)
    low = (rest - middle.astype(jnp.float32)).astype(jnp.bfloat16)
    return high, middle, low


def start(pairs, sems):
    copies = [pltpu.make_async_copy(src, dst, sems.at[i]) for i, (src, dst) in enumerate(pairs)]
    for copy in copies:
        copy.start()
    return copies


def finish(copies):
    for copy in copies:
        copy.wait()


def left_kernel(
    core_ref, grads_hbm, errors_hbm, q_hbm, merged_ref, send_ref, mine_ref, theirs_ref, grads, errors, q, in_sems
):
    core = core_ref[0]
    def fetch(j):
        return start(
            [
                (grads_hbm.at[0, :, :, chunk(j)], grads.at[:, :, chunk(j)]),
                (errors_hbm.at[0, :, :, chunk(j)], errors.at[:, :, chunk(j)]),
                (q_hbm.at[:, :, chunk(j)], q.at[:, :, chunk(j)]),
            ],
            in_sems.at[j],
        )

    inward = [fetch(j) for j in range(AHEAD)]
    totals = [jnp.zeros((R, ROWS), jnp.float32) for _ in range(MATS)]
    for j in range(CHUNKS):
        finish(inward[j])
        if j + AHEAD < CHUNKS:
            inward.append(fetch(j + AHEAD))
        for m in range(MATS):
            total = grads[m, :, chunk(j)].astype(jnp.float32) + errors[m, :, chunk(j)].astype(jnp.float32)
            value = total.astype(jnp.bfloat16)
            merged_ref[m, :, chunk(j)] = value
            totals[m] += lax.dot_general(
                q[m, :, chunk(j)], value, (((1,), (1,)), ((), ())), preferred_element_type=jnp.float32
            )
        send_ref[:, chunk(j)] = merged_ref[1 - core, :, chunk(j)].astype(jnp.float32)
    mine_ref[...] = jnp.where(core == 0, totals[0], totals[1])
    theirs_ref[...] = jnp.where(core == 0, totals[1], totals[0])


def left(core, grads, errors, q_t):
    return pl.pallas_call(
        left_kernel,
        in_specs=[IN_SMEM, IN_HBM, IN_HBM, IN_HBM],
        out_specs=[IN_VMEM, IN_VMEM, IN_VMEM, IN_VMEM],
        out_shape=(
            vmem(MATS, ROWS, COLS, dtype=jnp.bfloat16),
            vmem(ROWS, COLS),
            vmem(R, ROWS),
            vmem(R, ROWS),
        ),
        scratch_shapes=[
            pltpu.VMEM((MATS, ROWS, COLS), jnp.bfloat16),
            pltpu.VMEM((MATS, ROWS, COLS), jnp.bfloat16),
            pltpu.VMEM((MATS, R, COLS), jnp.bfloat16),
            pltpu.SemaphoreType.DMA((CHUNKS, 3)),
        ],
        compiler_params=PARAMS,
        cost_estimate=cost(1 << 27, 9 << 20),
    )(core, keep(grads, pltpu.HBM), keep(errors, pltpu.HBM), keep(q_t, pltpu.HBM))


def added(parts_ref):
    value = parts_ref[0]
    for part in range(1, parts_ref.shape[0]):
        value = value + parts_ref[part]
    return value


def sum_kernel(parts_ref, *refs):
    out_ref = refs[-1]
    value = added(parts_ref)
    for copy in range(out_ref.shape[0]):
        out_ref[copy] = value


def sum_parts(parts, count, after=()):
    return pl.pallas_call(
        sum_kernel,
        in_specs=[IN_VMEM] + [IN_VMEM] * len(after),
        out_specs=IN_VMEM,
        out_shape=f32(count, *parts.shape[1:]),
        compiler_params=PARAMS,
        cost_estimate=cost(1 << 18, 2 << 20),
    )(parts, *[keep(a, pltpu.VMEM) for a in after])


def middle_kernel(parts_ref, inverse_ref, out_ref):
    total = added(parts_ref)
    q = jnp.dot(inverse_ref[...], total, precision=HIGH, preferred_element_type=jnp.float32) * (1.0 / DP)
    for copy in range(GROUP):
        out_ref[copy] = q


def middle(parts, inverse):
    return pl.pallas_call(
        middle_kernel,
        in_specs=[IN_VMEM, IN_VMEM],
        out_specs=IN_VMEM,
        out_shape=vmem(GROUP, R, BLOCK),
        compiler_params=PARAMS,
        cost_estimate=cost(1 << 20, 2 << 20),
    )(parts, inverse)


def right_kernel(core_ref, summed_ref, merged_ref, received_ref, out_ref, terms, out_sems):
    core = core_ref[0]
    pieces = jnp.concatenate(split3(summed_ref[...]), axis=0)
    outward = []
    for j in range(CHUNKS):
        both = jnp.concatenate(
            [merged_ref[core, :, chunk(j)], received_ref[:, chunk(j)].astype(jnp.bfloat16)], axis=0
        )
        products = jnp.dot(pieces, both, preferred_element_type=jnp.float32)
        value = products[:R] + (products[R : 2 * R] + products[2 * R :])
        for i in range(PER):
            terms[j * PER + i] = value[:, i * BLOCK : (i + 1) * BLOCK]
        outward += start([(terms.at[pl.ds(j * PER, PER)], out_ref.at[pl.ds(j * PER, PER)])], out_sems.at[j])
    finish(outward)


def right(core, summed, merged, received):
    return pl.pallas_call(
        right_kernel,
        in_specs=[IN_SMEM, IN_VMEM, IN_VMEM, IN_VMEM],
        out_specs=IN_HBM,
        out_shape=hbm(GROUP, R, BLOCK),
        scratch_shapes=[pltpu.VMEM((GROUP, R, BLOCK), jnp.float32), pltpu.SemaphoreType.DMA((CHUNKS, 1))],
        compiler_params=PARAMS,
        cost_estimate=cost(12 * ROWS * R * COLS, 4 << 20),
    )(core, summed, keep(merged, pltpu.VMEM), received)


def factor_kernel(first_ref, second_ref, third_ref, fourth_ref, summed_ref, inverse_ref, own_ref, theirs_ref):
    gram = (first_ref[...] + second_ref[...]) + (third_ref[...] + fourth_ref[...])
    row = lax.broadcasted_iota(jnp.int32, (R, 2 * R), 0)
    lane = lax.broadcasted_iota(jnp.int32, (R, 2 * R), 1)
    unit = (lane - R == row).astype(jnp.float32)[:, R:]
    x = jnp.concatenate([gram, unit], axis=1)
    for j in range(R):
        ratio = x[:, j : j + 1] * (1.0 / x[j : j + 1, j : j + 1])
        x = x - jnp.where(row > j, ratio, 0.0) * x[j : j + 1]
    diagonal = jnp.sum(jnp.where(row == lane, x, 0.0), axis=1, keepdims=True)
    inverse = x[:, R:] / jnp.sqrt(diagonal)
    inverse_ref[...] = inverse
    ortho = jnp.dot(inverse, summed_ref[...], precision=HIGH, preferred_element_type=jnp.float32)
    own_ref[...] = ortho[:, :ROWS]
    theirs_ref[...] = ortho[:, ROWS:]


def factors(grams, summed):
    return pl.pallas_call(
        factor_kernel,
        in_specs=[IN_VMEM] * (NY + 1),
        out_specs=[IN_VMEM] * 3,
        compiler_params=PARAMS,
        out_shape=(vmem(R, R), vmem(R, ROWS), vmem(R, ROWS)),
        cost_estimate=cost(1 << 20, 12 << 20),
    )(*[keep(a, pltpu.VMEM) for a in grams], keep(summed, pltpu.VMEM))


def tail_kernel(which_ref, ortho_ref, q_in, merged_ref, *refs):
    error_hbm, q_hbm, ortho_hbm, errors, q_new, ortho_sem, out_sems = refs[-7:]
    which = which_ref[0]
    outward = start([(ortho_ref, ortho_hbm.at[which])], ortho_sem)
    rounded_p = ortho_ref[...].astype(jnp.bfloat16)
    for j in range(CHUNKS):
        q = jnp.concatenate([q_in[j * PER + i] for i in range(PER)], axis=1)
        q_new[:, chunk(j)] = q
        approx = lax.dot_general(
            rounded_p, q.astype(jnp.bfloat16), (((0,), (0,)), ((), ())), preferred_element_type=jnp.float32
        )
        error = merged_ref[which, :, chunk(j)].astype(jnp.float32) - approx
        errors[:, chunk(j)] = error.astype(jnp.bfloat16)
        outward += start(
            [
                (q_new.at[:, chunk(j)], q_hbm.at[which, :, chunk(j)]),
                (errors.at[:, chunk(j)], error_hbm.at[0, which, :, chunk(j)]),
            ],
            out_sems.at[j],
        )
    finish(outward)


def tail(which, ortho, q, merged, before=()):
    return pl.pallas_call(
        tail_kernel,
        in_specs=[IN_SMEM, IN_VMEM, IN_VMEM, IN_VMEM] + [IN_HBM] * len(before),
        out_specs=[IN_HBM, IN_HBM, IN_HBM],
        out_shape=(hbm(1, MATS, ROWS, COLS, dtype=jnp.bfloat16), hbm(MATS, R, COLS), hbm(MATS, R, ROWS)),
        input_output_aliases={4: 0, 5: 1, 6: 2} if before else {},
        scratch_shapes=[
            pltpu.VMEM((ROWS, COLS), jnp.bfloat16),
            pltpu.VMEM((R, COLS), jnp.float32),
            pltpu.SemaphoreType.DMA((1,)),
            pltpu.SemaphoreType.DMA((CHUNKS, 2)),
        ],
        compiler_params=PARAMS,
        cost_estimate=cost(2 * ROWS * R * COLS, 4 << 20),
    )(which, keep(ortho, pltpu.VMEM), keep(q, pltpu.VMEM), keep(merged, pltpu.VMEM), *before)


def local(grads, errors, q_init):
    core = lax.axis_index("c").astype(jnp.int32)
    own = core.reshape(1)
    other = (1 - core).reshape(1)

    merged, send, mine, theirs = left(own, grads, errors, q_init.transpose(0, 2, 1))
    terms = jnp.concatenate([mine, swap(theirs)], axis=1)
    terms, send = lax.optimization_barrier((jnp.broadcast_to(terms[None], (NX,) + terms.shape), send))
    received = swap(send)
    terms = sum_parts(exchange(terms, "x"), NV * NW)
    summed = jnp.sum(exchange(terms, ("v", "w")), axis=0)

    gram = jnp.einsum("kr,lr->kl", summed, summed, precision=HIGH)
    grams = [gram] + shifts(gram, "y", NY)

    half = exchange(right(own, summed, merged, received), ("x", "w", "y"))
    part = sum_parts(half, NV, after=grams)
    inverse, ortho, ortho_theirs = factors(grams, summed)
    part = exchange(part, "v")

    q_own = exchange(middle(part, inverse), ("x", "w", "y"))
    q_other = swap(q_own)
    first = tail(own, ortho, q_own, merged)
    ortho_other, first = lax.optimization_barrier((swap(ortho_theirs), first))
    error_new, q_t, orthonormal = tail(other, ortho_other, q_other, merged, first)
    return (error_new, q_t.transpose(0, 2, 1), orthonormal.transpose(0, 2, 1))


def solution(mesh):
    fine = Mesh(mesh.devices.reshape(NX, NV, NW, NY, NC), ("x", "v", "w", "y", "c"))
    big = P(("x", "v", "w"), None, ("y", "c"), None)
    return jax.shard_map(
        local,
        mesh=fine,
        in_specs=(big, big, P()),
        out_specs=(big, P(), P(None, ("y", "c"), None)),
        check_vma=False,
    )
```

time: 462 us -> 95.6 us (0.21)
  waiting for transfers between devices: 253 us -> 19.2 us
  blocking collectives: 167 us -> 40.1 us
  starting transfers between devices: 0.04 us -> 19.5 us
  Pallas kernels: 0 us -> 15.4 us
  other arithmetic: 15.3 us -> 0.09 us
  between operations: 14.1 us -> 0.71 us
  matrix products: 9.27 us -> 0.14 us
    psum x1 -> x0, waiting for transfers between devices: 253 us -> none  [local(): q_total = lax.psum(q_partial, ('dp', 'tensor'))]
    psum x2 -> x0, blocking collectives: 167 us -> none  [the longest x1 119 us: local(): summed = lax.psum(partial_value, 'dp')]
    all_to_all x0 -> x3, blocking collectives: none -> 40.1 us  [exchange(): return lax.all_to_all(a, axes, 0, 0)]
    pallas_call x0 -> x8, Pallas kernels: none -> 15.4 us  [the longest x2 4.48 us: tail(): pl.pallas_call(tail_kernel, in_specs=[IN_SMEM, IN_VMEM, IN_VMEM, IN_VMEM]...]
    ppermute x0 -> x7, waiting for transfers between devices: none -> 14.7 us  [the longest x3 13.1 us: shifts(): lax.ppermute(a, axis, [(i, (i + s) % size) for i in range(size)])]
    another operation x11 -> x0, other arithmetic: 13.4 us -> none  [the longest x6 7.18 us: local(): factor = jnp.linalg.cholesky(gram_matrix[matrix_index])]
    ppermute x0 -> x7, starting transfers between devices: none -> 10.9 us  [the longest x4 7.28 us: swap(): return lax.ppermute(a, 'c', [(0, 1), (1, 0)])]
    dot_general x4 -> x1, matrix products: 8.8 us -> 0.14 us  [local(): gram = jnp.einsum('kr,lr->kl', summed, summed, precision=HIGH)]
  transfers between devices with their start and end apart: 1 -> 9, of which waited for: 1 -> 6; matrix products, arithmetic and copies ran while one was open for 0% -> 0% of each run, Pallas kernels for 0% -> 5%
where the time goes in v4:
time: 95.6 us; the launch traced here: 95.1 us
  blocking collectives  40.1 us (42%)
  starting transfers between devices  19.5 us (20%)
  waiting for transfers between devices  19.2 us (20%)
  Pallas kernels  15.4 us (16%)
    all_to_all x3, blocking collectives, exchange(): return lax.all_to_all(a, axes, 0, 0)  40.1 us
    ppermute x3, waiting for transfers between devices, shifts(): lax.ppermute(a, axis, [(i, (i + s) % size) for i in range(size)])  13.1 us
    all_to_all x2, starting transfers between devices, exchange(): return lax.all_to_all(a, axes, 0, 0)  8.56 us
    ppermute x4, starting transfers between devices, swap(): return lax.ppermute(a, 'c', [(0, 1), (1, 0)])  7.28 us
    pallas_call x2, Pallas kernels, tail(): pl.pallas_call(tail_kernel, in_specs=[IN_SMEM, IN_VMEM, IN_VMEM, IN_VMEM]...  4.48 us
    all_to_all x2, waiting for transfers between devices, exchange(): return lax.all_to_all(a, axes, 0, 0)  4.45 us
    pallas_call x1, Pallas kernels, left(): pl.pallas_call(left_kernel, in_specs=[IN_SMEM, IN_HBM, IN_HBM, IN_HBM], o...  4.09 us
    ppermute x3, starting transfers between devices, shifts(): lax.ppermute(a, axis, [(i, (i + s) % size) for i in range(size)])  3.67 us
  transfers between devices with their start and end apart: 9, of which 6 were waited for; matrix products, arithmetic and copies ran while one was open for 0% of the time, Pallas kernels for 5%

profile of v4, /device:TPU:1, one launch (start us, length us, event | category | flops | bytes accessed | tf_op | source)
XLA Modules:
  0.0 95.1 jit_solution(11383020906353320280)
XLA Ops:
  0.6 4.1 %shard_map.58 = (bf16[2,64,8192]{2,1,0:T(8,128)(2,1)S(1)}, f32[64,8192]{1,0:T(8,128)}, f32[32,64]{1,0:T(8,128)S(1)}, f32[32,64]{1,0:T(8,128)S(1)}) custom-call(s32[1]{0:T(128)} %bitcast.1.core_ref.which_ref, bf16[1,2,64,8192]{3,2,1,0:T(8,128)(2,1)} %grads_hbm.1, bf16[1,2,64,8192]{3,2,1,0:T(8,128)(2,1)} %errors_hbm.1, bf16[2,32,8192]{2,1,0:T(8,128)(2,1)} %bitcast.8), custom_call_target="tpu_custom_call" | custom-call | flops 134217728 | bytes 9437184 | tf_op jit(solution)/shard_map/pallas_call | solution.py:116
  4.7 3.3 %collective-permute-start = (f32[32,64]{1,0:T(8,128)S(1)}, f32[32,64]{1,0:T(8,128)S(1)}, u32[]{:S(2)}, u32[]{:S(2)}) collective-permute-start(f32[32,64]{1,0:T(8,128)S(1)} %get-tuple-element.23), channel_id=1, source_target_pairs={{0,1},{1,0},{2,3},{3,2},{4,5},{5,4},{6,7},{7,6},{8,9},{9,8},{10,11... | collective-permute-start | bytes 24584 | tf_op jit(solution)/shard_map/ppermute | solution.py:48
  8.1 0.8 collective-permute-done
  8.9 0.1 pad_maximum_fusion
  9.0 0.4 collective-permute-start.5
  9.4 6.8 %all_to_all.25.parts_ref = f32[4,32,128]{2,1,0:T(8,128)S(1)} all-to-all(f32[4,32,128]{2,1,0:T(8,128)S(1)} %broadcast_in_dim.2), channel_id=1, replica_groups=mesh['x'=4,'v'=4,'w'=2,'y'=4,'c'=2] {'x'}, dimensions={0} | all-to-all | bytes 131072 | tf_op jit(solution)/shard_map/all_to_all | solution.py:56
  16.2 15.6 %all_to_all.26 = f32[8,32,128]{2,1,0:T(8,128)S(1)} all-to-all(f32[8,32,128]{2,1,0:T(8,128)S(1)} %shard_map.59), channel_id=1, replica_groups=mesh['x'=4,'v'=4,'w'=2,'y'=4,'c'=2] {'v','w'}, dimensions={0} | all-to-all | bytes 262144 | tf_op jit(solution)/shard_map/all_to_all | solution.py:56
  31.9 0.0 collective-permute-done.5.received_ref
  31.9 2.9 %shard_map.61 = f32[32,32,256]{2,1,0:T(8,128)} custom-call(s32[1]{0:T(128)} %bitcast.1.core_ref.which_ref, f32[32,128]{1,0:T(8,128)S(1)} %reduce_sum.9.summed_ref, bf16[2,64,8192]{2,1,0:T(8,128)(2,1)S(1)} %get-tuple-element.28.merged_ref, f32[64,8192]{1,0:T(8,128)} %collective-permute-done.5.received_ref), custom_call_target="tpu_custom_call" | custom-call | flops 201326592 | bytes 4194304 | tf_op jit(solution)/shard_map/pallas_call | solution.py:197
  34.8 5.2 %all-to-all-start.2 = ((f32[32,32,256]{2,1,0:T(8,128)}), f32[32,32,256]{2,1,0:T(8,128)S(1)}, u32[]{:S(2)}, u32[]{:S(2)}) async-start(f32[32,32,256]{2,1,0:T(8,128)} %shard_map.61), calls=%async_computation.2 | async-start | bytes 2097152 | tf_op jit(solution)/shard_map/all_to_all | solution.py:56
  40.1 0.1 fusion.first_ref.refs_0_
  40.2 2.5 %collective-permute-start.3 = (f32[32,32]{1,0:T(8,128)S(1)}, f32[32,32]{1,0:T(8,128)S(1)}, u32[]{:S(2)}, u32[]{:S(2)}) collective-permute-start(f32[32,32]{1,0:T(8,128)S(1)} %fusion.first_ref.refs_0_), channel_id=1, source_target_pairs={{0,6},{2,0},{4,2},{6,4},{1,7},{3,1},{5,3},{7,5},{8,14},{10,8},{12,... | collective-permute-start | bytes 12296 | tf_op jit(solution)/shard_map/ppermute | solution.py:52
  42.7 0.6 collective-permute-start.2
  43.3 0.6 collective-permute-start.1
  43.9 0.0 collective-permute-done.3.fourth_ref.refs_3_
  43.9 4.7 %collective-permute-done.2.third_ref.refs_2_ = f32[32,32]{1,0:T(8,128)S(1)} collective-permute-done((f32[32,32]{1,0:T(8,128)S(1)}, f32[32,32]{1,0:T(8,128)S(1)}, u32[]{:S(2)}, u32[]{:S(2)}) %collective-permute-start.2) | collective-permute-done | bytes 4128 | tf_op jit(solution)/shard_map/ppermute | solution.py:52
  48.6 8.3 %collective-permute-done.1.second_ref.refs_1_ = f32[32,32]{1,0:T(8,128)S(1)} collective-permute-done((f32[32,32]{1,0:T(8,128)S(1)}, f32[32,32]{1,0:T(8,128)S(1)}, u32[]{:S(2)}, u32[]{:S(2)}) %collective-permute-start.1) | collective-permute-done | bytes 4128 | tf_op jit(solution)/shard_map/ppermute | solution.py:52
  57.0 0.0 all-to-all-done.2.parts_ref
  57.0 0.7 shard_map.62
  57.7 3.3 %all-to-all-start.3 = ((f32[4,32,256]{2,1,0:T(8,128)}), f32[4,32,256]{2,1,0:T(8,128)S(1)}, u32[]{:S(2)}, u32[]{:S(2)}) async-start(f32[4,32,256]{2,1,0:T(8,128)} %shard_map.62), calls=%async_computation.3 | async-start | bytes 262144 | tf_op jit(solution)/shard_map/all_to_all | solution.py:56
  61.0 2.9 %shard_map.60 = (f32[32,32]{1,0:T(8,128)S(1)}, f32[32,64]{1,0:T(8,128)S(1)}, f32[32,64]{1,0:T(8,128)S(1)}) custom-call(f32[32,32]{1,0:T(8,128)S(1)} %fusion.first_ref.refs_0_, f32[32,32]{1,0:T(8,128)S(1)} %collective-permute-done.1.second_ref.refs_1_, f32[32,32]{1,0:T(8,128)S(1)} %collective-permute-done.2.third_ref.refs_2_, ...), custom_call_target="tpu_custom_call" | custom-call | flops 1048576 | bytes 12582912 | tf_op jit(solution)/shard_map/pallas_call | solution.py:226
  63.9 4.4 %all-to-all-done.3.parts_ref = f32[4,32,256]{2,1,0:T(8,128)S(1)} async-done(((f32[4,32,256]{2,1,0:T(8,128)}), f32[4,32,256]{2,1,0:T(8,128)S(1)}, u32[]{:S(2)}, u32[]{:S(2)}) %all-to-all-start.3) | async-done | bytes 131104 | tf_op jit(solution)/shard_map/all_to_all | solution.py:56
  68.4 0.3 shard_map.63
  68.6 17.6 %all_to_all.27.q_in = f32[32,32,256]{2,1,0:T(8,128)S(1)} all-to-all(f32[32,32,256]{2,1,0:T(8,128)S(1)} %shard_map.63), channel_id=1, replica_groups=mesh['x'=4,'v'=4,'w'=2,'y'=4,'c'=2] {'x','w','y'}, dimensions={0} | all-to-all | bytes 2097152 | tf_op jit(solution)/shard_map/all_to_all | solution.py:56
  86.3 3.5 %collective-permute-start.6 = (f32[32,32,256]{2,1,0:T(8,128)S(1)}, f32[32,32,256]{2,1,0:T(8,128)}, u32[]{:S(2)}, u32[]{:S(2)}) collective-permute-start(f32[32,32,256]{2,1,0:T(8,128)S(1)} %all_to_all.27.q_in), channel_id=1, source_target_pairs={{0,1},{1,0},{2,3},{3,2},{4,5},{5,4},{6,7},{7,6},{8,9},{9,8},{10,11... | collective-permute-start | bytes 3145736 | tf_op jit(solution)/shard_map/ppermute | solution.py:48
  89.8 0.0 collective-permute-start.4
  89.8 1.6 %shard_map.64 = (bf16[1,2,64,8192]{3,2,1,0:T(8,128)(2,1)}, f32[2,32,8192]{2,1,0:T(8,128)}, f32[2,32,64]{2,1,0:T(8,128)}) custom-call(s32[1]{0:T(128)} %bitcast.1.core_ref.which_ref, f32[32,64]{1,0:T(8,128)S(1)} %get-tuple-element.27.ortho_ref, f32[32,32,256]{2,1,0:T(8,128)S(1)} %all_to_all.27.q_in, bf16[2,64,8192]{2,1,0:T(8,128)(2,1)S(1)} %get-tuple-element.28.merged_ref), custom_call_target="tpu_custom_call" | custom-call | flops 33554432 | bytes 4194304 | tf_op jit(solution)/shard_map/pallas_call | solution.py:260
  91.5 0.5 collective-permute-done.4.ortho_ref
  92.0 0.3 collective-permute-done.6.q_in
  92.3 2.9 %shard_map.65 = (bf16[1,2,64,8192]{3,2,1,0:T(8,128)(2,1)}, f32[2,32,8192]{2,1,0:T(8,128)}, f32[2,32,64]{2,1,0:T(8,128)}) custom-call(s32[1]{0:T(128)} %bitcast.which_ref, f32[32,64]{1,0:T(8,128)S(1)} %collective-permute-done.4.ortho_ref, f32[32,32,256]{2,1,0:T(8,128)} %collective-permute-done.6.q_in, ...), custom_call_target="tpu_custom_call", output_to_operand_aliasing={{0}: (4, {}), {1}: (5, {}), {2}: (6, {})} | custom-call | flops 33554432 | bytes 4194304 | tf_op jit(solution)/shard_map/pallas_call | solution.py:260
  (3 shorter events, 0.0 us)
Async XLA Ops:
  4.7 4.2 %collective-permute-start = (f32[32,64]{1,0:T(8,128)S(1)}, f32[32,64]{1,0:T(8,128)S(1)}, u32[]{:S(2)}, u32[]{:S(2)}) collective-permute-start(f32[32,64]{1,0:T(8,128)S(1)} %get-tuple-element.23), channel_id=1, source_target_pairs={{0,1},{1,0},{2,3},{3,2},{4,5},{5,4},{6,7},{7,6},{8,9},{9,8},{10,11... | collective-permute-start | bytes 24584 | tf_op jit(solution)/shard_map/ppermute | solution.py:48
  9.0 22.9 %collective-permute-start.5 = (f32[64,8192]{1,0:T(8,128)}, f32[64,8192]{1,0:T(8,128)}, u32[]{:S(2)}, u32[]{:S(2)}) collective-permute-start(f32[64,8192]{1,0:T(8,128)} %get-tuple-element.29), channel_id=1, source_target_pairs={{0,1},{1,0},{2,3},{3,2},{4,5},{5,4},{6,7},{7,6},{8,9},{9,8},{10,11... | collective-permute-start | bytes 6291464 | tf_op jit(solution)/shard_map/ppermute | solution.py:48
  34.8 22.2 %all-to-all-start.2 = ((f32[32,32,256]{2,1,0:T(8,128)}), f32[32,32,256]{2,1,0:T(8,128)S(1)}, u32[]{:S(2)}, u32[]{:S(2)}) async-start(f32[32,32,256]{2,1,0:T(8,128)} %shard_map.61), calls=%async_computation.2 | async-start | bytes 2097152 | tf_op jit(solution)/shard_map/all_to_all | solution.py:56
  40.2 3.7 %collective-permute-start.3 = (f32[32,32]{1,0:T(8,128)S(1)}, f32[32,32]{1,0:T(8,128)S(1)}, u32[]{:S(2)}, u32[]{:S(2)}) collective-permute-start(f32[32,32]{1,0:T(8,128)S(1)} %fusion.first_ref.refs_0_), channel_id=1, source_target_pairs={{0,6},{2,0},{4,2},{6,4},{1,7},{3,1},{5,3},{7,5},{8,14},{10,8},{12,... | collective-permute-start | bytes 12296 | tf_op jit(solution)/shard_map/ppermute | solution.py:52
  42.7 5.9 %collective-permute-start.2 = (f32[32,32]{1,0:T(8,128)S(1)}, f32[32,32]{1,0:T(8,128)S(1)}, u32[]{:S(2)}, u32[]{:S(2)}) collective-permute-start(f32[32,32]{1,0:T(8,128)S(1)} %fusion.first_ref.refs_0_), channel_id=1, source_target_pairs={{0,4},{2,6},{4,0},{6,2},{1,5},{3,7},{5,1},{7,3},{8,12},{10,14},{12... | collective-permute-start | bytes 12296 | tf_op jit(solution)/shard_map/ppermute | solution.py:52
  43.3 13.7 %collective-permute-start.1 = (f32[32,32]{1,0:T(8,128)S(1)}, f32[32,32]{1,0:T(8,128)S(1)}, u32[]{:S(2)}, u32[]{:S(2)}) collective-permute-start(f32[32,32]{1,0:T(8,128)S(1)} %fusion.first_ref.refs_0_), channel_id=1, source_target_pairs={{0,2},{2,4},{4,6},{6,0},{1,3},{3,5},{5,7},{7,1},{8,10},{10,12},{12... | collective-permute-start | bytes 12296 | tf_op jit(solution)/shard_map/ppermute | solution.py:52
  57.7 10.6 %all-to-all-start.3 = ((f32[4,32,256]{2,1,0:T(8,128)}), f32[4,32,256]{2,1,0:T(8,128)S(1)}, u32[]{:S(2)}, u32[]{:S(2)}) async-start(f32[4,32,256]{2,1,0:T(8,128)} %shard_map.62), calls=%async_computation.3 | async-start | bytes 262144 | tf_op jit(solution)/shard_map/all_to_all | solution.py:56
  86.3 6.0 %collective-permute-start.6 = (f32[32,32,256]{2,1,0:T(8,128)S(1)}, f32[32,32,256]{2,1,0:T(8,128)}, u32[]{:S(2)}, u32[]{:S(2)}) collective-permute-start(f32[32,32,256]{2,1,0:T(8,128)S(1)} %all_to_all.27.q_in), channel_id=1, source_target_pairs={{0,1},{1,0},{2,3},{3,2},{4,5},{5,4},{6,7},{7,6},{8,9},{9,8},{10,11... | collective-permute-start | bytes 3145736 | tf_op jit(solution)/shard_map/ppermute | solution.py:48
  89.8 2.2 %collective-permute-start.4 = (f32[32,64]{1,0:T(8,128)S(1)}, f32[32,64]{1,0:T(8,128)S(1)}, u32[]{:S(2)}, u32[]{:S(2)}) collective-permute-start(f32[32,64]{1,0:T(8,128)S(1)} %get-tuple-element.26), channel_id=1, source_target_pairs={{0,1},{1,0},{2,3},{3,2},{4,5},{5,4},{6,7},{7,6},{8,9},{9,8},{10,11... | collective-permute-start | bytes 24584 | tf_op jit(solution)/shard_map/ppermute | solution.py:48

commit v5 on v4

--- a/solution.py
+++ b/solution.py
@@ -81,11 +81,11 @@
 
 
 def left_kernel(
-    core_ref, grads_hbm, errors_hbm, q_hbm, merged_ref, send_ref, mine_ref, theirs_ref, grads, errors, q, in_sems
+    core_ref, grads_hbm, errors_hbm, q_hbm, own_ref, other_ref, send_hbm, mine_ref, theirs_ref, grads, errors, q, send, in_sems, out_sems
 ):
     core = core_ref[0]
-    def fetch(j):
-        return start(
+    inward = [
+        start(
             [
                 (grads_hbm.at[0, :, :, chunk(j)], grads.at[:, :, chunk(j)]),
                 (errors_hbm.at[0, :, :, chunk(j)], errors.at[:, :, chunk(j)]),
@@ -93,33 +93,38 @@
             ],
             in_sems.at[j],
         )
-
-    inward = [fetch(j) for j in range(AHEAD)]
+        for j in range(CHUNKS)
+    ]
+    outward = []
     totals = [jnp.zeros((R, ROWS), jnp.float32) for _ in range(MATS)]
     for j in range(CHUNKS):
         finish(inward[j])
-        if j + AHEAD < CHUNKS:
-            inward.append(fetch(j + AHEAD))
-        for m in range(MATS):
+        for i, m in enumerate((core, 1 - core)):
             total = grads[m, :, chunk(j)].astype(jnp.float32) + errors[m, :, chunk(j)].astype(jnp.float32)
-            value = total.astype(jnp.bfloat16)
-            merged_ref[m, :, chunk(j)] = value
-            totals[m] += lax.dot_general(
-                q[m, :, chunk(j)], value, (((1,), (1,)), ((), ())), preferred_element_type=jnp.float32
+            merged = total.astype(jnp.bfloat16)
+            totals[i] += lax.dot_general(
+                q[m, :, chunk(j)], merged, (((1,), (1,)), ((), ())), preferred_element_type=jnp.float32
             )
-        send_ref[:, chunk(j)] = merged_ref[1 - core, :, chunk(j)].astype(jnp.float32)
-    mine_ref[...] = jnp.where(core == 0, totals[0], totals[1])
-    theirs_ref[...] = jnp.where(core == 0, totals[1], totals[0])
+            if i == 0:
+                own_ref[:, chunk(j)] = merged
+            else:
+                other_ref[:, chunk(j)] = merged
+                send[:, chunk(j)] = merged.astype(jnp.float32)
+        outward += start([(send.at[:, chunk(j)], send_hbm.at[:, chunk(j)])], out_sems.at[j])
+    mine_ref[...] = totals[0]
+    theirs_ref[...] = totals[1]
+    finish(outward)
 
 
 def left(core, grads, errors, q_t):
     return pl.pallas_call(
         left_kernel,
         in_specs=[IN_SMEM, IN_HBM, IN_HBM, IN_HBM],
-        out_specs=[IN_VMEM, IN_VMEM, IN_VMEM, IN_VMEM],
+        out_specs=[IN_VMEM, IN_VMEM, IN_HBM, IN_VMEM, IN_VMEM],
         out_shape=(
-            vmem(MATS, ROWS, COLS, dtype=jnp.bfloat16),
-            vmem(ROWS, COLS),
+            vmem(ROWS, COLS, dtype=jnp.bfloat16),
+            vmem(ROWS, COLS, dtype=jnp.bfloat16),
+            hbm(ROWS, COLS),
             vmem(R, ROWS),
             vmem(R, ROWS),
         ),
@@ -127,7 +132,9 @@
             pltpu.VMEM((MATS, ROWS, COLS), jnp.bfloat16),
             pltpu.VMEM((MATS, ROWS, COLS), jnp.bfloat16),
             pltpu.VMEM((MATS, R, COLS), jnp.bfloat16),
+            pltpu.VMEM((ROWS, COLS), jnp.float32),
             pltpu.SemaphoreType.DMA((CHUNKS, 3)),
+            pltpu.SemaphoreType.DMA((CHUNKS, 1)),
         ],
         compiler_params=PARAMS,
         cost_estimate=cost(1 << 27, 9 << 20),
@@ -144,23 +151,44 @@
 def sum_kernel(parts_ref, *refs):
     out_ref = refs[-1]
     value = added(parts_ref)
-    for copy in range(out_ref.shape[0]):
-        out_ref[copy] = value
-
-
-def sum_parts(parts, count, after=()):
+    if len(out_ref.shape) == len(value.shape):
+        out_ref[...] = value
+    else:
+        for copy in range(out_ref.shape[0]):
+            out_ref[copy] = value
+
+
+def sum_parts(parts, count=None, after=()):
+    shape = parts.shape[1:] if count is None else (count,) + parts.shape[1:]
     return pl.pallas_call(
         sum_kernel,
         in_specs=[IN_VMEM] + [IN_VMEM] * len(after),
         out_specs=IN_VMEM,
-        out_shape=f32(count, *parts.shape[1:]),
+        out_shape=f32(*shape),
         compiler_params=PARAMS,
         cost_estimate=cost(1 << 18, 2 << 20),
     )(parts, *[keep(a, pltpu.VMEM) for a in after])
 
 
-def middle_kernel(parts_ref, inverse_ref, out_ref):
-    total = added(parts_ref)
+def four_kernel(first_ref, second_ref, third_ref, fourth_ref, out_ref):
+    value = (first_ref[...] + second_ref[...]) + (third_ref[...] + fourth_ref[...])
+    for copy in range(out_ref.shape[0]):
+        out_ref[copy] = value
+
+
+def sum_four(parts, count):
+    return pl.pallas_call(
+        four_kernel,
+        in_specs=[IN_VMEM] * 4,
+        out_specs=IN_VMEM,
+        out_shape=f32(count, *parts[0].shape),
+        compiler_params=PARAMS,
+        cost_estimate=cost(1 << 18, 2 << 20),
+    )(*parts)
+
+
+def middle_kernel(first_ref, second_ref, third_ref, fourth_ref, inverse_ref, out_ref):
+    total = (first_ref[...] + second_ref[...]) + (third_ref[...] + fourth_ref[...])
     q = jnp.dot(inverse_ref[...], total, precision=HIGH, preferred_element_type=jnp.float32) * (1.0 / DP)
     for copy in range(GROUP):
         out_ref[copy] = q
@@ -169,21 +197,20 @@
 def middle(parts, inverse):
     return pl.pallas_call(
         middle_kernel,
-        in_specs=[IN_VMEM, IN_VMEM],
+        in_specs=[IN_VMEM] * (NV + 1),
         out_specs=IN_VMEM,
         out_shape=vmem(GROUP, R, BLOCK),
         compiler_params=PARAMS,
         cost_estimate=cost(1 << 20, 2 << 20),
-    )(parts, inverse)
-
-
-def right_kernel(core_ref, summed_ref, merged_ref, received_ref, out_ref, terms, out_sems):
-    core = core_ref[0]
+    )(*parts, inverse)
+
+
+def right_kernel(summed_ref, merged_ref, received_ref, out_ref, terms, out_sems):
     pieces = jnp.concatenate(split3(summed_ref[...]), axis=0)
     outward = []
     for j in range(CHUNKS):
         both = jnp.concatenate(
-            [merged_ref[core, :, chunk(j)], received_ref[:, chunk(j)].astype(jnp.bfloat16)], axis=0
+            [merged_ref[:, chunk(j)], received_ref[:, chunk(j)].astype(jnp.bfloat16)], axis=0
         )
         products = jnp.dot(pieces, both, preferred_element_type=jnp.float32)
         value = products[:R] + (products[R : 2 * R] + products[2 * R :])
@@ -193,16 +220,16 @@
     finish(outward)
 
 
-def right(core, summed, merged, received):
+def right(summed, merged, received):
     return pl.pallas_call(
         right_kernel,
-        in_specs=[IN_SMEM, IN_VMEM, IN_VMEM, IN_VMEM],
+        in_specs=[IN_VMEM, IN_VMEM, IN_VMEM],
         out_specs=IN_HBM,
         out_shape=hbm(GROUP, R, BLOCK),
         scratch_shapes=[pltpu.VMEM((GROUP, R, BLOCK), jnp.float32), pltpu.SemaphoreType.DMA((CHUNKS, 1))],
         compiler_params=PARAMS,
         cost_estimate=cost(12 * ROWS * R * COLS, 4 << 20),
-    )(core, summed, keep(merged, pltpu.VMEM), received)
+    )(summed, keep(merged, pltpu.VMEM), received)
 
 
 def factor_kernel(first_ref, second_ref, third_ref, fourth_ref, summed_ref, inverse_ref, own_ref, theirs_ref):
@@ -244,7 +271,7 @@
         approx = lax.dot_general(
             rounded_p, q.astype(jnp.bfloat16), (((0,), (0,)), ((), ())), preferred_element_type=jnp.float32
         )
-        error = merged_ref[which, :, chunk(j)].astype(jnp.float32) - approx
+        error = merged_ref[:, chunk(j)].astype(jnp.float32) - approx
         errors[:, chunk(j)] = error.astype(jnp.bfloat16)
         outward += start(
             [
@@ -279,26 +306,27 @@
     own = core.reshape(1)
     other = (1 - core).reshape(1)
 
-    merged, send, mine, theirs = left(own, grads, errors, q_init.transpose(0, 2, 1))
+    merged, merged_other, send, mine, theirs = left(own, grads, errors, q_init.transpose(0, 2, 1))
     terms = jnp.concatenate([mine, swap(theirs)], axis=1)
-    terms, send = lax.optimization_barrier((jnp.broadcast_to(terms[None], (NX,) + terms.shape), send))
+    terms, send = lax.optimization_barrier((terms, send))
+    parts = [terms] + shifts(terms, "x", NX)
     received = swap(send)
-    terms = sum_parts(exchange(terms, "x"), NV * NW)
+    terms = sum_four(parts, NV * NW)
     summed = jnp.sum(exchange(terms, ("v", "w")), axis=0)
 
     gram = jnp.einsum("kr,lr->kl", summed, summed, precision=HIGH)
     grams = [gram] + shifts(gram, "y", NY)
 
-    half = exchange(right(own, summed, merged, received), ("x", "w", "y"))
-    part = sum_parts(half, NV, after=grams)
+    half = exchange(right(summed, merged, received), ("x", "w", "y"))
+    part = sum_parts(half, after=grams)
     inverse, ortho, ortho_theirs = factors(grams, summed)
-    part = exchange(part, "v")
-
-    q_own = exchange(middle(part, inverse), ("x", "w", "y"))
+    parts = [part] + shifts(part, "v", NV)
+
+    q_own = exchange(middle(parts, inverse), ("x", "w", "y"))
     q_other = swap(q_own)
     first = tail(own, ortho, q_own, merged)
     ortho_other, first = lax.optimization_barrier((swap(ortho_theirs), first))
-    error_new, q_t, orthonormal = tail(other, ortho_other, q_other, merged, first)
+    error_new, q_t, orthonormal = tail(other, ortho_other, q_other, merged_other, first)
     return (error_new, q_t.transpose(0, 2, 1), orthonormal.transpose(0, 2, 1))
 
 

time: 95.6 us -> 91.7 us (0.959)
  starting transfers between devices: 19.5 us -> 25.2 us
  blocking collectives: 40.1 us -> 35.4 us
  waiting for transfers between devices: 19.2 us -> 15.3 us
    ppermute x3 -> x9, starting transfers between devices: 3.67 us -> 11.6 us  [shifts(): lax.ppermute(a, axis, [(i, (i + s) % size) for i in range(size)])]
    all_to_all x3 -> x2, blocking collectives: 40.1 us -> 35.4 us  [exchange(): return lax.all_to_all(a, axes, 0, 0)]
    all_to_all x2 -> x1, waiting for transfers between devices: 4.45 us -> 1.43 us  [exchange(): return lax.all_to_all(a, axes, 0, 0)]
    all_to_all x2 -> x1, starting transfers between devices: 8.56 us -> 5.73 us  [exchange(): return lax.all_to_all(a, axes, 0, 0)]
    ppermute x3 -> x9, waiting for transfers between devices: 13.1 us -> 12.2 us  [shifts(): lax.ppermute(a, axis, [(i, (i + s) % size) for i in range(size)])]
    pallas_call x2 -> x3, Pallas kernels: 3.18 us -> 3.19 us  [the longest x1 2.91 us: right(): pl.pallas_call(right_kernel, in_specs=[IN_VMEM, IN_VMEM, IN_VMEM], out_sp...]
  transfers between devices with their start and end apart: 9 -> 14, of which waited for: 6 -> 9; matrix products, arithmetic and copies ran while one was open for 0% -> 0% of each run, Pallas kernels for 5% -> 5%
where the time goes in v5:
time: 91.7 us; the launch traced here: 91.4 us
  blocking collectives  35.4 us (39%)
  starting transfers between devices  25.2 us (27%)
  waiting for transfers between devices  15.3 us (17%)
  Pallas kernels  14.5 us (16%)
    all_to_all x2, blocking collectives, exchange(): return lax.all_to_all(a, axes, 0, 0)  35.4 us
    ppermute x9, waiting for transfers between devices, shifts(): lax.ppermute(a, axis, [(i, (i + s) % size) for i in range(size)])  12.2 us
    ppermute x9, starting transfers between devices, shifts(): lax.ppermute(a, axis, [(i, (i + s) % size) for i in range(size)])  11.6 us
    ppermute x4, starting transfers between devices, swap(): return lax.ppermute(a, 'c', [(0, 1), (1, 0)])  7.81 us
    all_to_all x1, starting transfers between devices, exchange(): return lax.all_to_all(a, axes, 0, 0)  5.73 us
    pallas_call x2, Pallas kernels, tail(): pl.pallas_call(tail_kernel, in_specs=[IN_SMEM, IN_VMEM, IN_VMEM, IN_VMEM]...  4.48 us
    pallas_call x1, Pallas kernels, left(): pl.pallas_call(left_kernel, in_specs=[IN_SMEM, IN_HBM, IN_HBM, IN_HBM], o...  3.91 us
    pallas_call x1, Pallas kernels, right(): pl.pallas_call(right_kernel, in_specs=[IN_VMEM, IN_VMEM, IN_VMEM], out_sp...  2.91 us
  transfers between devices with their start and end apart: 14, of which 9 were waited for; matrix products, arithmetic and copies ran while one was open for 0% of the time, Pallas kernels for 5%

profile of v5, /device:TPU:1, one launch (start us, length us, event | category | flops | bytes accessed | tf_op | source)
XLA Modules:
  0.0 91.4 jit_solution(15070973653020787134)
XLA Ops:
  0.6 3.9 %shard_map.58 = (bf16[64,8192]{1,0:T(8,128)(2,1)S(1)}, bf16[64,8192]{1,0:T(8,128)(2,1)S(1)}, f32[64,8192]{1,0:T(8,128)}, f32[32,64]{1,0:T(8,128)S(1)}, f32[32,64]{1,0:T(8,128)S(1)}) custom-call(s32[1]{0:T(128)} %bitcast.1.core_ref.which_ref, bf16[1,2,64,8192]{3,2,1,0:T(8,128)(2,1)} %grads_hbm.1, bf16[1,2,64,8192]{3,2,1,0:T(8,128)(2,1)} %errors_hbm.1, ...), custom_call_target="tpu_custom_call" | custom-call | flops 134217728 | bytes 9437184 | tf_op jit(solution)/shard_map/pallas_call | solution.py:120
  4.6 3.3 %collective-permute-start = (f32[32,64]{1,0:T(8,128)S(1)}, f32[32,64]{1,0:T(8,128)S(1)}, u32[]{:S(2)}, u32[]{:S(2)}) collective-permute-start(f32[32,64]{1,0:T(8,128)S(1)} %get-tuple-element.24), channel_id=1, source_target_pairs={{0,1},{1,0},{2,3},{3,2},{4,5},{5,4},{6,7},{7,6},{8,9},{9,8},{10,11... | collective-permute-start | bytes 24584 | tf_op jit(solution)/shard_map/ppermute | solution.py:48
  7.9 0.8 collective-permute-done
  8.7 0.1 pad_maximum_fusion.first_ref
  8.8 0.4 collective-permute-start.8
  9.2 0.7 collective-permute-start.3
  9.9 0.5 collective-permute-start.2
  10.4 0.6 collective-permute-start.1
  11.0 0.7 collective-permute-done.3.fourth_ref
  11.8 2.2 %collective-permute-done.2.third_ref = f32[32,128]{1,0:T(8,128)S(1)} collective-permute-done((f32[32,128]{1,0:T(8,128)S(1)}, f32[32,128]{1,0:T(8,128)S(1)}, u32[]{:S(2)}, u32[]{:S(2)}) %collective-permute-start.2) | collective-permute-done | bytes 16416 | tf_op jit(solution)/shard_map/ppermute | solution.py:52
  14.0 0.2 collective-permute-done.1.second_ref
  14.2 16.0 %all_to_all.15 = f32[8,32,128]{2,1,0:T(8,128)S(1)} all-to-all(f32[8,32,128]{2,1,0:T(8,128)S(1)} %shard_map.59), channel_id=1, replica_groups=mesh['x'=4,'v'=4,'w'=2,'y'=4,'c'=2] {'v','w'}, dimensions={0} | all-to-all | bytes 262144 | tf_op jit(solution)/shard_map/all_to_all | solution.py:56
  30.3 0.0 collective-permute-done.8.received_ref
  30.3 2.9 %shard_map.61 = f32[32,32,256]{2,1,0:T(8,128)} custom-call(f32[32,128]{1,0:T(8,128)S(1)} %reduce_sum.9.summed_ref, bf16[64,8192]{1,0:T(8,128)(2,1)S(1)} %get-tuple-element.29.merged_ref, f32[64,8192]{1,0:T(8,128)} %collective-permute-done.8.received_ref), custom_call_target="tpu_custom_call" | custom-call | flops 201326592 | bytes 4194304 | tf_op jit(solution)/shard_map/pallas_call | solution.py:224
  33.2 5.7 %all-to-all-start.1 = ((f32[32,32,256]{2,1,0:T(8,128)}), f32[32,32,256]{2,1,0:T(8,128)S(1)}, u32[]{:S(2)}, u32[]{:S(2)}) async-start(f32[32,32,256]{2,1,0:T(8,128)} %shard_map.61), calls=%async_computation.1 | async-start | bytes 2097152 | tf_op jit(solution)/shard_map/all_to_all | solution.py:56
  39.0 0.1 fusion.first_ref.refs_0_
  39.1 2.5 %collective-permute-start.6 = (f32[32,32]{1,0:T(8,128)S(1)}, f32[32,32]{1,0:T(8,128)S(1)}, u32[]{:S(2)}, u32[]{:S(2)}) collective-permute-start(f32[32,32]{1,0:T(8,128)S(1)} %fusion.first_ref.refs_0_), channel_id=1, source_target_pairs={{0,6},{2,0},{4,2},{6,4},{1,7},{3,1},{5,3},{7,5},{8,14},{10,8},{12,... | collective-permute-start | bytes 12296 | tf_op jit(solution)/shard_map/ppermute | solution.py:52
  41.6 0.6 collective-permute-start.5
  42.2 0.6 collective-permute-start.4
  42.8 0.0 collective-permute-done.6.fourth_ref.refs_3_
  42.8 4.7 %collective-permute-done.5.third_ref.refs_2_ = f32[32,32]{1,0:T(8,128)S(1)} collective-permute-done((f32[32,32]{1,0:T(8,128)S(1)}, f32[32,32]{1,0:T(8,128)S(1)}, u32[]{:S(2)}, u32[]{:S(2)}) %collective-permute-start.5) | collective-permute-done | bytes 4128 | tf_op jit(solution)/shard_map/ppermute | solution.py:52
  47.5 4.3 %collective-permute-done.4.second_ref.refs_1_ = f32[32,32]{1,0:T(8,128)S(1)} collective-permute-done((f32[32,32]{1,0:T(8,128)S(1)}, f32[32,32]{1,0:T(8,128)S(1)}, u32[]{:S(2)}, u32[]{:S(2)}) %collective-permute-start.4) | collective-permute-done | bytes 4128 | tf_op jit(solution)/shard_map/ppermute | solution.py:52
  51.8 1.4 %all-to-all-done.1.parts_ref = f32[32,32,256]{2,1,0:T(8,128)S(1)} async-done(((f32[32,32,256]{2,1,0:T(8,128)}), f32[32,32,256]{2,1,0:T(8,128)S(1)}, u32[]{:S(2)}, u32[]{:S(2)}) %all-to-all-start.1) | async-done | bytes 1048608 | tf_op jit(solution)/shard_map/all_to_all | solution.py:56
  53.2 0.1 shard_map.62.first_ref
  53.3 0.1 collective-permute-start.11
  53.4 3.7 %collective-permute-start.10 = (f32[32,256]{1,0:T(8,128)S(1)}, f32[32,256]{1,0:T(8,128)S(1)}, u32[]{:S(2)}, u32[]{:S(2)}) collective-permute-start(f32[32,256]{1,0:T(8,128)S(1)} %shard_map.62.first_ref), channel_id=1, source_target_pairs={{0,32},{16,48},{32,0},{48,16},{1,33},{17,49},{33,1},{49,17},{2,34}... | collective-permute-start | bytes 98312 | tf_op jit(solution)/shard_map/ppermute | solution.py:52
  57.1 2.3 %collective-permute-start.9 = (f32[32,256]{1,0:T(8,128)S(1)}, f32[32,256]{1,0:T(8,128)S(1)}, u32[]{:S(2)}, u32[]{:S(2)}) collective-permute-start(f32[32,256]{1,0:T(8,128)S(1)} %shard_map.62.first_ref), channel_id=1, source_target_pairs={{0,16},{16,32},{32,48},{48,0},{1,17},{17,33},{33,49},{49,1},{2,18}... | collective-permute-start | bytes 98312 | tf_op jit(solution)/shard_map/ppermute | solution.py:52
  59.4 2.9 %shard_map.60 = (f32[32,32]{1,0:T(8,128)S(1)}, f32[32,64]{1,0:T(8,128)S(1)}, f32[32,64]{1,0:T(8,128)S(1)}) custom-call(f32[32,32]{1,0:T(8,128)S(1)} %fusion.first_ref.refs_0_, f32[32,32]{1,0:T(8,128)S(1)} %collective-permute-done.4.second_ref.refs_1_, f32[32,32]{1,0:T(8,128)S(1)} %collective-permute-done.5.third_ref.refs_2_, ...), custom_call_target="tpu_custom_call" | custom-call | flops 1048576 | bytes 12582912 | tf_op jit(solution)/shard_map/pallas_call | solution.py:253
  62.2 0.0 collective-permute-done.11.fourth_ref
  62.2 0.0 collective-permute-done.10.third_ref
  62.3 0.0 collective-permute-done.9.second_ref
  62.3 0.3 shard_map.63
  62.5 19.4 %all_to_all.16.q_in = f32[32,32,256]{2,1,0:T(8,128)S(1)} all-to-all(f32[32,32,256]{2,1,0:T(8,128)S(1)} %shard_map.63), channel_id=1, replica_groups=mesh['x'=4,'v'=4,'w'=2,'y'=4,'c'=2] {'x','w','y'}, dimensions={0} | all-to-all | bytes 2097152 | tf_op jit(solution)/shard_map/all_to_all | solution.py:56
  82.0 4.1 %collective-permute-start.12 = (f32[32,32,256]{2,1,0:T(8,128)S(1)}, f32[32,32,256]{2,1,0:T(8,128)}, u32[]{:S(2)}, u32[]{:S(2)}) collective-permute-start(f32[32,32,256]{2,1,0:T(8,128)S(1)} %all_to_all.16.q_in), channel_id=1, source_target_pairs={{0,1},{1,0},{2,3},{3,2},{4,5},{5,4},{6,7},{7,6},{8,9},{9,8},{10,11... | collective-permute-start | bytes 3145736 | tf_op jit(solution)/shard_map/ppermute | solution.py:48
  86.1 0.0 collective-permute-start.7
  86.1 1.6 %shard_map.64 = (bf16[1,2,64,8192]{3,2,1,0:T(8,128)(2,1)}, f32[2,32,8192]{2,1,0:T(8,128)}, f32[2,32,64]{2,1,0:T(8,128)}) custom-call(s32[1]{0:T(128)} %bitcast.1.core_ref.which_ref, f32[32,64]{1,0:T(8,128)S(1)} %get-tuple-element.28.ortho_ref, f32[32,32,256]{2,1,0:T(8,128)S(1)} %all_to_all.16.q_in, bf16[64,8192]{1,0:T(8,128)(2,1)S(1)} %get-tuple-element.29.merged_ref), custom_call_target="tpu_custom_call" | custom-call | flops 33554432 | bytes 4194304 | tf_op jit(solution)/shard_map/pallas_call | solution.py:287
  87.7 0.5 collective-permute-done.7.ortho_ref
  88.3 0.3 collective-permute-done.12.q_in
  88.5 2.9 %shard_map.65 = (bf16[1,2,64,8192]{3,2,1,0:T(8,128)(2,1)}, f32[2,32,8192]{2,1,0:T(8,128)}, f32[2,32,64]{2,1,0:T(8,128)}) custom-call(s32[1]{0:T(128)} %bitcast.which_ref, f32[32,64]{1,0:T(8,128)S(1)} %collective-permute-done.7.ortho_ref, f32[32,32,256]{2,1,0:T(8,128)} %collective-permute-done.12.q_in, ...), custom_call_target="tpu_custom_call", output_to_operand_aliasing={{0}: (4, {}), {1}: (5, {}), {2}: (6, {})} | custom-call | flops 33554432 | bytes 4194304 | tf_op jit(solution)/shard_map/pallas_call | solution.py:287
  (2 shorter events, 0.0 us)
Async XLA Ops:
  4.6 4.2 %collective-permute-start = (f32[32,64]{1,0:T(8,128)S(1)}, f32[32,64]{1,0:T(8,128)S(1)}, u32[]{:S(2)}, u32[]{:S(2)}) collective-permute-start(f32[32,64]{1,0:T(8,128)S(1)} %get-tuple-element.24), channel_id=1, source_target_pairs={{0,1},{1,0},{2,3},{3,2},{4,5},{5,4},{6,7},{7,6},{8,9},{9,8},{10,11... | collective-permute-start | bytes 24584 | tf_op jit(solution)/shard_map/ppermute | solution.py:48
  8.8 21.5 %collective-permute-start.8 = (f32[64,8192]{1,0:T(8,128)}, f32[64,8192]{1,0:T(8,128)}, u32[]{:S(2)}, u32[]{:S(2)}) collective-permute-start(f32[64,8192]{1,0:T(8,128)} %get-tuple-element.30), channel_id=1, source_target_pairs={{0,1},{1,0},{2,3},{3,2},{4,5},{5,4},{6,7},{7,6},{8,9},{9,8},{10,11... | collective-permute-start | bytes 6291464 | tf_op jit(solution)/shard_map/ppermute | solution.py:48
  9.2 2.6 %collective-permute-start.3 = (f32[32,128]{1,0:T(8,128)S(1)}, f32[32,128]{1,0:T(8,128)S(1)}, u32[]{:S(2)}, u32[]{:S(2)}) collective-permute-start(f32[32,128]{1,0:T(8,128)S(1)} %pad_maximum_fusion.first_ref), channel_id=1, source_target_pairs={{0,192},{64,0},{128,64},{192,128},{1,193},{65,1},{129,65},{193,129... | collective-permute-start | bytes 49160 | tf_op jit(solution)/shard_map/ppermute | solution.py:52
  9.9 4.1 %collective-permute-start.2 = (f32[32,128]{1,0:T(8,128)S(1)}, f32[32,128]{1,0:T(8,128)S(1)}, u32[]{:S(2)}, u32[]{:S(2)}) collective-permute-start(f32[32,128]{1,0:T(8,128)S(1)} %pad_maximum_fusion.first_ref), channel_id=1, source_target_pairs={{0,128},{64,192},{128,0},{192,64},{1,129},{65,193},{129,1},{193,65... | collective-permute-start | bytes 49160 | tf_op jit(solution)/shard_map/ppermute | solution.py:52
  10.4 3.8 %collective-permute-start.1 = (f32[32,128]{1,0:T(8,128)S(1)}, f32[32,128]{1,0:T(8,128)S(1)}, u32[]{:S(2)}, u32[]{:S(2)}) collective-permute-start(f32[32,128]{1,0:T(8,128)S(1)} %pad_maximum_fusion.first_ref), channel_id=1, source_target_pairs={{0,64},{64,128},{128,192},{192,0},{1,65},{65,129},{129,193},{193,1... | collective-permute-start | bytes 49160 | tf_op jit(solution)/shard_map/ppermute | solution.py:52
  33.2 20.0 %all-to-all-start.1 = ((f32[32,32,256]{2,1,0:T(8,128)}), f32[32,32,256]{2,1,0:T(8,128)S(1)}, u32[]{:S(2)}, u32[]{:S(2)}) async-start(f32[32,32,256]{2,1,0:T(8,128)} %shard_map.61), calls=%async_computation.1 | async-start | bytes 2097152 | tf_op jit(solution)/shard_map/all_to_all | solution.py:56
  39.1 3.7 %collective-permute-start.6 = (f32[32,32]{1,0:T(8,128)S(1)}, f32[32,32]{1,0:T(8,128)S(1)}, u32[]{:S(2)}, u32[]{:S(2)}) collective-permute-start(f32[32,32]{1,0:T(8,128)S(1)} %fusion.first_ref.refs_0_), channel_id=1, source_target_pairs={{0,6},{2,0},{4,2},{6,4},{1,7},{3,1},{5,3},{7,5},{8,14},{10,8},{12,... | collective-permute-start | bytes 12296 | tf_op jit(solution)/shard_map/ppermute | solution.py:52
  41.6 5.9 %collective-permute-start.5 = (f32[32,32]{1,0:T(8,128)S(1)}, f32[32,32]{1,0:T(8,128)S(1)}, u32[]{:S(2)}, u32[]{:S(2)}) collective-permute-start(f32[32,32]{1,0:T(8,128)S(1)} %fusion.first_ref.refs_0_), channel_id=1, source_target_pairs={{0,4},{2,6},{4,0},{6,2},{1,5},{3,7},{5,1},{7,3},{8,12},{10,14},{12... | collective-permute-start | bytes 12296 | tf_op jit(solution)/shard_map/ppermute | solution.py:52
  42.2 9.6 %collective-permute-start.4 = (f32[32,32]{1,0:T(8,128)S(1)}, f32[32,32]{1,0:T(8,128)S(1)}, u32[]{:S(2)}, u32[]{:S(2)}) collective-permute-start(f32[32,32]{1,0:T(8,128)S(1)} %fusion.first_ref.refs_0_), channel_id=1, source_target_pairs={{0,2},{2,4},{4,6},{6,0},{1,3},{3,5},{5,7},{7,1},{8,10},{10,12},{12... | collective-permute-start | bytes 12296 | tf_op jit(solution)/shard_map/ppermute | solution.py:52
  53.3 9.0 %collective-permute-start.11 = (f32[32,256]{1,0:T(8,128)S(1)}, f32[32,256]{1,0:T(8,128)S(1)}, u32[]{:S(2)}, u32[]{:S(2)}) collective-permute-start(f32[32,256]{1,0:T(8,128)S(1)} %shard_map.62.first_ref), channel_id=1, source_target_pairs={{0,48},{16,0},{32,16},{48,32},{1,49},{17,1},{33,17},{49,33},{2,50}... | collective-permute-start | bytes 98312 | tf_op jit(solution)/shard_map/ppermute | solution.py:52
  53.4 8.9 %collective-permute-start.10 = (f32[32,256]{1,0:T(8,128)S(1)}, f32[32,256]{1,0:T(8,128)S(1)}, u32[]{:S(2)}, u32[]{:S(2)}) collective-permute-start(f32[32,256]{1,0:T(8,128)S(1)} %shard_map.62.first_ref), channel_id=1, source_target_pairs={{0,32},{16,48},{32,0},{48,16},{1,33},{17,49},{33,1},{49,17},{2,34}... | collective-permute-start | bytes 98312 | tf_op jit(solution)/shard_map/ppermute | solution.py:52
  57.1 5.2 %collective-permute-start.9 = (f32[32,256]{1,0:T(8,128)S(1)}, f32[32,256]{1,0:T(8,128)S(1)}, u32[]{:S(2)}, u32[]{:S(2)}) collective-permute-start(f32[32,256]{1,0:T(8,128)S(1)} %shard_map.62.first_ref), channel_id=1, source_target_pairs={{0,16},{16,32},{32,48},{48,0},{1,17},{17,33},{33,49},{49,1},{2,18}... | collective-permute-start | bytes 98312 | tf_op jit(solution)/shard_map/ppermute | solution.py:52
  82.0 6.6 %collective-permute-start.12 = (f32[32,32,256]{2,1,0:T(8,128)S(1)}, f32[32,32,256]{2,1,0:T(8,128)}, u32[]{:S(2)}, u32[]{:S(2)}) collective-permute-start(f32[32,32,256]{2,1,0:T(8,128)S(1)} %all_to_all.16.q_in), channel_id=1, source_target_pairs={{0,1},{1,0},{2,3},{3,2},{4,5},{5,4},{6,7},{7,6},{8,9},{9,8},{10,11... | collective-permute-start | bytes 3145736 | tf_op jit(solution)/shard_map/ppermute | solution.py:48
  86.1 2.2 %collective-permute-start.7 = (f32[32,64]{1,0:T(8,128)S(1)}, f32[32,64]{1,0:T(8,128)S(1)}, u32[]{:S(2)}, u32[]{:S(2)}) collective-permute-start(f32[32,64]{1,0:T(8,128)S(1)} %get-tuple-element.27), channel_id=1, source_target_pairs={{0,1},{1,0},{2,3},{3,2},{4,5},{5,4},{6,7},{7,6},{8,9},{9,8},{10,11... | collective-permute-start | bytes 24584 | tf_op jit(solution)/shard_map/ppermute | solution.py:48

commit v6 on v5

--- a/solution.py
+++ b/solution.py
@@ -49,7 +49,7 @@
 
 
 def shifts(a, axis, size):
-    return [lax.ppermute(a, axis, [(i, (i + s) % size) for i in range(size)]) for s in range(1, size)]
+    return [lax.ppermute(a, axis, [(i, (i + s) % size) for i in range(size)]) for s in (1, 3, 2)[: size - 1]]
 
 
 def exchange(a, axes):
@@ -81,7 +81,7 @@
 
 
 def left_kernel(
-    core_ref, grads_hbm, errors_hbm, q_hbm, own_ref, other_ref, send_hbm, mine_ref, theirs_ref, grads, errors, q, send, in_sems, out_sems
+    core_ref, grads_hbm, errors_hbm, q_hbm, own_ref, other_ref, send_ref, mine_ref, theirs_ref, grads, errors, q, in_sems
 ):
     core = core_ref[0]
     inward = [
@@ -95,7 +95,6 @@
         )
         for j in range(CHUNKS)
     ]
-    outward = []
     totals = [jnp.zeros((R, ROWS), jnp.float32) for _ in range(MATS)]
     for j in range(CHUNKS):
         finish(inward[j])
@@ -109,22 +108,20 @@
                 own_ref[:, chunk(j)] = merged
             else:
                 other_ref[:, chunk(j)] = merged
-                send[:, chunk(j)] = merged.astype(jnp.float32)
-        outward += start([(send.at[:, chunk(j)], send_hbm.at[:, chunk(j)])], out_sems.at[j])
+                send_ref[:, chunk(j)] = merged.astype(jnp.float32)
     mine_ref[...] = totals[0]
     theirs_ref[...] = totals[1]
-    finish(outward)
 
 
 def left(core, grads, errors, q_t):
     return pl.pallas_call(
         left_kernel,
         in_specs=[IN_SMEM, IN_HBM, IN_HBM, IN_HBM],
-        out_specs=[IN_VMEM, IN_VMEM, IN_HBM, IN_VMEM, IN_VMEM],
+        out_specs=[IN_VMEM] * 5,
         out_shape=(
             vmem(ROWS, COLS, dtype=jnp.bfloat16),
             vmem(ROWS, COLS, dtype=jnp.bfloat16),
-            hbm(ROWS, COLS),
+            vmem(ROWS, COLS),
             vmem(R, ROWS),
             vmem(R, ROWS),
         ),
@@ -132,9 +129,7 @@
             pltpu.VMEM((MATS, ROWS, COLS), jnp.bfloat16),
             pltpu.VMEM((MATS, ROWS, COLS), jnp.bfloat16),
             pltpu.VMEM((MATS, R, COLS), jnp.bfloat16),
-            pltpu.VMEM((ROWS, COLS), jnp.float32),
             pltpu.SemaphoreType.DMA((CHUNKS, 3)),
-            pltpu.SemaphoreType.DMA((CHUNKS, 1)),
         ],
         compiler_params=PARAMS,
         cost_estimate=cost(1 << 27, 9 << 20),
@@ -172,16 +167,15 @@
 
 def four_kernel(first_ref, second_ref, third_ref, fourth_ref, out_ref):
     value = (first_ref[...] + second_ref[...]) + (third_ref[...] + fourth_ref[...])
-    for copy in range(out_ref.shape[0]):
-        out_ref[copy] = value
-
-
-def sum_four(parts, count):
+    out_ref[...] = value
+
+
+def sum_four(parts):
     return pl.pallas_call(
         four_kernel,
         in_specs=[IN_VMEM] * 4,
         out_specs=IN_VMEM,
-        out_shape=f32(count, *parts[0].shape),
+        out_shape=f32(*parts[0].shape),
         compiler_params=PARAMS,
         cost_estimate=cost(1 << 18, 2 << 20),
     )(*parts)
@@ -238,9 +232,17 @@
     lane = lax.broadcasted_iota(jnp.int32, (R, 2 * R), 1)
     unit = (lane - R == row).astype(jnp.float32)[:, R:]
     x = jnp.concatenate([gram, unit], axis=1)
-    for j in range(R):
-        ratio = x[:, j : j + 1] * (1.0 / x[j : j + 1, j : j + 1])
-        x = x - jnp.where(row > j, ratio, 0.0) * x[j : j + 1]
+    for j in range(0, R, 2):
+        row_a, row_b = x[j : j + 1], x[j + 1 : j + 2]
+        column_a, column_b = x[:, j : j + 1], x[:, j + 1 : j + 2]
+        pivot, between = row_a[:, j : j + 1], row_b[:, j : j + 1]
+        inverse_a = 1.0 / pivot
+        factor = between * inverse_a
+        inverse_b = 1.0 / (row_b[:, j + 1 : j + 2] - factor * between)
+        row_b = row_b - factor * row_a
+        column_b = column_b - column_a * factor
+        x = x - jnp.where(row > j, column_a * inverse_a, 0.0) * row_a
+        x = x - jnp.where(row > j + 1, column_b * inverse_b, 0.0) * row_b
     diagonal = jnp.sum(jnp.where(row == lane, x, 0.0), axis=1, keepdims=True)
     inverse = x[:, R:] / jnp.sqrt(diagonal)
     inverse_ref[...] = inverse
@@ -260,26 +262,37 @@
     )(*[keep(a, pltpu.VMEM) for a in grams], keep(summed, pltpu.VMEM))
 
 
-def tail_kernel(which_ref, ortho_ref, q_in, merged_ref, *refs):
-    error_hbm, q_hbm, ortho_hbm, errors, q_new, ortho_sem, out_sems = refs[-7:]
+def spread_kernel(blocks_ref, out_ref):
+    for i in range(GROUP):
+        out_ref[:, i * BLOCK : (i + 1) * BLOCK] = blocks_ref[i]
+
+
+def spread(blocks):
+    return pl.pallas_call(
+        spread_kernel,
+        in_specs=[IN_VMEM],
+        out_specs=IN_VMEM,
+        out_shape=vmem(R, COLS),
+        compiler_params=PARAMS,
+        cost_estimate=cost(0, 2 << 20),
+    )(blocks)
+
+
+def tail_kernel(which_ref, ortho_ref, q_ref, merged_ref, *refs):
+    error_hbm, q_hbm, ortho_hbm, errors, sems, out_sems = refs[-6:]
     which = which_ref[0]
-    outward = start([(ortho_ref, ortho_hbm.at[which])], ortho_sem)
+    outward = start([(q_ref, q_hbm.at[which]), (ortho_ref, ortho_hbm.at[which])], sems)
     rounded_p = ortho_ref[...].astype(jnp.bfloat16)
     for j in range(CHUNKS):
-        q = jnp.concatenate([q_in[j * PER + i] for i in range(PER)], axis=1)
-        q_new[:, chunk(j)] = q
         approx = lax.dot_general(
-            rounded_p, q.astype(jnp.bfloat16), (((0,), (0,)), ((), ())), preferred_element_type=jnp.float32
+            rounded_p,
+            q_ref[:, chunk(j)].astype(jnp.bfloat16),
+            (((0,), (0,)), ((), ())),
+            preferred_element_type=jnp.float32,
         )
         error = merged_ref[:, chunk(j)].astype(jnp.float32) - approx
         errors[:, chunk(j)] = error.astype(jnp.bfloat16)
-        outward += start(
-            [
-                (q_new.at[:, chunk(j)], q_hbm.at[which, :, chunk(j)]),
-                (errors.at[:, chunk(j)], error_hbm.at[0, which, :, chunk(j)]),
-            ],
-            out_sems.at[j],
-        )
+        outward += start([(errors.at[:, chunk(j)], error_hbm.at[0, which, :, chunk(j)])], out_sems.at[j])
     finish(outward)
 
 
@@ -292,9 +305,8 @@
         input_output_aliases={4: 0, 5: 1, 6: 2} if before else {},
         scratch_shapes=[
             pltpu.VMEM((ROWS, COLS), jnp.bfloat16),
-            pltpu.VMEM((R, COLS), jnp.float32),
-            pltpu.SemaphoreType.DMA((1,)),
-            pltpu.SemaphoreType.DMA((CHUNKS, 2)),
+            pltpu.SemaphoreType.DMA((2,)),
+            pltpu.SemaphoreType.DMA((CHUNKS, 1)),
         ],
         compiler_params=PARAMS,
         cost_estimate=cost(2 * ROWS * R * COLS, 4 << 20),
@@ -311,8 +323,9 @@
     terms, send = lax.optimization_barrier((terms, send))
     parts = [terms] + shifts(terms, "x", NX)
     received = swap(send)
-    terms = sum_four(parts, NV * NW)
-    summed = jnp.sum(exchange(terms, ("v", "w")), axis=0)
+    terms = sum_four(parts)
+    terms = terms + shifts(terms, "w", NW)[0]
+    summed = sum_four([terms] + shifts(terms, "v", NV))
 
     gram = jnp.einsum("kr,lr->kl", summed, summed, precision=HIGH)
     grams = [gram] + shifts(gram, "y", NY)
@@ -322,7 +335,7 @@
     inverse, ortho, ortho_theirs = factors(grams, summed)
     parts = [part] + shifts(part, "v", NV)
 
-    q_own = exchange(middle(parts, inverse), ("x", "w", "y"))
+    q_own = spread(exchange(middle(parts, inverse), ("x", "w", "y")))
     q_other = swap(q_own)
     first = tail(own, ortho, q_own, merged)
     ortho_other, first = lax.optimization_barrier((swap(ortho_theirs), first))

time: 91.7 us -> 89.4 us (0.975)
  starting transfers between devices: 25.2 us -> 38.8 us
  blocking collectives: 35.4 us -> 21.9 us
  Pallas kernels: 14.5 us -> 11.9 us
    all_to_all x2 -> x1, blocking collectives: 35.4 us -> 21.9 us  [exchange(): return lax.all_to_all(a, axes, 0, 0)]
    ppermute x9 -> x13, starting transfers between devices: 11.6 us -> 24.9 us  [shifts(): lax.ppermute(a, axis, [(i, (i + s) % size) for i in range(size)])]
    pallas_call x1, Pallas kernels: 2.91 us -> 1.32 us  [right(): pl.pallas_call(right_kernel, in_specs=[IN_VMEM, IN_VMEM, IN_VMEM], out_sp...]
    ppermute x9 -> x13, waiting for transfers between devices: 12.2 us -> 13.6 us  [shifts(): lax.ppermute(a, axis, [(i, (i + s) % size) for i in range(size)])]
    all_to_all x1, waiting for transfers between devices: 1.43 us -> 0.3 us  [exchange(): return lax.all_to_all(a, axes, 0, 0)]
    pallas_call x1, Pallas kernels: 3.91 us -> 2.89 us  [left(): pl.pallas_call(left_kernel, in_specs=[IN_SMEM, IN_HBM, IN_HBM, IN_HBM], o...]
  transfers between devices with their start and end apart: 14 -> 18, of which waited for: 9 -> 12; matrix products, arithmetic and copies ran while one was open for 0% -> 0% of each run, Pallas kernels for 5% -> 5%
where the time goes in v6:
time: 89.4 us; the launch traced here: 89.2 us
  starting transfers between devices  38.8 us (43%)
  blocking collectives  21.9 us (24%)
  waiting for transfers between devices  15.4 us (17%)
  Pallas kernels  11.9 us (13%)
    ppermute x13, starting transfers between devices, shifts(): lax.ppermute(a, axis, [(i, (i + s) % size) for i in range(size)])  24.9 us
    all_to_all x1, blocking collectives, exchange(): return lax.all_to_all(a, axes, 0, 0)  21.9 us
    ppermute x13, waiting for transfers between devices, shifts(): lax.ppermute(a, axis, [(i, (i + s) % size) for i in range(size)])  13.6 us
    ppermute x4, starting transfers between devices, swap(): return lax.ppermute(a, 'c', [(0, 1), (1, 0)])  8.48 us
    all_to_all x1, starting transfers between devices, exchange(): return lax.all_to_all(a, axes, 0, 0)  5.39 us
    pallas_call x2, Pallas kernels, tail(): pl.pallas_call(tail_kernel, in_specs=[IN_SMEM, IN_VMEM, IN_VMEM, IN_VMEM]...  4.45 us
    pallas_call x1, Pallas kernels, left(): pl.pallas_call(left_kernel, in_specs=[IN_SMEM, IN_HBM, IN_HBM, IN_HBM], o...  2.89 us
    pallas_call x1, Pallas kernels, factors(): pl.pallas_call(factor_kernel, in_specs=[IN_VMEM] * (NY + 1), out_specs=[I...  2.86 us
  transfers between devices with their start and end apart: 18, of which 12 were waited for; matrix products, arithmetic and copies ran while one was open for 0% of the time, Pallas kernels for 5%

profile of v6, /device:TPU:1, one launch (start us, length us, event | category | flops | bytes accessed | tf_op | source)
XLA Modules:
  0.0 89.2 jit_solution(2348059006021228678)
XLA Ops:
  0.6 2.9 %shard_map.58 = (bf16[64,8192]{1,0:T(8,128)(2,1)S(1)}, bf16[64,8192]{1,0:T(8,128)(2,1)S(1)}, f32[64,8192]{1,0:T(8,128)S(1)}, f32[32,64]{1,0:T(8,128)S(1)}, f32[32,64]{1,0:T(8,128)S(1)}) custom-call(s32[1]{0:T(128)} %bitcast.1.core_ref.which_ref, bf16[1,2,64,8192]{3,2,1,0:T(8,128)(2,1)} %grads_hbm.1, bf16[1,2,64,8192]{3,2,1,0:T(8,128)(2,1)} %errors_hbm.1, ...), custom_call_target="tpu_custom_call" | custom-call | flops 134217728 | bytes 9437184 | tf_op jit(solution)/shard_map/pallas_call | solution.py:117
  3.5 3.3 %collective-permute-start = (f32[32,64]{1,0:T(8,128)S(1)}, f32[32,64]{1,0:T(8,128)S(1)}, u32[]{:S(2)}, u32[]{:S(2)}) collective-permute-start(f32[32,64]{1,0:T(8,128)S(1)} %get-tuple-element.24), channel_id=1, source_target_pairs={{0,1},{1,0},{2,3},{3,2},{4,5},{5,4},{6,7},{7,6},{8,9},{9,8},{10,11... | collective-permute-start | bytes 24584 | tf_op jit(solution)/shard_map/ppermute | solution.py:48
  6.9 0.8 collective-permute-done
  7.7 0.1 pad_maximum_fusion.first_ref
  7.8 0.4 collective-permute-start.12
  8.1 1.0 %collective-permute-start.3 = (f32[32,128]{1,0:T(8,128)S(1)}, f32[32,128]{1,0:T(8,128)S(1)}, u32[]{:S(2)}, u32[]{:S(2)}) collective-permute-start(f32[32,128]{1,0:T(8,128)S(1)} %pad_maximum_fusion.first_ref), channel_id=1, source_target_pairs={{0,128},{64,192},{128,0},{192,64},{1,129},{65,193},{129,1},{193,65... | collective-permute-start | bytes 49160 | tf_op jit(solution)/shard_map/ppermute | solution.py:52
  9.2 0.9 collective-permute-start.2
  10.0 0.6 collective-permute-start.1
  10.6 1.6 %collective-permute-done.3.fourth_ref = f32[32,128]{1,0:T(8,128)S(1)} collective-permute-done((f32[32,128]{1,0:T(8,128)S(1)}, f32[32,128]{1,0:T(8,128)S(1)}, u32[]{:S(2)}, u32[]{:S(2)}) %collective-permute-start.3) | collective-permute-done | bytes 16416 | tf_op jit(solution)/shard_map/ppermute | solution.py:52
  12.2 0.0 collective-permute-done.2.third_ref
  12.2 1.6 %collective-permute-done.1.second_ref = f32[32,128]{1,0:T(8,128)S(1)} collective-permute-done((f32[32,128]{1,0:T(8,128)S(1)}, f32[32,128]{1,0:T(8,128)S(1)}, u32[]{:S(2)}, u32[]{:S(2)}) %collective-permute-start.1) | collective-permute-done | bytes 16416 | tf_op jit(solution)/shard_map/ppermute | solution.py:52
  13.8 1.7 %collective-permute-start.4 = (f32[32,128]{1,0:T(8,128)S(1)}, f32[32,128]{1,0:T(8,128)S(1)}, u32[]{:S(2)}, u32[]{:S(2)}) collective-permute-start(f32[32,128]{1,0:T(8,128)S(1)} %shard_map.59), channel_id=1, source_target_pairs={{0,8},{8,0},{1,9},{9,1},{2,10},{10,2},{3,11},{11,3},{4,12},{12,4},... | collective-permute-start | bytes 49160 | tf_op jit(solution)/shard_map/ppermute | solution.py:52
  15.5 1.1 %collective-permute-done.4 = f32[32,128]{1,0:T(8,128)S(1)} collective-permute-done((f32[32,128]{1,0:T(8,128)S(1)}, f32[32,128]{1,0:T(8,128)S(1)}, u32[]{:S(2)}, u32[]{:S(2)}) %collective-permute-start.4) | collective-permute-done | bytes 16416 | tf_op jit(solution)/shard_map/ppermute | solution.py:52
  16.7 6.7 %collective-permute-start.7 = (f32[32,128]{1,0:T(8,128)S(1)}, f32[32,128]{1,0:T(8,128)S(1)}, u32[]{:S(2)}, u32[]{:S(2)}) collective-permute-start(f32[32,128]{1,0:T(8,128)S(1)} %add.3.first_ref), channel_id=1, source_target_pairs={{0,32},{16,48},{32,0},{48,16},{1,33},{17,49},{33,1},{49,17},{2,34}... | collective-permute-start | bytes 49160 | tf_op jit(solution)/shard_map/ppermute | solution.py:52
  23.4 0.0 collective-permute-start.6
  23.4 2.4 %collective-permute-start.5 = (f32[32,128]{1,0:T(8,128)S(1)}, f32[32,128]{1,0:T(8,128)S(1)}, u32[]{:S(2)}, u32[]{:S(2)}) collective-permute-start(f32[32,128]{1,0:T(8,128)S(1)} %add.3.first_ref), channel_id=1, source_target_pairs={{0,16},{16,32},{32,48},{48,0},{1,17},{17,33},{33,49},{49,1},{2,18}... | collective-permute-start | bytes 49160 | tf_op jit(solution)/shard_map/ppermute | solution.py:52
  25.8 0.0 collective-permute-done.7.fourth_ref
  25.8 1.4 %collective-permute-done.6.third_ref = f32[32,128]{1,0:T(8,128)S(1)} collective-permute-done((f32[32,128]{1,0:T(8,128)S(1)}, f32[32,128]{1,0:T(8,128)S(1)}, u32[]{:S(2)}, u32[]{:S(2)}) %collective-permute-start.6) | collective-permute-done | bytes 16416 | tf_op jit(solution)/shard_map/ppermute | solution.py:52
  27.2 0.9 %collective-permute-done.5.second_ref = f32[32,128]{1,0:T(8,128)S(1)} collective-permute-done((f32[32,128]{1,0:T(8,128)S(1)}, f32[32,128]{1,0:T(8,128)S(1)}, u32[]{:S(2)}, u32[]{:S(2)}) %collective-permute-start.5) | collective-permute-done | bytes 16416 | tf_op jit(solution)/shard_map/ppermute | solution.py:52
  28.1 0.0 collective-permute-done.12.received_ref
  28.1 1.3 %shard_map.62 = f32[32,32,256]{2,1,0:T(8,128)} custom-call(f32[32,128]{1,0:T(8,128)S(1)} %shard_map.60.summed_ref, bf16[64,8192]{1,0:T(8,128)(2,1)S(1)} %get-tuple-element.29.merged_ref, f32[64,8192]{1,0:T(8,128)S(1)} %collective-permute-done.12.received_ref), custom_call_target="tpu_custom_call" | custom-call | flops 201326592 | bytes 4194304 | tf_op jit(solution)/shard_map/pallas_call | solution.py:218
  29.4 5.4 %all-to-all-start = ((f32[32,32,256]{2,1,0:T(8,128)}), f32[32,32,256]{2,1,0:T(8,128)S(1)}, u32[]{:S(2)}, u32[]{:S(2)}) async-start(f32[32,32,256]{2,1,0:T(8,128)} %shard_map.62), calls=%async_computation | async-start | bytes 2097152 | tf_op jit(solution)/shard_map/all_to_all | solution.py:56
  34.8 0.1 fusion.first_ref.refs_0_
  35.0 2.8 %collective-permute-start.10 = (f32[32,32]{1,0:T(8,128)S(1)}, f32[32,32]{1,0:T(8,128)S(1)}, u32[]{:S(2)}, u32[]{:S(2)}) collective-permute-start(f32[32,32]{1,0:T(8,128)S(1)} %fusion.first_ref.refs_0_), channel_id=1, source_target_pairs={{0,4},{2,6},{4,0},{6,2},{1,5},{3,7},{5,1},{7,3},{8,12},{10,14},{12... | collective-permute-start | bytes 12296 | tf_op jit(solution)/shard_map/ppermute | solution.py:52
  37.8 0.9 collective-permute-start.9
  38.7 0.6 collective-permute-start.8
  39.3 0.2 collective-permute-done.10.fourth_ref.refs_3_
  39.5 5.9 %collective-permute-done.9.third_ref.refs_2_ = f32[32,32]{1,0:T(8,128)S(1)} collective-permute-done((f32[32,32]{1,0:T(8,128)S(1)}, f32[32,32]{1,0:T(8,128)S(1)}, u32[]{:S(2)}, u32[]{:S(2)}) %collective-permute-start.9) | collective-permute-done | bytes 4128 | tf_op jit(solution)/shard_map/ppermute | solution.py:52
  45.4 0.8 collective-permute-done.8.second_ref.refs_1_
  46.2 0.3 all-to-all-done.parts_ref
  46.5 0.1 shard_map.63.first_ref
  46.6 5.0 %collective-permute-start.15 = (f32[32,256]{1,0:T(8,128)S(1)}, f32[32,256]{1,0:T(8,128)S(1)}, u32[]{:S(2)}, u32[]{:S(2)}) collective-permute-start(f32[32,256]{1,0:T(8,128)S(1)} %shard_map.63.first_ref), channel_id=1, source_target_pairs={{0,32},{16,48},{32,0},{48,16},{1,33},{17,49},{33,1},{49,17},{2,34}... | collective-permute-start | bytes 98312 | tf_op jit(solution)/shard_map/ppermute | solution.py:52
  51.5 0.0 collective-permute-start.14
  51.5 2.4 %collective-permute-start.13 = (f32[32,256]{1,0:T(8,128)S(1)}, f32[32,256]{1,0:T(8,128)S(1)}, u32[]{:S(2)}, u32[]{:S(2)}) collective-permute-start(f32[32,256]{1,0:T(8,128)S(1)} %shard_map.63.first_ref), channel_id=1, source_target_pairs={{0,16},{16,32},{32,48},{48,0},{1,17},{17,33},{33,49},{49,1},{2,18}... | collective-permute-start | bytes 98312 | tf_op jit(solution)/shard_map/ppermute | solution.py:52
  53.9 2.9 %shard_map.61 = (f32[32,32]{1,0:T(8,128)S(1)}, f32[32,64]{1,0:T(8,128)S(1)}, f32[32,64]{1,0:T(8,128)S(1)}) custom-call(f32[32,32]{1,0:T(8,128)S(1)} %fusion.first_ref.refs_0_, f32[32,32]{1,0:T(8,128)S(1)} %collective-permute-done.8.second_ref.refs_1_, f32[32,32]{1,0:T(8,128)S(1)} %collective-permute-done.9.third_ref.refs_2_, ...), custom_call_target="tpu_custom_call" | custom-call | flops 1048576 | bytes 12582912 | tf_op jit(solution)/shard_map/pallas_call | solution.py:255
  56.8 0.0 collective-permute-done.15.fourth_ref
  56.8 0.0 collective-permute-done.14.third_ref
  56.8 0.0 collective-permute-done.13.second_ref
  56.8 0.3 shard_map.64
  57.1 21.9 %all_to_all.10.blocks_ref = f32[32,32,256]{2,1,0:T(8,128)S(1)} all-to-all(f32[32,32,256]{2,1,0:T(8,128)S(1)} %shard_map.64), channel_id=1, replica_groups=mesh['x'=4,'v'=4,'w'=2,'y'=4,'c'=2] {'x','w','y'}, dimensions={0} | all-to-all | bytes 2097152 | tf_op jit(solution)/shard_map/all_to_all | solution.py:56
  79.0 0.1 shard_map.65.q_ref
  79.0 4.7 %collective-permute-start.16 = (f32[32,8192]{1,0:T(8,128)S(1)}, f32[32,8192]{1,0:T(8,128)}, u32[]{:S(2)}, u32[]{:S(2)}) collective-permute-start(f32[32,8192]{1,0:T(8,128)S(1)} %shard_map.65.q_ref), channel_id=1, source_target_pairs={{0,1},{1,0},{2,3},{3,2},{4,5},{5,4},{6,7},{7,6},{8,9},{9,8},{10,11... | collective-permute-start | bytes 3145736 | tf_op jit(solution)/shard_map/ppermute | solution.py:48
  83.7 0.1 collective-permute-start.11
  83.8 1.6 %shard_map.66 = (bf16[1,2,64,8192]{3,2,1,0:T(8,128)(2,1)}, f32[2,32,8192]{2,1,0:T(8,128)}, f32[2,32,64]{2,1,0:T(8,128)}) custom-call(s32[1]{0:T(128)} %bitcast.1.core_ref.which_ref, f32[32,64]{1,0:T(8,128)S(1)} %get-tuple-element.28.ortho_ref, f32[32,8192]{1,0:T(8,128)S(1)} %shard_map.65.q_ref, bf16[64,8192]{1,0:T(8,128)(2,1)S(1)} %get-tuple-element.29.merged_ref), custom_call_target="tpu_custom_call" | custom-call | flops 33554432 | bytes 4194304 | tf_op jit(solution)/shard_map/pallas_call | solution.py:300
  85.4 0.5 collective-permute-done.11.ortho_ref
  85.9 0.3 collective-permute-done.16.q_ref
  86.2 2.8 %shard_map.67 = (bf16[1,2,64,8192]{3,2,1,0:T(8,128)(2,1)}, f32[2,32,8192]{2,1,0:T(8,128)}, f32[2,32,64]{2,1,0:T(8,128)}) custom-call(s32[1]{0:T(128)} %bitcast.which_ref, f32[32,64]{1,0:T(8,128)S(1)} %collective-permute-done.11.ortho_ref, f32[32,8192]{1,0:T(8,128)} %collective-permute-done.16.q_ref, ...), custom_call_target="tpu_custom_call", output_to_operand_aliasing={{0}: (4, {}), {1}: (5, {}), {2}: (6, {})} | custom-call | flops 33554432 | bytes 4194304 | tf_op jit(solution)/shard_map/pallas_call | solution.py:300
  (3 shorter events, 0.0 us)
Async XLA Ops:
  3.5 4.2 %collective-permute-start = (f32[32,64]{1,0:T(8,128)S(1)}, f32[32,64]{1,0:T(8,128)S(1)}, u32[]{:S(2)}, u32[]{:S(2)}) collective-permute-start(f32[32,64]{1,0:T(8,128)S(1)} %get-tuple-element.24), channel_id=1, source_target_pairs={{0,1},{1,0},{2,3},{3,2},{4,5},{5,4},{6,7},{7,6},{8,9},{9,8},{10,11... | collective-permute-start | bytes 24584 | tf_op jit(solution)/shard_map/ppermute | solution.py:48
  7.8 20.3 %collective-permute-start.12 = (f32[64,8192]{1,0:T(8,128)S(1)}, f32[64,8192]{1,0:T(8,128)S(1)}, u32[]{:S(2)}, u32[]{:S(2)}) collective-permute-start(f32[64,8192]{1,0:T(8,128)S(1)} %get-tuple-element.30), channel_id=1, source_target_pairs={{0,1},{1,0},{2,3},{3,2},{4,5},{5,4},{6,7},{7,6},{8,9},{9,8},{10,11... | collective-permute-start | bytes 6291464 | tf_op jit(solution)/shard_map/ppermute | solution.py:48
  8.1 4.1 %collective-permute-start.3 = (f32[32,128]{1,0:T(8,128)S(1)}, f32[32,128]{1,0:T(8,128)S(1)}, u32[]{:S(2)}, u32[]{:S(2)}) collective-permute-start(f32[32,128]{1,0:T(8,128)S(1)} %pad_maximum_fusion.first_ref), channel_id=1, source_target_pairs={{0,128},{64,192},{128,0},{192,64},{1,129},{65,193},{129,1},{193,65... | collective-permute-start | bytes 49160 | tf_op jit(solution)/shard_map/ppermute | solution.py:52
  9.2 3.1 %collective-permute-start.2 = (f32[32,128]{1,0:T(8,128)S(1)}, f32[32,128]{1,0:T(8,128)S(1)}, u32[]{:S(2)}, u32[]{:S(2)}) collective-permute-start(f32[32,128]{1,0:T(8,128)S(1)} %pad_maximum_fusion.first_ref), channel_id=1, source_target_pairs={{0,192},{64,0},{128,64},{192,128},{1,193},{65,1},{129,65},{193,129... | collective-permute-start | bytes 49160 | tf_op jit(solution)/shard_map/ppermute | solution.py:52
  10.0 3.8 %collective-permute-start.1 = (f32[32,128]{1,0:T(8,128)S(1)}, f32[32,128]{1,0:T(8,128)S(1)}, u32[]{:S(2)}, u32[]{:S(2)}) collective-permute-start(f32[32,128]{1,0:T(8,128)S(1)} %pad_maximum_fusion.first_ref), channel_id=1, source_target_pairs={{0,64},{64,128},{128,192},{192,0},{1,65},{65,129},{129,193},{193,1... | collective-permute-start | bytes 49160 | tf_op jit(solution)/shard_map/ppermute | solution.py:52
  13.8 2.8 %collective-permute-start.4 = (f32[32,128]{1,0:T(8,128)S(1)}, f32[32,128]{1,0:T(8,128)S(1)}, u32[]{:S(2)}, u32[]{:S(2)}) collective-permute-start(f32[32,128]{1,0:T(8,128)S(1)} %shard_map.59), channel_id=1, source_target_pairs={{0,8},{8,0},{1,9},{9,1},{2,10},{10,2},{3,11},{11,3},{4,12},{12,4},... | collective-permute-start | bytes 49160 | tf_op jit(solution)/shard_map/ppermute | solution.py:52
  16.7 9.1 %collective-permute-start.7 = (f32[32,128]{1,0:T(8,128)S(1)}, f32[32,128]{1,0:T(8,128)S(1)}, u32[]{:S(2)}, u32[]{:S(2)}) collective-permute-start(f32[32,128]{1,0:T(8,128)S(1)} %add.3.first_ref), channel_id=1, source_target_pairs={{0,32},{16,48},{32,0},{48,16},{1,33},{17,49},{33,1},{49,17},{2,34}... | collective-permute-start | bytes 49160 | tf_op jit(solution)/shard_map/ppermute | solution.py:52
  23.4 3.8 %collective-permute-start.6 = (f32[32,128]{1,0:T(8,128)S(1)}, f32[32,128]{1,0:T(8,128)S(1)}, u32[]{:S(2)}, u32[]{:S(2)}) collective-permute-start(f32[32,128]{1,0:T(8,128)S(1)} %add.3.first_ref), channel_id=1, source_target_pairs={{0,48},{16,0},{32,16},{48,32},{1,49},{17,1},{33,17},{49,33},{2,50}... | collective-permute-start | bytes 49160 | tf_op jit(solution)/shard_map/ppermute | solution.py:52
  23.4 4.7 %collective-permute-start.5 = (f32[32,128]{1,0:T(8,128)S(1)}, f32[32,128]{1,0:T(8,128)S(1)}, u32[]{:S(2)}, u32[]{:S(2)}) collective-permute-start(f32[32,128]{1,0:T(8,128)S(1)} %add.3.first_ref), channel_id=1, source_target_pairs={{0,16},{16,32},{32,48},{48,0},{1,17},{17,33},{33,49},{49,1},{2,18}... | collective-permute-start | bytes 49160 | tf_op jit(solution)/shard_map/ppermute | solution.py:52
  29.4 17.0 %all-to-all-start = ((f32[32,32,256]{2,1,0:T(8,128)}), f32[32,32,256]{2,1,0:T(8,128)S(1)}, u32[]{:S(2)}, u32[]{:S(2)}) async-start(f32[32,32,256]{2,1,0:T(8,128)} %shard_map.62), calls=%async_computation | async-start | bytes 2097152 | tf_op jit(solution)/shard_map/all_to_all | solution.py:56
  35.0 4.5 %collective-permute-start.10 = (f32[32,32]{1,0:T(8,128)S(1)}, f32[32,32]{1,0:T(8,128)S(1)}, u32[]{:S(2)}, u32[]{:S(2)}) collective-permute-start(f32[32,32]{1,0:T(8,128)S(1)} %fusion.first_ref.refs_0_), channel_id=1, source_target_pairs={{0,4},{2,6},{4,0},{6,2},{1,5},{3,7},{5,1},{7,3},{8,12},{10,14},{12... | collective-permute-start | bytes 12296 | tf_op jit(solution)/shard_map/ppermute | solution.py:52
  37.8 7.6 %collective-permute-start.9 = (f32[32,32]{1,0:T(8,128)S(1)}, f32[32,32]{1,0:T(8,128)S(1)}, u32[]{:S(2)}, u32[]{:S(2)}) collective-permute-start(f32[32,32]{1,0:T(8,128)S(1)} %fusion.first_ref.refs_0_), channel_id=1, source_target_pairs={{0,6},{2,0},{4,2},{6,4},{1,7},{3,1},{5,3},{7,5},{8,14},{10,8},{12,... | collective-permute-start | bytes 12296 | tf_op jit(solution)/shard_map/ppermute | solution.py:52
  38.7 7.5 %collective-permute-start.8 = (f32[32,32]{1,0:T(8,128)S(1)}, f32[32,32]{1,0:T(8,128)S(1)}, u32[]{:S(2)}, u32[]{:S(2)}) collective-permute-start(f32[32,32]{1,0:T(8,128)S(1)} %fusion.first_ref.refs_0_), channel_id=1, source_target_pairs={{0,2},{2,4},{4,6},{6,0},{1,3},{3,5},{5,7},{7,1},{8,10},{10,12},{12... | collective-permute-start | bytes 12296 | tf_op jit(solution)/shard_map/ppermute | solution.py:52
  46.6 10.2 %collective-permute-start.15 = (f32[32,256]{1,0:T(8,128)S(1)}, f32[32,256]{1,0:T(8,128)S(1)}, u32[]{:S(2)}, u32[]{:S(2)}) collective-permute-start(f32[32,256]{1,0:T(8,128)S(1)} %shard_map.63.first_ref), channel_id=1, source_target_pairs={{0,32},{16,48},{32,0},{48,16},{1,33},{17,49},{33,1},{49,17},{2,34}... | collective-permute-start | bytes 98312 | tf_op jit(solution)/shard_map/ppermute | solution.py:52
  51.5 5.2 %collective-permute-start.14 = (f32[32,256]{1,0:T(8,128)S(1)}, f32[32,256]{1,0:T(8,128)S(1)}, u32[]{:S(2)}, u32[]{:S(2)}) collective-permute-start(f32[32,256]{1,0:T(8,128)S(1)} %shard_map.63.first_ref), channel_id=1, source_target_pairs={{0,48},{16,0},{32,16},{48,32},{1,49},{17,1},{33,17},{49,33},{2,50}... | collective-permute-start | bytes 98312 | tf_op jit(solution)/shard_map/ppermute | solution.py:52
  51.5 5.2 %collective-permute-start.13 = (f32[32,256]{1,0:T(8,128)S(1)}, f32[32,256]{1,0:T(8,128)S(1)}, u32[]{:S(2)}, u32[]{:S(2)}) collective-permute-start(f32[32,256]{1,0:T(8,128)S(1)} %shard_map.63.first_ref), channel_id=1, source_target_pairs={{0,16},{16,32},{32,48},{48,0},{1,17},{17,33},{33,49},{49,1},{2,18}... | collective-permute-start | bytes 98312 | tf_op jit(solution)/shard_map/ppermute | solution.py:52
  79.0 7.1 %collective-permute-start.16 = (f32[32,8192]{1,0:T(8,128)S(1)}, f32[32,8192]{1,0:T(8,128)}, u32[]{:S(2)}, u32[]{:S(2)}) collective-permute-start(f32[32,8192]{1,0:T(8,128)S(1)} %shard_map.65.q_ref), channel_id=1, source_target_pairs={{0,1},{1,0},{2,3},{3,2},{4,5},{5,4},{6,7},{7,6},{8,9},{9,8},{10,11... | collective-permute-start | bytes 3145736 | tf_op jit(solution)/shard_map/ppermute | solution.py:48
  83.7 2.2 %collective-permute-start.11 = (f32[32,64]{1,0:T(8,128)S(1)}, f32[32,64]{1,0:T(8,128)S(1)}, u32[]{:S(2)}, u32[]{:S(2)}) collective-permute-start(f32[32,64]{1,0:T(8,128)S(1)} %get-tuple-element.27), channel_id=1, source_target_pairs={{0,1},{1,0},{2,3},{3,2},{4,5},{5,4},{6,7},{7,6},{8,9},{9,8},{10,11... | collective-permute-start | bytes 24584 | tf_op jit(solution)/shard_map/ppermute | solution.py:48

commit v7 on v6

--- a/solution.py
+++ b/solution.py
@@ -1,3 +1,5 @@
+import functools
+
 import jax
 import jax.numpy as jnp
 from jax import lax
@@ -278,9 +280,9 @@
     )(blocks)
 
 
-def tail_kernel(which_ref, ortho_ref, q_ref, merged_ref, *refs):
+def tail_kernel(other, core_ref, ortho_ref, q_ref, merged_ref, *refs):
     error_hbm, q_hbm, ortho_hbm, errors, sems, out_sems = refs[-6:]
-    which = which_ref[0]
+    which = 1 - core_ref[0] if other else core_ref[0]
     outward = start([(q_ref, q_hbm.at[which]), (ortho_ref, ortho_hbm.at[which])], sems)
     rounded_p = ortho_ref[...].astype(jnp.bfloat16)
     for j in range(CHUNKS):
@@ -296,9 +298,9 @@
     finish(outward)
 
 
-def tail(which, ortho, q, merged, before=()):
-    return pl.pallas_call(
-        tail_kernel,
+def tail(core, ortho, q, merged, before=()):
+    return pl.pallas_call(
+        functools.partial(tail_kernel, bool(before)),
         in_specs=[IN_SMEM, IN_VMEM, IN_VMEM, IN_VMEM] + [IN_HBM] * len(before),
         out_specs=[IN_HBM, IN_HBM, IN_HBM],
         out_shape=(hbm(1, MATS, ROWS, COLS, dtype=jnp.bfloat16), hbm(MATS, R, COLS), hbm(MATS, R, ROWS)),
@@ -310,13 +312,12 @@
         ],
         compiler_params=PARAMS,
         cost_estimate=cost(2 * ROWS * R * COLS, 4 << 20),
-    )(which, keep(ortho, pltpu.VMEM), keep(q, pltpu.VMEM), keep(merged, pltpu.VMEM), *before)
+    )(core, keep(ortho, pltpu.VMEM), keep(q, pltpu.VMEM), keep(merged, pltpu.VMEM), *before)
 
 
 def local(grads, errors, q_init):
     core = lax.axis_index("c").astype(jnp.int32)
     own = core.reshape(1)
-    other = (1 - core).reshape(1)
 
     merged, merged_other, send, mine, theirs = left(own, grads, errors, q_init.transpose(0, 2, 1))
     terms = jnp.concatenate([mine, swap(theirs)], axis=1)
@@ -339,7 +340,7 @@
     q_other = swap(q_own)
     first = tail(own, ortho, q_own, merged)
     ortho_other, first = lax.optimization_barrier((swap(ortho_theirs), first))
-    error_new, q_t, orthonormal = tail(other, ortho_other, q_other, merged_other, first)
+    error_new, q_t, orthonormal = tail(own, ortho_other, q_other, merged_other, first)
     return (error_new, q_t.transpose(0, 2, 1), orthonormal.transpose(0, 2, 1))
 
 

time: 89.4 us -> 88 us (0.984)
  Pallas kernels: 11.9 us -> 10.7 us
    pallas_call x2, Pallas kernels: 4.45 us -> 3.23 us  [tail(): pl.pallas_call(functools.partial(tail_kernel, bool(before)), in_specs=[IN...]
  transfers between devices with their start and end apart: 18 -> 18, of which waited for: 12 -> 11; matrix products, arithmetic and copies ran while one was open for 0% -> 0% of each run, Pallas kernels for 5% -> 5%
where the time goes in v7:
time: 88 us; the launch traced here: 87.8 us
  starting transfers between devices  38.8 us (44%)
  blocking collectives  21.9 us (25%)
  waiting for transfers between devices  15.3 us (17%)
  Pallas kernels  10.7 us (12%)
  between operations  0.89 us (1%)
    ppermute x13, starting transfers between devices, shifts(): lax.ppermute(a, axis, [(i, (i + s) % size) for i in range(size)])  24.9 us
    all_to_all x1, blocking collectives, exchange(): return lax.all_to_all(a, axes, 0, 0)  21.9 us
    ppermute x13, waiting for transfers between devices, shifts(): lax.ppermute(a, axis, [(i, (i + s) % size) for i in range(size)])  13.6 us
    ppermute x4, starting transfers between devices, swap(): return lax.ppermute(a, 'c', [(0, 1), (1, 0)])  8.48 us
    all_to_all x1, starting transfers between devices, exchange(): return lax.all_to_all(a, axes, 0, 0)  5.39 us
    pallas_call x2, Pallas kernels, tail(): pl.pallas_call(functools.partial(tail_kernel, bool(before)), in_specs=[IN...  3.23 us
    pallas_call x1, Pallas kernels, left(): pl.pallas_call(left_kernel, in_specs=[IN_SMEM, IN_HBM, IN_HBM, IN_HBM], o...  2.89 us
    pallas_call x1, Pallas kernels, factors(): pl.pallas_call(factor_kernel, in_specs=[IN_VMEM] * (NY + 1), out_specs=[I...  2.86 us
  transfers between devices with their start and end apart: 18, of which 11 were waited for; matrix products, arithmetic and copies ran while one was open for 0% of the time, Pallas kernels for 5%

profile of v7, /device:TPU:1, one launch (start us, length us, event | category | flops | bytes accessed | tf_op | source)
XLA Modules:
  0.0 87.8 jit_solution(9025346155264231863)
XLA Ops:
  0.6 2.9 %shard_map.58 = (bf16[64,8192]{1,0:T(8,128)(2,1)S(1)}, bf16[64,8192]{1,0:T(8,128)(2,1)S(1)}, f32[64,8192]{1,0:T(8,128)S(1)}, f32[32,64]{1,0:T(8,128)S(1)}, f32[32,64]{1,0:T(8,128)S(1)}) custom-call(s32[1]{0:T(128)} %bitcast.core_ref, bf16[1,2,64,8192]{3,2,1,0:T(8,128)(2,1)} %grads_hbm.1, bf16[1,2,64,8192]{3,2,1,0:T(8,128)(2,1)} %errors_hbm.1, ...), custom_call_target="tpu_custom_call" | custom-call | flops 134217728 | bytes 9437184 | tf_op jit(solution)/shard_map/pallas_call | solution.py:119
  3.5 3.3 %collective-permute-start = (f32[32,64]{1,0:T(8,128)S(1)}, f32[32,64]{1,0:T(8,128)S(1)}, u32[]{:S(2)}, u32[]{:S(2)}) collective-permute-start(f32[32,64]{1,0:T(8,128)S(1)} %get-tuple-element.24), channel_id=1, source_target_pairs={{0,1},{1,0},{2,3},{3,2},{4,5},{5,4},{6,7},{7,6},{8,9},{9,8},{10,11... | collective-permute-start | bytes 24584 | tf_op jit(solution)/shard_map/ppermute | solution.py:50
  6.9 0.8 collective-permute-done
  7.7 0.1 pad_maximum_fusion.first_ref
  7.8 0.4 collective-permute-start.12
  8.1 1.0 %collective-permute-start.3 = (f32[32,128]{1,0:T(8,128)S(1)}, f32[32,128]{1,0:T(8,128)S(1)}, u32[]{:S(2)}, u32[]{:S(2)}) collective-permute-start(f32[32,128]{1,0:T(8,128)S(1)} %pad_maximum_fusion.first_ref), channel_id=1, source_target_pairs={{0,128},{64,192},{128,0},{192,64},{1,129},{65,193},{129,1},{193,65... | collective-permute-start | bytes 49160 | tf_op jit(solution)/shard_map/ppermute | solution.py:54
  9.2 0.9 collective-permute-start.2
  10.0 0.6 collective-permute-start.1
  10.6 1.6 %collective-permute-done.3.fourth_ref = f32[32,128]{1,0:T(8,128)S(1)} collective-permute-done((f32[32,128]{1,0:T(8,128)S(1)}, f32[32,128]{1,0:T(8,128)S(1)}, u32[]{:S(2)}, u32[]{:S(2)}) %collective-permute-start.3) | collective-permute-done | bytes 16416 | tf_op jit(solution)/shard_map/ppermute | solution.py:54
  12.2 0.0 collective-permute-done.2.third_ref
  12.2 1.6 %collective-permute-done.1.second_ref = f32[32,128]{1,0:T(8,128)S(1)} collective-permute-done((f32[32,128]{1,0:T(8,128)S(1)}, f32[32,128]{1,0:T(8,128)S(1)}, u32[]{:S(2)}, u32[]{:S(2)}) %collective-permute-start.1) | collective-permute-done | bytes 16416 | tf_op jit(solution)/shard_map/ppermute | solution.py:54
  13.8 1.7 %collective-permute-start.4 = (f32[32,128]{1,0:T(8,128)S(1)}, f32[32,128]{1,0:T(8,128)S(1)}, u32[]{:S(2)}, u32[]{:S(2)}) collective-permute-start(f32[32,128]{1,0:T(8,128)S(1)} %shard_map.59), channel_id=1, source_target_pairs={{0,8},{8,0},{1,9},{9,1},{2,10},{10,2},{3,11},{11,3},{4,12},{12,4},... | collective-permute-start | bytes 49160 | tf_op jit(solution)/shard_map/ppermute | solution.py:54
  15.5 1.1 %collective-permute-done.4 = f32[32,128]{1,0:T(8,128)S(1)} collective-permute-done((f32[32,128]{1,0:T(8,128)S(1)}, f32[32,128]{1,0:T(8,128)S(1)}, u32[]{:S(2)}, u32[]{:S(2)}) %collective-permute-start.4) | collective-permute-done | bytes 16416 | tf_op jit(solution)/shard_map/ppermute | solution.py:54
  16.7 6.7 %collective-permute-start.7 = (f32[32,128]{1,0:T(8,128)S(1)}, f32[32,128]{1,0:T(8,128)S(1)}, u32[]{:S(2)}, u32[]{:S(2)}) collective-permute-start(f32[32,128]{1,0:T(8,128)S(1)} %add.3.first_ref), channel_id=1, source_target_pairs={{0,32},{16,48},{32,0},{48,16},{1,33},{17,49},{33,1},{49,17},{2,34}... | collective-permute-start | bytes 49160 | tf_op jit(solution)/shard_map/ppermute | solution.py:54
  23.4 0.0 collective-permute-start.6
  23.4 2.4 %collective-permute-start.5 = (f32[32,128]{1,0:T(8,128)S(1)}, f32[32,128]{1,0:T(8,128)S(1)}, u32[]{:S(2)}, u32[]{:S(2)}) collective-permute-start(f32[32,128]{1,0:T(8,128)S(1)} %add.3.first_ref), channel_id=1, source_target_pairs={{0,16},{16,32},{32,48},{48,0},{1,17},{17,33},{33,49},{49,1},{2,18}... | collective-permute-start | bytes 49160 | tf_op jit(solution)/shard_map/ppermute | solution.py:54
  25.8 0.0 collective-permute-done.7.fourth_ref
  25.8 1.4 %collective-permute-done.6.third_ref = f32[32,128]{1,0:T(8,128)S(1)} collective-permute-done((f32[32,128]{1,0:T(8,128)S(1)}, f32[32,128]{1,0:T(8,128)S(1)}, u32[]{:S(2)}, u32[]{:S(2)}) %collective-permute-start.6) | collective-permute-done | bytes 16416 | tf_op jit(solution)/shard_map/ppermute | solution.py:54
  27.2 0.9 %collective-permute-done.5.second_ref = f32[32,128]{1,0:T(8,128)S(1)} collective-permute-done((f32[32,128]{1,0:T(8,128)S(1)}, f32[32,128]{1,0:T(8,128)S(1)}, u32[]{:S(2)}, u32[]{:S(2)}) %collective-permute-start.5) | collective-permute-done | bytes 16416 | tf_op jit(solution)/shard_map/ppermute | solution.py:54
  28.1 0.0 collective-permute-done.12.received_ref
  28.1 1.3 %shard_map.62 = f32[32,32,256]{2,1,0:T(8,128)} custom-call(f32[32,128]{1,0:T(8,128)S(1)} %shard_map.60.summed_ref, bf16[64,8192]{1,0:T(8,128)(2,1)S(1)} %get-tuple-element.29.merged_ref, f32[64,8192]{1,0:T(8,128)S(1)} %collective-permute-done.12.received_ref), custom_call_target="tpu_custom_call" | custom-call | flops 201326592 | bytes 4194304 | tf_op jit(solution)/shard_map/pallas_call | solution.py:220
  29.4 5.4 %all-to-all-start = ((f32[32,32,256]{2,1,0:T(8,128)}), f32[32,32,256]{2,1,0:T(8,128)S(1)}, u32[]{:S(2)}, u32[]{:S(2)}) async-start(f32[32,32,256]{2,1,0:T(8,128)} %shard_map.62), calls=%async_computation | async-start | bytes 2097152 | tf_op jit(solution)/shard_map/all_to_all | solution.py:58
  34.8 0.1 fusion.first_ref.refs_0_
  35.0 2.8 %collective-permute-start.10 = (f32[32,32]{1,0:T(8,128)S(1)}, f32[32,32]{1,0:T(8,128)S(1)}, u32[]{:S(2)}, u32[]{:S(2)}) collective-permute-start(f32[32,32]{1,0:T(8,128)S(1)} %fusion.first_ref.refs_0_), channel_id=1, source_target_pairs={{0,4},{2,6},{4,0},{6,2},{1,5},{3,7},{5,1},{7,3},{8,12},{10,14},{12... | collective-permute-start | bytes 12296 | tf_op jit(solution)/shard_map/ppermute | solution.py:54
  37.8 0.9 %collective-permute-start.9 = (f32[32,32]{1,0:T(8,128)S(1)}, f32[32,32]{1,0:T(8,128)S(1)}, u32[]{:S(2)}, u32[]{:S(2)}) collective-permute-start(f32[32,32]{1,0:T(8,128)S(1)} %fusion.first_ref.refs_0_), channel_id=1, source_target_pairs={{0,6},{2,0},{4,2},{6,4},{1,7},{3,1},{5,3},{7,5},{8,14},{10,8},{12,... | collective-permute-start | bytes 12296 | tf_op jit(solution)/shard_map/ppermute | solution.py:54
  38.7 0.6 collective-permute-start.8
  39.3 0.2 collective-permute-done.10.fourth_ref.refs_3_
  39.5 5.9 %collective-permute-done.9.third_ref.refs_2_ = f32[32,32]{1,0:T(8,128)S(1)} collective-permute-done((f32[32,32]{1,0:T(8,128)S(1)}, f32[32,32]{1,0:T(8,128)S(1)}, u32[]{:S(2)}, u32[]{:S(2)}) %collective-permute-start.9) | collective-permute-done | bytes 4128 | tf_op jit(solution)/shard_map/ppermute | solution.py:54
  45.4 0.8 collective-permute-done.8.second_ref.refs_1_
  46.2 0.3 all-to-all-done.parts_ref
  46.5 0.1 shard_map.63.first_ref
  46.6 5.0 %collective-permute-start.15 = (f32[32,256]{1,0:T(8,128)S(1)}, f32[32,256]{1,0:T(8,128)S(1)}, u32[]{:S(2)}, u32[]{:S(2)}) collective-permute-start(f32[32,256]{1,0:T(8,128)S(1)} %shard_map.63.first_ref), channel_id=1, source_target_pairs={{0,32},{16,48},{32,0},{48,16},{1,33},{17,49},{33,1},{49,17},{2,34}... | collective-permute-start | bytes 98312 | tf_op jit(solution)/shard_map/ppermute | solution.py:54
  51.5 0.0 collective-permute-start.14
  51.5 2.4 %collective-permute-start.13 = (f32[32,256]{1,0:T(8,128)S(1)}, f32[32,256]{1,0:T(8,128)S(1)}, u32[]{:S(2)}, u32[]{:S(2)}) collective-permute-start(f32[32,256]{1,0:T(8,128)S(1)} %shard_map.63.first_ref), channel_id=1, source_target_pairs={{0,16},{16,32},{32,48},{48,0},{1,17},{17,33},{33,49},{49,1},{2,18}... | collective-permute-start | bytes 98312 | tf_op jit(solution)/shard_map/ppermute | solution.py:54
  53.9 2.9 %shard_map.61 = (f32[32,32]{1,0:T(8,128)S(1)}, f32[32,64]{1,0:T(8,128)S(1)}, f32[32,64]{1,0:T(8,128)S(1)}) custom-call(f32[32,32]{1,0:T(8,128)S(1)} %fusion.first_ref.refs_0_, f32[32,32]{1,0:T(8,128)S(1)} %collective-permute-done.8.second_ref.refs_1_, f32[32,32]{1,0:T(8,128)S(1)} %collective-permute-done.9.third_ref.refs_2_, ...), custom_call_target="tpu_custom_call" | custom-call | flops 1048576 | bytes 12582912 | tf_op jit(solution)/shard_map/pallas_call | solution.py:257
  56.8 0.0 collective-permute-done.15.fourth_ref
  56.8 0.0 collective-permute-done.14.third_ref
  56.8 0.0 collective-permute-done.13.second_ref
  56.8 0.3 shard_map.64
  57.1 21.9 %all_to_all.10.blocks_ref = f32[32,32,256]{2,1,0:T(8,128)S(1)} all-to-all(f32[32,32,256]{2,1,0:T(8,128)S(1)} %shard_map.64), channel_id=1, replica_groups=mesh['x'=4,'v'=4,'w'=2,'y'=4,'c'=2] {'x','w','y'}, dimensions={0} | all-to-all | bytes 2097152 | tf_op jit(solution)/shard_map/all_to_all | solution.py:58
  79.0 0.1 shard_map.65.q_ref
  79.0 4.7 %collective-permute-start.16 = (f32[32,8192]{1,0:T(8,128)S(1)}, f32[32,8192]{1,0:T(8,128)S(1)}, u32[]{:S(2)}, u32[]{:S(2)}) collective-permute-start(f32[32,8192]{1,0:T(8,128)S(1)} %shard_map.65.q_ref), channel_id=1, source_target_pairs={{0,1},{1,0},{2,3},{3,2},{4,5},{5,4},{6,7},{7,6},{8,9},{9,8},{10,11... | collective-permute-start | bytes 3145736 | tf_op jit(solution)/shard_map/ppermute | solution.py:50
  83.7 0.1 collective-permute-start.11
  83.8 1.6 %shard_map.66 = (bf16[1,2,64,8192]{3,2,1,0:T(8,128)(2,1)}, f32[2,32,8192]{2,1,0:T(8,128)}, f32[2,32,64]{2,1,0:T(8,128)}) custom-call(s32[1]{0:T(128)} %bitcast.core_ref, f32[32,64]{1,0:T(8,128)S(1)} %get-tuple-element.28.ortho_ref, f32[32,8192]{1,0:T(8,128)S(1)} %shard_map.65.q_ref, bf16[64,8192]{1,0:T(8,128)(2,1)S(1)} %get-tuple-element.29.merged_ref), custom_call_target="tpu_custom_call" | custom-call | flops 33554432 | bytes 4194304 | tf_op jit(solution)/shard_map/pallas_call | solution.py:302
  85.4 0.6 collective-permute-done.11.ortho_ref
  86.0 0.0 collective-permute-done.16.q_ref
  86.0 1.6 %shard_map.67 = (bf16[1,2,64,8192]{3,2,1,0:T(8,128)(2,1)}, f32[2,32,8192]{2,1,0:T(8,128)}, f32[2,32,64]{2,1,0:T(8,128)}) custom-call(s32[1]{0:T(128)} %bitcast.core_ref, f32[32,64]{1,0:T(8,128)S(1)} %collective-permute-done.11.ortho_ref, f32[32,8192]{1,0:T(8,128)S(1)} %collective-permute-done.16.q_ref, ...), custom_call_target="tpu_custom_call", output_to_operand_aliasing={{0}: (4, {}), {1}: (5, {}), {2}: (6, {})} | custom-call | flops 33554432 | bytes 4194304 | tf_op jit(solution)/shard_map/pallas_call | solution.py:302
  (3 shorter events, 0.0 us)
Async XLA Ops:
  3.5 4.2 %collective-permute-start = (f32[32,64]{1,0:T(8,128)S(1)}, f32[32,64]{1,0:T(8,128)S(1)}, u32[]{:S(2)}, u32[]{:S(2)}) collective-permute-start(f32[32,64]{1,0:T(8,128)S(1)} %get-tuple-element.24), channel_id=1, source_target_pairs={{0,1},{1,0},{2,3},{3,2},{4,5},{5,4},{6,7},{7,6},{8,9},{9,8},{10,11... | collective-permute-start | bytes 24584 | tf_op jit(solution)/shard_map/ppermute | solution.py:50
  7.8 20.3 %collective-permute-start.12 = (f32[64,8192]{1,0:T(8,128)S(1)}, f32[64,8192]{1,0:T(8,128)S(1)}, u32[]{:S(2)}, u32[]{:S(2)}) collective-permute-start(f32[64,8192]{1,0:T(8,128)S(1)} %get-tuple-element.30), channel_id=1, source_target_pairs={{0,1},{1,0},{2,3},{3,2},{4,5},{5,4},{6,7},{7,6},{8,9},{9,8},{10,11... | collective-permute-start | bytes 6291464 | tf_op jit(solution)/shard_map/ppermute | solution.py:50
  8.1 4.1 %collective-permute-start.3 = (f32[32,128]{1,0:T(8,128)S(1)}, f32[32,128]{1,0:T(8,128)S(1)}, u32[]{:S(2)}, u32[]{:S(2)}) collective-permute-start(f32[32,128]{1,0:T(8,128)S(1)} %pad_maximum_fusion.first_ref), channel_id=1, source_target_pairs={{0,128},{64,192},{128,0},{192,64},{1,129},{65,193},{129,1},{193,65... | collective-permute-start | bytes 49160 | tf_op jit(solution)/shard_map/ppermute | solution.py:54
  9.2 3.1 %collective-permute-start.2 = (f32[32,128]{1,0:T(8,128)S(1)}, f32[32,128]{1,0:T(8,128)S(1)}, u32[]{:S(2)}, u32[]{:S(2)}) collective-permute-start(f32[32,128]{1,0:T(8,128)S(1)} %pad_maximum_fusion.first_ref), channel_id=1, source_target_pairs={{0,192},{64,0},{128,64},{192,128},{1,193},{65,1},{129,65},{193,129... | collective-permute-start | bytes 49160 | tf_op jit(solution)/shard_map/ppermute | solution.py:54
  10.0 3.8 %collective-permute-start.1 = (f32[32,128]{1,0:T(8,128)S(1)}, f32[32,128]{1,0:T(8,128)S(1)}, u32[]{:S(2)}, u32[]{:S(2)}) collective-permute-start(f32[32,128]{1,0:T(8,128)S(1)} %pad_maximum_fusion.first_ref), channel_id=1, source_target_pairs={{0,64},{64,128},{128,192},{192,0},{1,65},{65,129},{129,193},{193,1... | collective-permute-start | bytes 49160 | tf_op jit(solution)/shard_map/ppermute | solution.py:54
  13.8 2.8 %collective-permute-start.4 = (f32[32,128]{1,0:T(8,128)S(1)}, f32[32,128]{1,0:T(8,128)S(1)}, u32[]{:S(2)}, u32[]{:S(2)}) collective-permute-start(f32[32,128]{1,0:T(8,128)S(1)} %shard_map.59), channel_id=1, source_target_pairs={{0,8},{8,0},{1,9},{9,1},{2,10},{10,2},{3,11},{11,3},{4,12},{12,4},... | collective-permute-start | bytes 49160 | tf_op jit(solution)/shard_map/ppermute | solution.py:54
  16.7 9.1 %collective-permute-start.7 = (f32[32,128]{1,0:T(8,128)S(1)}, f32[32,128]{1,0:T(8,128)S(1)}, u32[]{:S(2)}, u32[]{:S(2)}) collective-permute-start(f32[32,128]{1,0:T(8,128)S(1)} %add.3.first_ref), channel_id=1, source_target_pairs={{0,32},{16,48},{32,0},{48,16},{1,33},{17,49},{33,1},{49,17},{2,34}... | collective-permute-start | bytes 49160 | tf_op jit(solution)/shard_map/ppermute | solution.py:54
  23.4 3.8 %collective-permute-start.6 = (f32[32,128]{1,0:T(8,128)S(1)}, f32[32,128]{1,0:T(8,128)S(1)}, u32[]{:S(2)}, u32[]{:S(2)}) collective-permute-start(f32[32,128]{1,0:T(8,128)S(1)} %add.3.first_ref), channel_id=1, source_target_pairs={{0,48},{16,0},{32,16},{48,32},{1,49},{17,1},{33,17},{49,33},{2,50}... | collective-permute-start | bytes 49160 | tf_op jit(solution)/shard_map/ppermute | solution.py:54
  23.4 4.7 %collective-permute-start.5 = (f32[32,128]{1,0:T(8,128)S(1)}, f32[32,128]{1,0:T(8,128)S(1)}, u32[]{:S(2)}, u32[]{:S(2)}) collective-permute-start(f32[32,128]{1,0:T(8,128)S(1)} %add.3.first_ref), channel_id=1, source_target_pairs={{0,16},{16,32},{32,48},{48,0},{1,17},{17,33},{33,49},{49,1},{2,18}... | collective-permute-start | bytes 49160 | tf_op jit(solution)/shard_map/ppermute | solution.py:54
  29.4 17.0 %all-to-all-start = ((f32[32,32,256]{2,1,0:T(8,128)}), f32[32,32,256]{2,1,0:T(8,128)S(1)}, u32[]{:S(2)}, u32[]{:S(2)}) async-start(f32[32,32,256]{2,1,0:T(8,128)} %shard_map.62), calls=%async_computation | async-start | bytes 2097152 | tf_op jit(solution)/shard_map/all_to_all | solution.py:58
  35.0 4.5 %collective-permute-start.10 = (f32[32,32]{1,0:T(8,128)S(1)}, f32[32,32]{1,0:T(8,128)S(1)}, u32[]{:S(2)}, u32[]{:S(2)}) collective-permute-start(f32[32,32]{1,0:T(8,128)S(1)} %fusion.first_ref.refs_0_), channel_id=1, source_target_pairs={{0,4},{2,6},{4,0},{6,2},{1,5},{3,7},{5,1},{7,3},{8,12},{10,14},{12... | collective-permute-start | bytes 12296 | tf_op jit(solution)/shard_map/ppermute | solution.py:54
  37.8 7.6 %collective-permute-start.9 = (f32[32,32]{1,0:T(8,128)S(1)}, f32[32,32]{1,0:T(8,128)S(1)}, u32[]{:S(2)}, u32[]{:S(2)}) collective-permute-start(f32[32,32]{1,0:T(8,128)S(1)} %fusion.first_ref.refs_0_), channel_id=1, source_target_pairs={{0,6},{2,0},{4,2},{6,4},{1,7},{3,1},{5,3},{7,5},{8,14},{10,8},{12,... | collective-permute-start | bytes 12296 | tf_op jit(solution)/shard_map/ppermute | solution.py:54
  38.7 7.5 %collective-permute-start.8 = (f32[32,32]{1,0:T(8,128)S(1)}, f32[32,32]{1,0:T(8,128)S(1)}, u32[]{:S(2)}, u32[]{:S(2)}) collective-permute-start(f32[32,32]{1,0:T(8,128)S(1)} %fusion.first_ref.refs_0_), channel_id=1, source_target_pairs={{0,2},{2,4},{4,6},{6,0},{1,3},{3,5},{5,7},{7,1},{8,10},{10,12},{12... | collective-permute-start | bytes 12296 | tf_op jit(solution)/shard_map/ppermute | solution.py:54
  46.6 10.2 %collective-permute-start.15 = (f32[32,256]{1,0:T(8,128)S(1)}, f32[32,256]{1,0:T(8,128)S(1)}, u32[]{:S(2)}, u32[]{:S(2)}) collective-permute-start(f32[32,256]{1,0:T(8,128)S(1)} %shard_map.63.first_ref), channel_id=1, source_target_pairs={{0,32},{16,48},{32,0},{48,16},{1,33},{17,49},{33,1},{49,17},{2,34}... | collective-permute-start | bytes 98312 | tf_op jit(solution)/shard_map/ppermute | solution.py:54
  51.5 5.2 %collective-permute-start.14 = (f32[32,256]{1,0:T(8,128)S(1)}, f32[32,256]{1,0:T(8,128)S(1)}, u32[]{:S(2)}, u32[]{:S(2)}) collective-permute-start(f32[32,256]{1,0:T(8,128)S(1)} %shard_map.63.first_ref), channel_id=1, source_target_pairs={{0,48},{16,0},{32,16},{48,32},{1,49},{17,1},{33,17},{49,33},{2,50}... | collective-permute-start | bytes 98312 | tf_op jit(solution)/shard_map/ppermute | solution.py:54
  51.5 5.2 %collective-permute-start.13 = (f32[32,256]{1,0:T(8,128)S(1)}, f32[32,256]{1,0:T(8,128)S(1)}, u32[]{:S(2)}, u32[]{:S(2)}) collective-permute-start(f32[32,256]{1,0:T(8,128)S(1)} %shard_map.63.first_ref), channel_id=1, source_target_pairs={{0,16},{16,32},{32,48},{48,0},{1,17},{17,33},{33,49},{49,1},{2,18}... | collective-permute-start | bytes 98312 | tf_op jit(solution)/shard_map/ppermute | solution.py:54
  79.0 7.0 %collective-permute-start.16 = (f32[32,8192]{1,0:T(8,128)S(1)}, f32[32,8192]{1,0:T(8,128)S(1)}, u32[]{:S(2)}, u32[]{:S(2)}) collective-permute-start(f32[32,8192]{1,0:T(8,128)S(1)} %shard_map.65.q_ref), channel_id=1, source_target_pairs={{0,1},{1,0},{2,3},{3,2},{4,5},{5,4},{6,7},{7,6},{8,9},{9,8},{10,11... | collective-permute-start | bytes 3145736 | tf_op jit(solution)/shard_map/ppermute | solution.py:50
  83.7 2.3 %collective-permute-start.11 = (f32[32,64]{1,0:T(8,128)S(1)}, f32[32,64]{1,0:T(8,128)S(1)}, u32[]{:S(2)}, u32[]{:S(2)}) collective-permute-start(f32[32,64]{1,0:T(8,128)S(1)} %get-tuple-element.27), channel_id=1, source_target_pairs={{0,1},{1,0},{2,3},{3,2},{4,5},{5,4},{6,7},{7,6},{8,9},{9,8},{10,11... | collective-permute-start | bytes 24584 | tf_op jit(solution)/shard_map/ppermute | solution.py:50

commit v8 on v7

--- a/solution.py
+++ b/solution.py
@@ -169,15 +169,20 @@
 
 def four_kernel(first_ref, second_ref, third_ref, fourth_ref, out_ref):
     value = (first_ref[...] + second_ref[...]) + (third_ref[...] + fourth_ref[...])
-    out_ref[...] = value
-
-
-def sum_four(parts):
+    if len(out_ref.shape) == len(value.shape):
+        out_ref[...] = value
+    else:
+        for copy in range(out_ref.shape[0]):
+            out_ref[copy] = value
+
+
+def sum_four(parts, count=None):
+    shape = parts[0].shape if count is None else (count,) + parts[0].shape
     return pl.pallas_call(
         four_kernel,
         in_specs=[IN_VMEM] * 4,
         out_specs=IN_VMEM,
-        out_shape=f32(*parts[0].shape),
+        out_shape=f32(*shape),
         compiler_params=PARAMS,
         cost_estimate=cost(1 << 18, 2 << 20),
     )(*parts)
@@ -324,9 +329,8 @@
     terms, send = lax.optimization_barrier((terms, send))
     parts = [terms] + shifts(terms, "x", NX)
     received = swap(send)
-    terms = sum_four(parts)
-    terms = terms + shifts(terms, "w", NW)[0]
-    summed = sum_four([terms] + shifts(terms, "v", NV))
+    terms = sum_four(parts, NV * NW)
+    summed = sum_parts(exchange(terms, ("v", "w")))
 
     gram = jnp.einsum("kr,lr->kl", summed, summed, precision=HIGH)
     grams = [gram] + shifts(gram, "y", NY)

time: 88 us -> 87.2 us (level)
  starting transfers between devices: 38.8 us -> 22.9 us
  blocking collectives: 21.9 us -> 33.1 us
  waiting for transfers between devices: 15.3 us -> 19.2 us
    ppermute x13 -> x9, starting transfers between devices: 24.9 us -> 10.2 us  [shifts(): lax.ppermute(a, axis, [(i, (i + s) % size) for i in range(size)])]
    all_to_all x1 -> x2, blocking collectives: 21.9 us -> 33.1 us  [exchange(): return lax.all_to_all(a, axes, 0, 0)]
    ppermute x13 -> x9, waiting for transfers between devices: 13.6 us -> 17.8 us  [shifts(): lax.ppermute(a, axis, [(i, (i + s) % size) for i in range(size)])]
  transfers between devices with their start and end apart: 18 -> 14, of which waited for: 11 -> 9; matrix products, arithmetic and copies ran while one was open for 0% -> 0% of each run, Pallas kernels for 5% -> 5%
where the time goes in v8:
time: 87.2 us; the launch traced here: 86.9 us
  blocking collectives  33.1 us (38%)
  starting transfers between devices  22.9 us (26%)
  waiting for transfers between devices  19.2 us (22%)
  Pallas kernels  10.7 us (12%)
    all_to_all x2, blocking collectives, exchange(): return lax.all_to_all(a, axes, 0, 0)  33.1 us
    ppermute x9, waiting for transfers between devices, shifts(): lax.ppermute(a, axis, [(i, (i + s) % size) for i in range(size)])  17.8 us
    ppermute x9, starting transfers between devices, shifts(): lax.ppermute(a, axis, [(i, (i + s) % size) for i in range(size)])  10.2 us
    ppermute x4, starting transfers between devices, swap(): return lax.ppermute(a, 'c', [(0, 1), (1, 0)])  8.14 us
    all_to_all x1, starting transfers between devices, exchange(): return lax.all_to_all(a, axes, 0, 0)  4.59 us
    pallas_call x2, Pallas kernels, tail(): pl.pallas_call(functools.partial(tail_kernel, bool(before)), in_specs=[IN...  3.23 us
    pallas_call x1, Pallas kernels, left(): pl.pallas_call(left_kernel, in_specs=[IN_SMEM, IN_HBM, IN_HBM, IN_HBM], o...  2.89 us
    pallas_call x1, Pallas kernels, factors(): pl.pallas_call(factor_kernel, in_specs=[IN_VMEM] * (NY + 1), out_specs=[I...  2.86 us
  transfers between devices with their start and end apart: 14, of which 9 were waited for; matrix products, arithmetic and copies ran while one was open for 0% of the time, Pallas kernels for 5%

profile of v8, /device:TPU:1, one launch (start us, length us, event | category | flops | bytes accessed | tf_op | source)
XLA Modules:
  0.0 86.9 jit_solution(16362505830190204448)
XLA Ops:
  0.6 2.9 %shard_map.58 = (bf16[64,8192]{1,0:T(8,128)(2,1)S(1)}, bf16[64,8192]{1,0:T(8,128)(2,1)S(1)}, f32[64,8192]{1,0:T(8,128)S(1)}, f32[32,64]{1,0:T(8,128)S(1)}, f32[32,64]{1,0:T(8,128)S(1)}) custom-call(s32[1]{0:T(128)} %bitcast.core_ref, bf16[1,2,64,8192]{3,2,1,0:T(8,128)(2,1)} %grads_hbm.1, bf16[1,2,64,8192]{3,2,1,0:T(8,128)(2,1)} %errors_hbm.1, ...), custom_call_target="tpu_custom_call" | custom-call | flops 134217728 | bytes 9437184 | tf_op jit(solution)/shard_map/pallas_call | solution.py:119
  3.5 3.3 %collective-permute-start = (f32[32,64]{1,0:T(8,128)S(1)}, f32[32,64]{1,0:T(8,128)S(1)}, u32[]{:S(2)}, u32[]{:S(2)}) collective-permute-start(f32[32,64]{1,0:T(8,128)S(1)} %get-tuple-element.24), channel_id=1, source_target_pairs={{0,1},{1,0},{2,3},{3,2},{4,5},{5,4},{6,7},{7,6},{8,9},{9,8},{10,11... | collective-permute-start | bytes 24584 | tf_op jit(solution)/shard_map/ppermute | solution.py:50
  6.9 0.8 collective-permute-done
  7.7 0.1 pad_maximum_fusion.first_ref
  7.8 0.4 collective-permute-start.8
  8.1 1.0 %collective-permute-start.3 = (f32[32,128]{1,0:T(8,128)S(1)}, f32[32,128]{1,0:T(8,128)S(1)}, u32[]{:S(2)}, u32[]{:S(2)}) collective-permute-start(f32[32,128]{1,0:T(8,128)S(1)} %pad_maximum_fusion.first_ref), channel_id=1, source_target_pairs={{0,128},{64,192},{128,0},{192,64},{1,129},{65,193},{129,1},{193,65... | collective-permute-start | bytes 49160 | tf_op jit(solution)/shard_map/ppermute | solution.py:54
  9.2 0.9 collective-permute-start.2
  10.0 0.6 collective-permute-start.1
  10.6 1.6 %collective-permute-done.3.fourth_ref = f32[32,128]{1,0:T(8,128)S(1)} collective-permute-done((f32[32,128]{1,0:T(8,128)S(1)}, f32[32,128]{1,0:T(8,128)S(1)}, u32[]{:S(2)}, u32[]{:S(2)}) %collective-permute-start.3) | collective-permute-done | bytes 16416 | tf_op jit(solution)/shard_map/ppermute | solution.py:54
  12.2 0.0 collective-permute-done.2.third_ref
  12.2 1.6 %collective-permute-done.1.second_ref = f32[32,128]{1,0:T(8,128)S(1)} collective-permute-done((f32[32,128]{1,0:T(8,128)S(1)}, f32[32,128]{1,0:T(8,128)S(1)}, u32[]{:S(2)}, u32[]{:S(2)}) %collective-permute-start.1) | collective-permute-done | bytes 16416 | tf_op jit(solution)/shard_map/ppermute | solution.py:54
  13.8 16.0 %all_to_all.15.parts_ref = f32[8,32,128]{2,1,0:T(8,128)S(1)} all-to-all(f32[8,32,128]{2,1,0:T(8,128)S(1)} %shard_map.59), channel_id=1, replica_groups=mesh['x'=4,'v'=4,'w'=2,'y'=4,'c'=2] {'v','w'}, dimensions={0} | all-to-all | bytes 262144 | tf_op jit(solution)/shard_map/all_to_all | solution.py:58
  29.9 0.0 collective-permute-done.8.received_ref
  29.9 1.3 %shard_map.62 = f32[32,32,256]{2,1,0:T(8,128)} custom-call(f32[32,128]{1,0:T(8,128)S(1)} %shard_map.60.summed_ref, bf16[64,8192]{1,0:T(8,128)(2,1)S(1)} %get-tuple-element.29.merged_ref, f32[64,8192]{1,0:T(8,128)S(1)} %collective-permute-done.8.received_ref), custom_call_target="tpu_custom_call" | custom-call | flops 201326592 | bytes 4194304 | tf_op jit(solution)/shard_map/pallas_call | solution.py:225
  31.2 4.6 %all-to-all-start.1 = ((f32[32,32,256]{2,1,0:T(8,128)}), f32[32,32,256]{2,1,0:T(8,128)S(1)}, u32[]{:S(2)}, u32[]{:S(2)}) async-start(f32[32,32,256]{2,1,0:T(8,128)} %shard_map.62), calls=%async_computation.1 | async-start | bytes 2097152 | tf_op jit(solution)/shard_map/all_to_all | solution.py:58
  35.8 0.1 fusion.first_ref.refs_0_
  35.9 2.8 %collective-permute-start.6 = (f32[32,32]{1,0:T(8,128)S(1)}, f32[32,32]{1,0:T(8,128)S(1)}, u32[]{:S(2)}, u32[]{:S(2)}) collective-permute-start(f32[32,32]{1,0:T(8,128)S(1)} %fusion.first_ref.refs_0_), channel_id=1, source_target_pairs={{0,4},{2,6},{4,0},{6,2},{1,5},{3,7},{5,1},{7,3},{8,12},{10,14},{12... | collective-permute-start | bytes 12296 | tf_op jit(solution)/shard_map/ppermute | solution.py:54
  38.8 0.9 %collective-permute-start.5 = (f32[32,32]{1,0:T(8,128)S(1)}, f32[32,32]{1,0:T(8,128)S(1)}, u32[]{:S(2)}, u32[]{:S(2)}) collective-permute-start(f32[32,32]{1,0:T(8,128)S(1)} %fusion.first_ref.refs_0_), channel_id=1, source_target_pairs={{0,6},{2,0},{4,2},{6,4},{1,7},{3,1},{5,3},{7,5},{8,14},{10,8},{12,... | collective-permute-start | bytes 12296 | tf_op jit(solution)/shard_map/ppermute | solution.py:54
  39.7 0.6 collective-permute-start.4
  40.2 0.2 collective-permute-done.6.fourth_ref.refs_3_
  40.5 11.0 %collective-permute-done.5.third_ref.refs_2_ = f32[32,32]{1,0:T(8,128)S(1)} collective-permute-done((f32[32,32]{1,0:T(8,128)S(1)}, f32[32,32]{1,0:T(8,128)S(1)}, u32[]{:S(2)}, u32[]{:S(2)}) %collective-permute-start.5) | collective-permute-done | bytes 4128 | tf_op jit(solution)/shard_map/ppermute | solution.py:54
  51.4 1.3 %collective-permute-done.4.second_ref.refs_1_ = f32[32,32]{1,0:T(8,128)S(1)} collective-permute-done((f32[32,32]{1,0:T(8,128)S(1)}, f32[32,32]{1,0:T(8,128)S(1)}, u32[]{:S(2)}, u32[]{:S(2)}) %collective-permute-start.4) | collective-permute-done | bytes 4128 | tf_op jit(solution)/shard_map/ppermute | solution.py:54
  52.7 0.0 all-to-all-done.1.parts_ref
  52.7 0.1 shard_map.63.first_ref
  52.8 0.9 %collective-permute-start.11 = (f32[32,256]{1,0:T(8,128)S(1)}, f32[32,256]{1,0:T(8,128)S(1)}, u32[]{:S(2)}, u32[]{:S(2)}) collective-permute-start(f32[32,256]{1,0:T(8,128)S(1)} %shard_map.63.first_ref), channel_id=1, source_target_pairs={{0,32},{16,48},{32,0},{48,16},{1,33},{17,49},{33,1},{49,17},{2,34}... | collective-permute-start | bytes 98312 | tf_op jit(solution)/shard_map/ppermute | solution.py:54
  53.7 2.5 %collective-permute-start.10 = (f32[32,256]{1,0:T(8,128)S(1)}, f32[32,256]{1,0:T(8,128)S(1)}, u32[]{:S(2)}, u32[]{:S(2)}) collective-permute-start(f32[32,256]{1,0:T(8,128)S(1)} %shard_map.63.first_ref), channel_id=1, source_target_pairs={{0,48},{16,0},{32,16},{48,32},{1,49},{17,1},{33,17},{49,33},{2,50}... | collective-permute-start | bytes 98312 | tf_op jit(solution)/shard_map/ppermute | solution.py:54
  56.2 0.0 collective-permute-start.9
  56.2 2.9 %shard_map.61 = (f32[32,32]{1,0:T(8,128)S(1)}, f32[32,64]{1,0:T(8,128)S(1)}, f32[32,64]{1,0:T(8,128)S(1)}) custom-call(f32[32,32]{1,0:T(8,128)S(1)} %fusion.first_ref.refs_0_, f32[32,32]{1,0:T(8,128)S(1)} %collective-permute-done.4.second_ref.refs_1_, f32[32,32]{1,0:T(8,128)S(1)} %collective-permute-done.5.third_ref.refs_2_, ...), custom_call_target="tpu_custom_call" | custom-call | flops 1048576 | bytes 12582912 | tf_op jit(solution)/shard_map/pallas_call | solution.py:262
  59.1 0.5 collective-permute-done.11.fourth_ref
  59.5 0.0 collective-permute-done.10.third_ref
  59.5 1.6 %collective-permute-done.9.second_ref = f32[32,256]{1,0:T(8,128)S(1)} collective-permute-done((f32[32,256]{1,0:T(8,128)S(1)}, f32[32,256]{1,0:T(8,128)S(1)}, u32[]{:S(2)}, u32[]{:S(2)}) %collective-permute-start.9) | collective-permute-done | bytes 32800 | tf_op jit(solution)/shard_map/ppermute | solution.py:54
  61.2 0.3 shard_map.64
  61.5 17.1 %all_to_all.16.blocks_ref = f32[32,32,256]{2,1,0:T(8,128)S(1)} all-to-all(f32[32,32,256]{2,1,0:T(8,128)S(1)} %shard_map.64), channel_id=1, replica_groups=mesh['x'=4,'v'=4,'w'=2,'y'=4,'c'=2] {'x','w','y'}, dimensions={0} | all-to-all | bytes 2097152 | tf_op jit(solution)/shard_map/all_to_all | solution.py:58
  78.5 0.1 shard_map.65.q_ref
  78.6 4.3 %collective-permute-start.12 = (f32[32,8192]{1,0:T(8,128)S(1)}, f32[32,8192]{1,0:T(8,128)S(1)}, u32[]{:S(2)}, u32[]{:S(2)}) collective-permute-start(f32[32,8192]{1,0:T(8,128)S(1)} %shard_map.65.q_ref), channel_id=1, source_target_pairs={{0,1},{1,0},{2,3},{3,2},{4,5},{5,4},{6,7},{7,6},{8,9},{9,8},{10,11... | collective-permute-start | bytes 3145736 | tf_op jit(solution)/shard_map/ppermute | solution.py:50
  83.0 0.1 collective-permute-start.7
  83.1 1.6 %shard_map.66 = (bf16[1,2,64,8192]{3,2,1,0:T(8,128)(2,1)}, f32[2,32,8192]{2,1,0:T(8,128)}, f32[2,32,64]{2,1,0:T(8,128)}) custom-call(s32[1]{0:T(128)} %bitcast.core_ref, f32[32,64]{1,0:T(8,128)S(1)} %get-tuple-element.28.ortho_ref, f32[32,8192]{1,0:T(8,128)S(1)} %shard_map.65.q_ref, bf16[64,8192]{1,0:T(8,128)(2,1)S(1)} %get-tuple-element.29.merged_ref), custom_call_target="tpu_custom_call" | custom-call | flops 33554432 | bytes 4194304 | tf_op jit(solution)/shard_map/pallas_call | solution.py:307
  84.7 0.6 collective-permute-done.7.ortho_ref
  85.3 0.0 collective-permute-done.12.q_ref
  85.3 1.6 %shard_map.67 = (bf16[1,2,64,8192]{3,2,1,0:T(8,128)(2,1)}, f32[2,32,8192]{2,1,0:T(8,128)}, f32[2,32,64]{2,1,0:T(8,128)}) custom-call(s32[1]{0:T(128)} %bitcast.core_ref, f32[32,64]{1,0:T(8,128)S(1)} %collective-permute-done.7.ortho_ref, f32[32,8192]{1,0:T(8,128)S(1)} %collective-permute-done.12.q_ref, ...), custom_call_target="tpu_custom_call", output_to_operand_aliasing={{0}: (4, {}), {1}: (5, {}), {2}: (6, {})} | custom-call | flops 33554432 | bytes 4194304 | tf_op jit(solution)/shard_map/pallas_call | solution.py:307
  (2 shorter events, 0.0 us)
Async XLA Ops:
  3.5 4.2 %collective-permute-start = (f32[32,64]{1,0:T(8,128)S(1)}, f32[32,64]{1,0:T(8,128)S(1)}, u32[]{:S(2)}, u32[]{:S(2)}) collective-permute-start(f32[32,64]{1,0:T(8,128)S(1)} %get-tuple-element.24), channel_id=1, source_target_pairs={{0,1},{1,0},{2,3},{3,2},{4,5},{5,4},{6,7},{7,6},{8,9},{9,8},{10,11... | collective-permute-start | bytes 24584 | tf_op jit(solution)/shard_map/ppermute | solution.py:50
  7.8 22.1 %collective-permute-start.8 = (f32[64,8192]{1,0:T(8,128)S(1)}, f32[64,8192]{1,0:T(8,128)S(1)}, u32[]{:S(2)}, u32[]{:S(2)}) collective-permute-start(f32[64,8192]{1,0:T(8,128)S(1)} %get-tuple-element.30), channel_id=1, source_target_pairs={{0,1},{1,0},{2,3},{3,2},{4,5},{5,4},{6,7},{7,6},{8,9},{9,8},{10,11... | collective-permute-start | bytes 6291464 | tf_op jit(solution)/shard_map/ppermute | solution.py:50
  8.1 4.1 %collective-permute-start.3 = (f32[32,128]{1,0:T(8,128)S(1)}, f32[32,128]{1,0:T(8,128)S(1)}, u32[]{:S(2)}, u32[]{:S(2)}) collective-permute-start(f32[32,128]{1,0:T(8,128)S(1)} %pad_maximum_fusion.first_ref), channel_id=1, source_target_pairs={{0,128},{64,192},{128,0},{192,64},{1,129},{65,193},{129,1},{193,65... | collective-permute-start | bytes 49160 | tf_op jit(solution)/shard_map/ppermute | solution.py:54
  9.2 3.1 %collective-permute-start.2 = (f32[32,128]{1,0:T(8,128)S(1)}, f32[32,128]{1,0:T(8,128)S(1)}, u32[]{:S(2)}, u32[]{:S(2)}) collective-permute-start(f32[32,128]{1,0:T(8,128)S(1)} %pad_maximum_fusion.first_ref), channel_id=1, source_target_pairs={{0,192},{64,0},{128,64},{192,128},{1,193},{65,1},{129,65},{193,129... | collective-permute-start | bytes 49160 | tf_op jit(solution)/shard_map/ppermute | solution.py:54
  10.0 3.8 %collective-permute-start.1 = (f32[32,128]{1,0:T(8,128)S(1)}, f32[32,128]{1,0:T(8,128)S(1)}, u32[]{:S(2)}, u32[]{:S(2)}) collective-permute-start(f32[32,128]{1,0:T(8,128)S(1)} %pad_maximum_fusion.first_ref), channel_id=1, source_target_pairs={{0,64},{64,128},{128,192},{192,0},{1,65},{65,129},{129,193},{193,1... | collective-permute-start | bytes 49160 | tf_op jit(solution)/shard_map/ppermute | solution.py:54
  31.2 21.5 %all-to-all-start.1 = ((f32[32,32,256]{2,1,0:T(8,128)}), f32[32,32,256]{2,1,0:T(8,128)S(1)}, u32[]{:S(2)}, u32[]{:S(2)}) async-start(f32[32,32,256]{2,1,0:T(8,128)} %shard_map.62), calls=%async_computation.1 | async-start | bytes 2097152 | tf_op jit(solution)/shard_map/all_to_all | solution.py:58
  35.9 4.5 %collective-permute-start.6 = (f32[32,32]{1,0:T(8,128)S(1)}, f32[32,32]{1,0:T(8,128)S(1)}, u32[]{:S(2)}, u32[]{:S(2)}) collective-permute-start(f32[32,32]{1,0:T(8,128)S(1)} %fusion.first_ref.refs_0_), channel_id=1, source_target_pairs={{0,4},{2,6},{4,0},{6,2},{1,5},{3,7},{5,1},{7,3},{8,12},{10,14},{12... | collective-permute-start | bytes 12296 | tf_op jit(solution)/shard_map/ppermute | solution.py:54
  38.8 12.6 %collective-permute-start.5 = (f32[32,32]{1,0:T(8,128)S(1)}, f32[32,32]{1,0:T(8,128)S(1)}, u32[]{:S(2)}, u32[]{:S(2)}) collective-permute-start(f32[32,32]{1,0:T(8,128)S(1)} %fusion.first_ref.refs_0_), channel_id=1, source_target_pairs={{0,6},{2,0},{4,2},{6,4},{1,7},{3,1},{5,3},{7,5},{8,14},{10,8},{12,... | collective-permute-start | bytes 12296 | tf_op jit(solution)/shard_map/ppermute | solution.py:54
  39.7 13.0 %collective-permute-start.4 = (f32[32,32]{1,0:T(8,128)S(1)}, f32[32,32]{1,0:T(8,128)S(1)}, u32[]{:S(2)}, u32[]{:S(2)}) collective-permute-start(f32[32,32]{1,0:T(8,128)S(1)} %fusion.first_ref.refs_0_), channel_id=1, source_target_pairs={{0,2},{2,4},{4,6},{6,0},{1,3},{3,5},{5,7},{7,1},{8,10},{10,12},{12... | collective-permute-start | bytes 12296 | tf_op jit(solution)/shard_map/ppermute | solution.py:54
  52.8 6.8 %collective-permute-start.11 = (f32[32,256]{1,0:T(8,128)S(1)}, f32[32,256]{1,0:T(8,128)S(1)}, u32[]{:S(2)}, u32[]{:S(2)}) collective-permute-start(f32[32,256]{1,0:T(8,128)S(1)} %shard_map.63.first_ref), channel_id=1, source_target_pairs={{0,32},{16,48},{32,0},{48,16},{1,33},{17,49},{33,1},{49,17},{2,34}... | collective-permute-start | bytes 98312 | tf_op jit(solution)/shard_map/ppermute | solution.py:54
  53.7 5.8 %collective-permute-start.10 = (f32[32,256]{1,0:T(8,128)S(1)}, f32[32,256]{1,0:T(8,128)S(1)}, u32[]{:S(2)}, u32[]{:S(2)}) collective-permute-start(f32[32,256]{1,0:T(8,128)S(1)} %shard_map.63.first_ref), channel_id=1, source_target_pairs={{0,48},{16,0},{32,16},{48,32},{1,49},{17,1},{33,17},{49,33},{2,50}... | collective-permute-start | bytes 98312 | tf_op jit(solution)/shard_map/ppermute | solution.py:54
  56.2 5.0 %collective-permute-start.9 = (f32[32,256]{1,0:T(8,128)S(1)}, f32[32,256]{1,0:T(8,128)S(1)}, u32[]{:S(2)}, u32[]{:S(2)}) collective-permute-start(f32[32,256]{1,0:T(8,128)S(1)} %shard_map.63.first_ref), channel_id=1, source_target_pairs={{0,16},{16,32},{32,48},{48,0},{1,17},{17,33},{33,49},{49,1},{2,18}... | collective-permute-start | bytes 98312 | tf_op jit(solution)/shard_map/ppermute | solution.py:54
  78.6 6.7 %collective-permute-start.12 = (f32[32,8192]{1,0:T(8,128)S(1)}, f32[32,8192]{1,0:T(8,128)S(1)}, u32[]{:S(2)}, u32[]{:S(2)}) collective-permute-start(f32[32,8192]{1,0:T(8,128)S(1)} %shard_map.65.q_ref), channel_id=1, source_target_pairs={{0,1},{1,0},{2,3},{3,2},{4,5},{5,4},{6,7},{7,6},{8,9},{9,8},{10,11... | collective-permute-start | bytes 3145736 | tf_op jit(solution)/shard_map/ppermute | solution.py:50
  83.0 2.3 %collective-permute-start.7 = (f32[32,64]{1,0:T(8,128)S(1)}, f32[32,64]{1,0:T(8,128)S(1)}, u32[]{:S(2)}, u32[]{:S(2)}) collective-permute-start(f32[32,64]{1,0:T(8,128)S(1)} %get-tuple-element.27), channel_id=1, source_target_pairs={{0,1},{1,0},{2,3},{3,2},{4,5},{5,4},{6,7},{7,6},{8,9},{9,8},{10,11... | collective-permute-start | bytes 24584 | tf_op jit(solution)/shard_map/ppermute | solution.py:50

commit v9 on v8

--- a/solution.py
+++ b/solution.py
@@ -233,8 +233,28 @@
     )(summed, keep(merged, pltpu.VMEM), received)
 
 
+def gram_kernel(summed_ref, out_ref):
+    summed = summed_ref[...]
+    gram = lax.dot_general(
+        summed, summed, (((1,), (1,)), ((), ())), precision=HIGH, preferred_element_type=jnp.float32
+    )
+    out_ref[...] = jnp.concatenate([gram[i : i + 8] for i in range(0, R, 8)], axis=1)
+
+
+def packed_gram(summed):
+    return pl.pallas_call(
+        gram_kernel,
+        in_specs=[IN_VMEM],
+        out_specs=IN_VMEM,
+        out_shape=vmem(8, R * R // 8),
+        compiler_params=PARAMS,
+        cost_estimate=cost(1 << 18, 1 << 15),
+    )(keep(summed, pltpu.VMEM))
+
+
 def factor_kernel(first_ref, second_ref, third_ref, fourth_ref, summed_ref, inverse_ref, own_ref, theirs_ref):
-    gram = (first_ref[...] + second_ref[...]) + (third_ref[...] + fourth_ref[...])
+    packed = (first_ref[...] + second_ref[...]) + (third_ref[...] + fourth_ref[...])
+    gram = jnp.concatenate([packed[:, i * R : (i + 1) * R] for i in range(R // 8)], axis=0)
     row = lax.broadcasted_iota(jnp.int32, (R, 2 * R), 0)
     lane = lax.broadcasted_iota(jnp.int32, (R, 2 * R), 1)
     unit = (lane - R == row).astype(jnp.float32)[:, R:]
@@ -332,7 +352,7 @@
     terms = sum_four(parts, NV * NW)
     summed = sum_parts(exchange(terms, ("v", "w")))
 
-    gram = jnp.einsum("kr,lr->kl", summed, summed, precision=HIGH)
+    gram = packed_gram(summed)
     grams = [gram] + shifts(gram, "y", NY)
 
     half = exchange(right(summed, merged, received), ("x", "w", "y"))

time: 87.2 us -> 86 us (0.986)
  waiting for transfers between devices: 19.2 us -> 16.3 us
  starting transfers between devices: 22.9 us -> 25 us
    ppermute x9, waiting for transfers between devices: 17.8 us -> 9.32 us  [shifts(): lax.ppermute(a, axis, [(i, (i + s) % size) for i in range(size)])]
    all_to_all x1, waiting for transfers between devices: 0.01 us -> 5.54 us  [exchange(): return lax.all_to_all(a, axes, 0, 0)]
    ppermute x4, starting transfers between devices: 8.14 us -> 10.3 us  [swap(): return lax.ppermute(a, 'c', [(0, 1), (1, 0)])]
  transfers between devices with their start and end apart: 14 -> 14, of which waited for: 9 -> 10; matrix products, arithmetic and copies ran while one was open for 0% -> 0% of each run, Pallas kernels for 5% -> 6%
where the time goes in v9:
time: 86 us; the launch traced here: 85.7 us
  blocking collectives  32.7 us (38%)
  starting transfers between devices  25 us (29%)
  waiting for transfers between devices  16.3 us (19%)
  Pallas kernels  10.9 us (13%)
    all_to_all x2, blocking collectives, exchange(): return lax.all_to_all(a, axes, 0, 0)  32.7 us
    ppermute x4, starting transfers between devices, swap(): return lax.ppermute(a, 'c', [(0, 1), (1, 0)])  10.3 us
    ppermute x9, starting transfers between devices, shifts(): lax.ppermute(a, axis, [(i, (i + s) % size) for i in range(size)])  10.1 us
    ppermute x9, waiting for transfers between devices, shifts(): lax.ppermute(a, axis, [(i, (i + s) % size) for i in range(size)])  9.32 us
    all_to_all x1, waiting for transfers between devices, exchange(): return lax.all_to_all(a, axes, 0, 0)  5.54 us
    all_to_all x1, starting transfers between devices, exchange(): return lax.all_to_all(a, axes, 0, 0)  4.59 us
    pallas_call x2, Pallas kernels, tail(): pl.pallas_call(functools.partial(tail_kernel, bool(before)), in_specs=[IN...  3.22 us
    pallas_call x1, Pallas kernels, left(): pl.pallas_call(left_kernel, in_specs=[IN_SMEM, IN_HBM, IN_HBM, IN_HBM], o...  2.89 us
  transfers between devices with their start and end apart: 14, of which 10 were waited for; matrix products, arithmetic and copies ran while one was open for 0% of the time, Pallas kernels for 6%

profile of v9, /device:TPU:1, one launch (start us, length us, event | category | flops | bytes accessed | tf_op | source)
XLA Modules:
  0.0 85.7 jit_solution(17662173132939795152)
XLA Ops:
  0.6 2.9 %shard_map.58 = (bf16[64,8192]{1,0:T(8,128)(2,1)S(1)}, bf16[64,8192]{1,0:T(8,128)(2,1)S(1)}, f32[64,8192]{1,0:T(8,128)S(1)}, f32[32,64]{1,0:T(8,128)S(1)}, f32[32,64]{1,0:T(8,128)S(1)}) custom-call(s32[1]{0:T(128)} %bitcast.core_ref, bf16[1,2,64,8192]{3,2,1,0:T(8,128)(2,1)} %grads_hbm.1, bf16[1,2,64,8192]{3,2,1,0:T(8,128)(2,1)} %errors_hbm.1, ...), custom_call_target="tpu_custom_call" | custom-call | flops 134217728 | bytes 9437184 | tf_op jit(solution)/shard_map/pallas_call | solution.py:119
  3.5 3.3 %collective-permute-start = (f32[32,64]{1,0:T(8,128)S(1)}, f32[32,64]{1,0:T(8,128)S(1)}, u32[]{:S(2)}, u32[]{:S(2)}) collective-permute-start(f32[32,64]{1,0:T(8,128)S(1)} %get-tuple-element.24), channel_id=1, source_target_pairs={{0,1},{1,0},{2,3},{3,2},{4,5},{5,4},{6,7},{7,6},{8,9},{9,8},{10,11... | collective-permute-start | bytes 24584 | tf_op jit(solution)/shard_map/ppermute | solution.py:50
  6.9 0.8 collective-permute-done
  7.7 0.1 pad_maximum_fusion.first_ref
  7.8 0.4 collective-permute-start.8
  8.1 1.0 %collective-permute-start.3 = (f32[32,128]{1,0:T(8,128)S(1)}, f32[32,128]{1,0:T(8,128)S(1)}, u32[]{:S(2)}, u32[]{:S(2)}) collective-permute-start(f32[32,128]{1,0:T(8,128)S(1)} %pad_maximum_fusion.first_ref), channel_id=1, source_target_pairs={{0,128},{64,192},{128,0},{192,64},{1,129},{65,193},{129,1},{193,65... | collective-permute-start | bytes 49160 | tf_op jit(solution)/shard_map/ppermute | solution.py:54
  9.2 0.9 %collective-permute-start.2 = (f32[32,128]{1,0:T(8,128)S(1)}, f32[32,128]{1,0:T(8,128)S(1)}, u32[]{:S(2)}, u32[]{:S(2)}) collective-permute-start(f32[32,128]{1,0:T(8,128)S(1)} %pad_maximum_fusion.first_ref), channel_id=1, source_target_pairs={{0,192},{64,0},{128,64},{192,128},{1,193},{65,1},{129,65},{193,129... | collective-permute-start | bytes 49160 | tf_op jit(solution)/shard_map/ppermute | solution.py:54
  10.0 0.6 collective-permute-start.1
  10.6 1.6 %collective-permute-done.3.fourth_ref = f32[32,128]{1,0:T(8,128)S(1)} collective-permute-done((f32[32,128]{1,0:T(8,128)S(1)}, f32[32,128]{1,0:T(8,128)S(1)}, u32[]{:S(2)}, u32[]{:S(2)}) %collective-permute-start.3) | collective-permute-done | bytes 16416 | tf_op jit(solution)/shard_map/ppermute | solution.py:54
  12.2 0.0 collective-permute-done.2.third_ref
  12.2 1.6 %collective-permute-done.1.second_ref = f32[32,128]{1,0:T(8,128)S(1)} collective-permute-done((f32[32,128]{1,0:T(8,128)S(1)}, f32[32,128]{1,0:T(8,128)S(1)}, u32[]{:S(2)}, u32[]{:S(2)}) %collective-permute-start.1) | collective-permute-done | bytes 16416 | tf_op jit(solution)/shard_map/ppermute | solution.py:54
  13.8 16.0 %all_to_all.15.parts_ref = f32[8,32,128]{2,1,0:T(8,128)S(1)} all-to-all(f32[8,32,128]{2,1,0:T(8,128)S(1)} %shard_map.59), channel_id=1, replica_groups=mesh['x'=4,'v'=4,'w'=2,'y'=4,'c'=2] {'v','w'}, dimensions={0} | all-to-all | bytes 262144 | tf_op jit(solution)/shard_map/all_to_all | solution.py:58
  29.9 0.0 collective-permute-done.8.received_ref
  29.9 1.3 %shard_map.63 = f32[32,32,256]{2,1,0:T(8,128)} custom-call(f32[32,128]{1,0:T(8,128)S(1)} %shard_map.60.summed_ref, bf16[64,8192]{1,0:T(8,128)(2,1)S(1)} %get-tuple-element.29.merged_ref, f32[64,8192]{1,0:T(8,128)S(1)} %collective-permute-done.8.received_ref), custom_call_target="tpu_custom_call" | custom-call | flops 201326592 | bytes 4194304 | tf_op jit(solution)/shard_map/pallas_call | solution.py:225
  31.2 4.6 %all-to-all-start.1 = ((f32[32,32,256]{2,1,0:T(8,128)}), f32[32,32,256]{2,1,0:T(8,128)S(1)}, u32[]{:S(2)}, u32[]{:S(2)}) async-start(f32[32,32,256]{2,1,0:T(8,128)} %shard_map.63), calls=%async_computation.1 | async-start | bytes 2097152 | tf_op jit(solution)/shard_map/all_to_all | solution.py:58
  35.8 0.2 shard_map.61.first_ref.refs_0_
  36.0 2.8 %collective-permute-start.6 = (f32[8,128]{1,0:T(8,128)S(1)}, f32[8,128]{1,0:T(8,128)S(1)}, u32[]{:S(2)}, u32[]{:S(2)}) collective-permute-start(f32[8,128]{1,0:T(8,128)S(1)} %shard_map.61.first_ref.refs_0_), channel_id=1, source_target_pairs={{0,4},{2,6},{4,0},{6,2},{1,5},{3,7},{5,1},{7,3},{8,12},{10,14},{12... | collective-permute-start | bytes 12296 | tf_op jit(solution)/shard_map/ppermute | solution.py:54
  38.8 0.9 %collective-permute-start.5 = (f32[8,128]{1,0:T(8,128)S(1)}, f32[8,128]{1,0:T(8,128)S(1)}, u32[]{:S(2)}, u32[]{:S(2)}) collective-permute-start(f32[8,128]{1,0:T(8,128)S(1)} %shard_map.61.first_ref.refs_0_), channel_id=1, source_target_pairs={{0,6},{2,0},{4,2},{6,4},{1,7},{3,1},{5,3},{7,5},{8,14},{10,8},{12,... | collective-permute-start | bytes 12296 | tf_op jit(solution)/shard_map/ppermute | solution.py:54
  39.6 0.6 collective-permute-start.4
  40.2 0.1 collective-permute-done.6.fourth_ref.refs_3_
  40.3 1.3 %collective-permute-done.5.third_ref.refs_2_ = f32[8,128]{1,0:T(8,128)S(1)} collective-permute-done((f32[8,128]{1,0:T(8,128)S(1)}, f32[8,128]{1,0:T(8,128)S(1)}, u32[]{:S(2)}, u32[]{:S(2)}) %collective-permute-start.5) | collective-permute-done | bytes 4128 | tf_op jit(solution)/shard_map/ppermute | solution.py:54
  41.6 2.8 %collective-permute-done.4.second_ref.refs_1_ = f32[8,128]{1,0:T(8,128)S(1)} collective-permute-done((f32[8,128]{1,0:T(8,128)S(1)}, f32[8,128]{1,0:T(8,128)S(1)}, u32[]{:S(2)}, u32[]{:S(2)}) %collective-permute-start.4) | collective-permute-done | bytes 4128 | tf_op jit(solution)/shard_map/ppermute | solution.py:54
  44.4 5.5 %all-to-all-done.1.parts_ref = f32[32,32,256]{2,1,0:T(8,128)S(1)} async-done(((f32[32,32,256]{2,1,0:T(8,128)}), f32[32,32,256]{2,1,0:T(8,128)S(1)}, u32[]{:S(2)}, u32[]{:S(2)}) %all-to-all-start.1) | async-done | bytes 1048608 | tf_op jit(solution)/shard_map/all_to_all | solution.py:58
  49.9 0.1 shard_map.64.first_ref
  50.0 1.0 %collective-permute-start.11 = (f32[32,256]{1,0:T(8,128)S(1)}, f32[32,256]{1,0:T(8,128)S(1)}, u32[]{:S(2)}, u32[]{:S(2)}) collective-permute-start(f32[32,256]{1,0:T(8,128)S(1)} %shard_map.64.first_ref), channel_id=1, source_target_pairs={{0,32},{16,48},{32,0},{48,16},{1,33},{17,49},{33,1},{49,17},{2,34}... | collective-permute-start | bytes 98312 | tf_op jit(solution)/shard_map/ppermute | solution.py:54
  51.0 2.3 %collective-permute-start.10 = (f32[32,256]{1,0:T(8,128)S(1)}, f32[32,256]{1,0:T(8,128)S(1)}, u32[]{:S(2)}, u32[]{:S(2)}) collective-permute-start(f32[32,256]{1,0:T(8,128)S(1)} %shard_map.64.first_ref), channel_id=1, source_target_pairs={{0,48},{16,0},{32,16},{48,32},{1,49},{17,1},{33,17},{49,33},{2,50}... | collective-permute-start | bytes 98312 | tf_op jit(solution)/shard_map/ppermute | solution.py:54
  53.4 0.0 collective-permute-start.9
  53.4 2.9 %shard_map.62 = (f32[32,32]{1,0:T(8,128)S(1)}, f32[32,64]{1,0:T(8,128)S(1)}, f32[32,64]{1,0:T(8,128)S(1)}) custom-call(f32[8,128]{1,0:T(8,128)S(1)} %shard_map.61.first_ref.refs_0_, f32[8,128]{1,0:T(8,128)S(1)} %collective-permute-done.4.second_ref.refs_1_, f32[8,128]{1,0:T(8,128)S(1)} %collective-permute-done.5.third_ref.refs_2_, ...), custom_call_target="tpu_custom_call" | custom-call | flops 1048576 | bytes 12582912 | tf_op jit(solution)/shard_map/pallas_call | solution.py:282
  56.3 0.8 collective-permute-done.11.fourth_ref
  57.1 0.0 collective-permute-done.10.third_ref
  57.1 1.2 %collective-permute-done.9.second_ref = f32[32,256]{1,0:T(8,128)S(1)} collective-permute-done((f32[32,256]{1,0:T(8,128)S(1)}, f32[32,256]{1,0:T(8,128)S(1)}, u32[]{:S(2)}, u32[]{:S(2)}) %collective-permute-start.9) | collective-permute-done | bytes 32800 | tf_op jit(solution)/shard_map/ppermute | solution.py:54
  58.2 0.3 shard_map.65
  58.5 16.6 %all_to_all.16.blocks_ref = f32[32,32,256]{2,1,0:T(8,128)S(1)} all-to-all(f32[32,32,256]{2,1,0:T(8,128)S(1)} %shard_map.65), channel_id=1, replica_groups=mesh['x'=4,'v'=4,'w'=2,'y'=4,'c'=2] {'x','w','y'}, dimensions={0} | all-to-all | bytes 2097152 | tf_op jit(solution)/shard_map/all_to_all | solution.py:58
  75.2 0.1 shard_map.66.q_ref
  75.2 6.5 %collective-permute-start.12 = (f32[32,8192]{1,0:T(8,128)S(1)}, f32[32,8192]{1,0:T(8,128)S(1)}, u32[]{:S(2)}, u32[]{:S(2)}) collective-permute-start(f32[32,8192]{1,0:T(8,128)S(1)} %shard_map.66.q_ref), channel_id=1, source_target_pairs={{0,1},{1,0},{2,3},{3,2},{4,5},{5,4},{6,7},{7,6},{8,9},{9,8},{10,11... | collective-permute-start | bytes 3145736 | tf_op jit(solution)/shard_map/ppermute | solution.py:50
  81.8 0.1 collective-permute-start.7
  81.9 1.6 %shard_map.67 = (bf16[1,2,64,8192]{3,2,1,0:T(8,128)(2,1)}, f32[2,32,8192]{2,1,0:T(8,128)}, f32[2,32,64]{2,1,0:T(8,128)}) custom-call(s32[1]{0:T(128)} %bitcast.core_ref, f32[32,64]{1,0:T(8,128)S(1)} %get-tuple-element.28.ortho_ref, f32[32,8192]{1,0:T(8,128)S(1)} %shard_map.66.q_ref, bf16[64,8192]{1,0:T(8,128)(2,1)S(1)} %get-tuple-element.29.merged_ref), custom_call_target="tpu_custom_call" | custom-call | flops 33554432 | bytes 4194304 | tf_op jit(solution)/shard_map/pallas_call | solution.py:327
  83.5 0.6 collective-permute-done.7.ortho_ref
  84.1 0.0 collective-permute-done.12.q_ref
  84.1 1.6 %shard_map.68 = (bf16[1,2,64,8192]{3,2,1,0:T(8,128)(2,1)}, f32[2,32,8192]{2,1,0:T(8,128)}, f32[2,32,64]{2,1,0:T(8,128)}) custom-call(s32[1]{0:T(128)} %bitcast.core_ref, f32[32,64]{1,0:T(8,128)S(1)} %collective-permute-done.7.ortho_ref, f32[32,8192]{1,0:T(8,128)S(1)} %collective-permute-done.12.q_ref, ...), custom_call_target="tpu_custom_call", output_to_operand_aliasing={{0}: (4, {}), {1}: (5, {}), {2}: (6, {})} | custom-call | flops 33554432 | bytes 4194304 | tf_op jit(solution)/shard_map/pallas_call | solution.py:327
  (2 shorter events, 0.0 us)
Async XLA Ops:
  3.5 4.2 %collective-permute-start = (f32[32,64]{1,0:T(8,128)S(1)}, f32[32,64]{1,0:T(8,128)S(1)}, u32[]{:S(2)}, u32[]{:S(2)}) collective-permute-start(f32[32,64]{1,0:T(8,128)S(1)} %get-tuple-element.24), channel_id=1, source_target_pairs={{0,1},{1,0},{2,3},{3,2},{4,5},{5,4},{6,7},{7,6},{8,9},{9,8},{10,11... | collective-permute-start | bytes 24584 | tf_op jit(solution)/shard_map/ppermute | solution.py:50
  7.8 22.1 %collective-permute-start.8 = (f32[64,8192]{1,0:T(8,128)S(1)}, f32[64,8192]{1,0:T(8,128)S(1)}, u32[]{:S(2)}, u32[]{:S(2)}) collective-permute-start(f32[64,8192]{1,0:T(8,128)S(1)} %get-tuple-element.30), channel_id=1, source_target_pairs={{0,1},{1,0},{2,3},{3,2},{4,5},{5,4},{6,7},{7,6},{8,9},{9,8},{10,11... | collective-permute-start | bytes 6291464 | tf_op jit(solution)/shard_map/ppermute | solution.py:50
  8.1 4.1 %collective-permute-start.3 = (f32[32,128]{1,0:T(8,128)S(1)}, f32[32,128]{1,0:T(8,128)S(1)}, u32[]{:S(2)}, u32[]{:S(2)}) collective-permute-start(f32[32,128]{1,0:T(8,128)S(1)} %pad_maximum_fusion.first_ref), channel_id=1, source_target_pairs={{0,128},{64,192},{128,0},{192,64},{1,129},{65,193},{129,1},{193,65... | collective-permute-start | bytes 49160 | tf_op jit(solution)/shard_map/ppermute | solution.py:54
  9.2 3.1 %collective-permute-start.2 = (f32[32,128]{1,0:T(8,128)S(1)}, f32[32,128]{1,0:T(8,128)S(1)}, u32[]{:S(2)}, u32[]{:S(2)}) collective-permute-start(f32[32,128]{1,0:T(8,128)S(1)} %pad_maximum_fusion.first_ref), channel_id=1, source_target_pairs={{0,192},{64,0},{128,64},{192,128},{1,193},{65,1},{129,65},{193,129... | collective-permute-start | bytes 49160 | tf_op jit(solution)/shard_map/ppermute | solution.py:54
  10.0 3.8 %collective-permute-start.1 = (f32[32,128]{1,0:T(8,128)S(1)}, f32[32,128]{1,0:T(8,128)S(1)}, u32[]{:S(2)}, u32[]{:S(2)}) collective-permute-start(f32[32,128]{1,0:T(8,128)S(1)} %pad_maximum_fusion.first_ref), channel_id=1, source_target_pairs={{0,64},{64,128},{128,192},{192,0},{1,65},{65,129},{129,193},{193,1... | collective-permute-start | bytes 49160 | tf_op jit(solution)/shard_map/ppermute | solution.py:54
  31.2 18.7 %all-to-all-start.1 = ((f32[32,32,256]{2,1,0:T(8,128)}), f32[32,32,256]{2,1,0:T(8,128)S(1)}, u32[]{:S(2)}, u32[]{:S(2)}) async-start(f32[32,32,256]{2,1,0:T(8,128)} %shard_map.63), calls=%async_computation.1 | async-start | bytes 2097152 | tf_op jit(solution)/shard_map/all_to_all | solution.py:58
  36.0 4.3 %collective-permute-start.6 = (f32[8,128]{1,0:T(8,128)S(1)}, f32[8,128]{1,0:T(8,128)S(1)}, u32[]{:S(2)}, u32[]{:S(2)}) collective-permute-start(f32[8,128]{1,0:T(8,128)S(1)} %shard_map.61.first_ref.refs_0_), channel_id=1, source_target_pairs={{0,4},{2,6},{4,0},{6,2},{1,5},{3,7},{5,1},{7,3},{8,12},{10,14},{12... | collective-permute-start | bytes 12296 | tf_op jit(solution)/shard_map/ppermute | solution.py:54
  38.8 2.9 %collective-permute-start.5 = (f32[8,128]{1,0:T(8,128)S(1)}, f32[8,128]{1,0:T(8,128)S(1)}, u32[]{:S(2)}, u32[]{:S(2)}) collective-permute-start(f32[8,128]{1,0:T(8,128)S(1)} %shard_map.61.first_ref.refs_0_), channel_id=1, source_target_pairs={{0,6},{2,0},{4,2},{6,4},{1,7},{3,1},{5,3},{7,5},{8,14},{10,8},{12,... | collective-permute-start | bytes 12296 | tf_op jit(solution)/shard_map/ppermute | solution.py:54
  39.6 4.8 %collective-permute-start.4 = (f32[8,128]{1,0:T(8,128)S(1)}, f32[8,128]{1,0:T(8,128)S(1)}, u32[]{:S(2)}, u32[]{:S(2)}) collective-permute-start(f32[8,128]{1,0:T(8,128)S(1)} %shard_map.61.first_ref.refs_0_), channel_id=1, source_target_pairs={{0,2},{2,4},{4,6},{6,0},{1,3},{3,5},{5,7},{7,1},{8,10},{10,12},{12... | collective-permute-start | bytes 12296 | tf_op jit(solution)/shard_map/ppermute | solution.py:54
  50.0 7.0 %collective-permute-start.11 = (f32[32,256]{1,0:T(8,128)S(1)}, f32[32,256]{1,0:T(8,128)S(1)}, u32[]{:S(2)}, u32[]{:S(2)}) collective-permute-start(f32[32,256]{1,0:T(8,128)S(1)} %shard_map.64.first_ref), channel_id=1, source_target_pairs={{0,32},{16,48},{32,0},{48,16},{1,33},{17,49},{33,1},{49,17},{2,34}... | collective-permute-start | bytes 98312 | tf_op jit(solution)/shard_map/ppermute | solution.py:54
  51.0 6.0 %collective-permute-start.10 = (f32[32,256]{1,0:T(8,128)S(1)}, f32[32,256]{1,0:T(8,128)S(1)}, u32[]{:S(2)}, u32[]{:S(2)}) collective-permute-start(f32[32,256]{1,0:T(8,128)S(1)} %shard_map.64.first_ref), channel_id=1, source_target_pairs={{0,48},{16,0},{32,16},{48,32},{1,49},{17,1},{33,17},{49,33},{2,50}... | collective-permute-start | bytes 98312 | tf_op jit(solution)/shard_map/ppermute | solution.py:54
  53.4 4.9 %collective-permute-start.9 = (f32[32,256]{1,0:T(8,128)S(1)}, f32[32,256]{1,0:T(8,128)S(1)}, u32[]{:S(2)}, u32[]{:S(2)}) collective-permute-start(f32[32,256]{1,0:T(8,128)S(1)} %shard_map.64.first_ref), channel_id=1, source_target_pairs={{0,16},{16,32},{32,48},{48,0},{1,17},{17,33},{33,49},{49,1},{2,18}... | collective-permute-start | bytes 98312 | tf_op jit(solution)/shard_map/ppermute | solution.py:54
  75.2 8.9 %collective-permute-start.12 = (f32[32,8192]{1,0:T(8,128)S(1)}, f32[32,8192]{1,0:T(8,128)S(1)}, u32[]{:S(2)}, u32[]{:S(2)}) collective-permute-start(f32[32,8192]{1,0:T(8,128)S(1)} %shard_map.66.q_ref), channel_id=1, source_target_pairs={{0,1},{1,0},{2,3},{3,2},{4,5},{5,4},{6,7},{7,6},{8,9},{9,8},{10,11... | collective-permute-start | bytes 3145736 | tf_op jit(solution)/shard_map/ppermute | solution.py:50
  81.8 2.3 %collective-permute-start.7 = (f32[32,64]{1,0:T(8,128)S(1)}, f32[32,64]{1,0:T(8,128)S(1)}, u32[]{:S(2)}, u32[]{:S(2)}) collective-permute-start(f32[32,64]{1,0:T(8,128)S(1)} %get-tuple-element.27), channel_id=1, source_target_pairs={{0,1},{1,0},{2,3},{3,2},{4,5},{5,4},{6,7},{7,6},{8,9},{9,8},{10,11... | collective-permute-start | bytes 24584 | tf_op jit(solution)/shard_map/ppermute | solution.py:50

commit v10 on v9

--- a/solution.py
+++ b/solution.py
@@ -355,12 +355,12 @@
     gram = packed_gram(summed)
     grams = [gram] + shifts(gram, "y", NY)
 
-    half = exchange(right(summed, merged, received), ("x", "w", "y"))
+    half = exchange(right(summed, merged, received), ("w", "y", "x"))
     part = sum_parts(half, after=grams)
     inverse, ortho, ortho_theirs = factors(grams, summed)
     parts = [part] + shifts(part, "v", NV)
 
-    q_own = spread(exchange(middle(parts, inverse), ("x", "w", "y")))
+    q_own = spread(exchange(middle(parts, inverse), ("w", "y", "x")))
     q_other = swap(q_own)
     first = tail(own, ortho, q_own, merged)
     ortho_other, first = lax.optimization_barrier((swap(ortho_theirs), first))

time: 86 us -> 85.4 us (level)
  waiting for transfers between devices: 16.3 us -> 14.4 us
  blocking collectives: 32.7 us -> 33.6 us
    all_to_all x1, waiting for transfers between devices: 5.54 us -> 4.48 us  [exchange(): return lax.all_to_all(a, axes, 0, 0)]
    all_to_all x2, blocking collectives: 32.7 us -> 33.6 us  [exchange(): return lax.all_to_all(a, axes, 0, 0)]
    ppermute x9, waiting for transfers between devices: 9.32 us -> 8.45 us  [shifts(): lax.ppermute(a, axis, [(i, (i + s) % size) for i in range(size)])]
where the time goes in v10:
time: 85.4 us; the launch traced here: 85.1 us
  blocking collectives  33.6 us (39%)
  starting transfers between devices  25.4 us (30%)
  waiting for transfers between devices  14.4 us (17%)
  Pallas kernels  11 us (13%)
    all_to_all x2, blocking collectives, exchange(): return lax.all_to_all(a, axes, 0, 0)  33.6 us
    ppermute x4, starting transfers between devices, swap(): return lax.ppermute(a, 'c', [(0, 1), (1, 0)])  10.6 us
    ppermute x9, starting transfers between devices, shifts(): lax.ppermute(a, axis, [(i, (i + s) % size) for i in range(size)])  10.2 us
    ppermute x9, waiting for transfers between devices, shifts(): lax.ppermute(a, axis, [(i, (i + s) % size) for i in range(size)])  8.45 us
    all_to_all x1, starting transfers between devices, exchange(): return lax.all_to_all(a, axes, 0, 0)  4.59 us
    all_to_all x1, waiting for transfers between devices, exchange(): return lax.all_to_all(a, axes, 0, 0)  4.48 us
    pallas_call x2, Pallas kernels, tail(): pl.pallas_call(functools.partial(tail_kernel, bool(before)), in_specs=[IN...  3.23 us
    pallas_call x1, Pallas kernels, factors(): pl.pallas_call(factor_kernel, in_specs=[IN_VMEM] * (NY + 1), out_specs=[I...  2.89 us
  transfers between devices with their start and end apart: 14, of which 10 were waited for; matrix products, arithmetic and copies ran while one was open for 0% of the time, Pallas kernels for 6%

profile of v10, /device:TPU:1, one launch (start us, length us, event | category | flops | bytes accessed | tf_op | source)
XLA Modules:
  0.0 85.1 jit_solution(14757129062662915775)
XLA Ops:
  0.6 2.9 %shard_map.58 = (bf16[64,8192]{1,0:T(8,128)(2,1)S(1)}, bf16[64,8192]{1,0:T(8,128)(2,1)S(1)}, f32[64,8192]{1,0:T(8,128)S(1)}, f32[32,64]{1,0:T(8,128)S(1)}, f32[32,64]{1,0:T(8,128)S(1)}) custom-call(s32[1]{0:T(128)} %bitcast.core_ref, bf16[1,2,64,8192]{3,2,1,0:T(8,128)(2,1)} %grads_hbm.1, bf16[1,2,64,8192]{3,2,1,0:T(8,128)(2,1)} %errors_hbm.1, ...), custom_call_target="tpu_custom_call" | custom-call | flops 134217728 | bytes 9437184 | tf_op jit(solution)/shard_map/pallas_call | solution.py:119
  3.5 3.3 %collective-permute-start = (f32[32,64]{1,0:T(8,128)S(1)}, f32[32,64]{1,0:T(8,128)S(1)}, u32[]{:S(2)}, u32[]{:S(2)}) collective-permute-start(f32[32,64]{1,0:T(8,128)S(1)} %get-tuple-element.24), channel_id=1, source_target_pairs={{0,1},{1,0},{2,3},{3,2},{4,5},{5,4},{6,7},{7,6},{8,9},{9,8},{10,11... | collective-permute-start | bytes 24584 | tf_op jit(solution)/shard_map/ppermute | solution.py:50
  6.9 0.8 collective-permute-done
  7.7 0.1 pad_maximum_fusion.first_ref
  7.8 0.4 collective-permute-start.8
  8.1 1.0 %collective-permute-start.3 = (f32[32,128]{1,0:T(8,128)S(1)}, f32[32,128]{1,0:T(8,128)S(1)}, u32[]{:S(2)}, u32[]{:S(2)}) collective-permute-start(f32[32,128]{1,0:T(8,128)S(1)} %pad_maximum_fusion.first_ref), channel_id=1, source_target_pairs={{0,128},{64,192},{128,0},{192,64},{1,129},{65,193},{129,1},{193,65... | collective-permute-start | bytes 49160 | tf_op jit(solution)/shard_map/ppermute | solution.py:54
  9.2 0.9 %collective-permute-start.2 = (f32[32,128]{1,0:T(8,128)S(1)}, f32[32,128]{1,0:T(8,128)S(1)}, u32[]{:S(2)}, u32[]{:S(2)}) collective-permute-start(f32[32,128]{1,0:T(8,128)S(1)} %pad_maximum_fusion.first_ref), channel_id=1, source_target_pairs={{0,192},{64,0},{128,64},{192,128},{1,193},{65,1},{129,65},{193,129... | collective-permute-start | bytes 49160 | tf_op jit(solution)/shard_map/ppermute | solution.py:54
  10.0 0.6 collective-permute-start.1
  10.6 1.6 %collective-permute-done.3.fourth_ref = f32[32,128]{1,0:T(8,128)S(1)} collective-permute-done((f32[32,128]{1,0:T(8,128)S(1)}, f32[32,128]{1,0:T(8,128)S(1)}, u32[]{:S(2)}, u32[]{:S(2)}) %collective-permute-start.3) | collective-permute-done | bytes 16416 | tf_op jit(solution)/shard_map/ppermute | solution.py:54
  12.2 0.0 collective-permute-done.2.third_ref
  12.2 1.6 %collective-permute-done.1.second_ref = f32[32,128]{1,0:T(8,128)S(1)} collective-permute-done((f32[32,128]{1,0:T(8,128)S(1)}, f32[32,128]{1,0:T(8,128)S(1)}, u32[]{:S(2)}, u32[]{:S(2)}) %collective-permute-start.1) | collective-permute-done | bytes 16416 | tf_op jit(solution)/shard_map/ppermute | solution.py:54
  13.8 16.0 %all_to_all.15.parts_ref = f32[8,32,128]{2,1,0:T(8,128)S(1)} all-to-all(f32[8,32,128]{2,1,0:T(8,128)S(1)} %shard_map.59), channel_id=1, replica_groups=mesh['x'=4,'v'=4,'w'=2,'y'=4,'c'=2] {'v','w'}, dimensions={0} | all-to-all | bytes 262144 | tf_op jit(solution)/shard_map/all_to_all | solution.py:58
  29.9 0.0 collective-permute-done.8.received_ref
  29.9 1.3 %shard_map.63 = f32[32,32,256]{2,1,0:T(8,128)} custom-call(f32[32,128]{1,0:T(8,128)S(1)} %shard_map.60.summed_ref, bf16[64,8192]{1,0:T(8,128)(2,1)S(1)} %get-tuple-element.29.merged_ref, f32[64,8192]{1,0:T(8,128)S(1)} %collective-permute-done.8.received_ref), custom_call_target="tpu_custom_call" | custom-call | flops 201326592 | bytes 4194304 | tf_op jit(solution)/shard_map/pallas_call | solution.py:225
  31.2 4.6 %all-to-all-start.1 = ((f32[32,32,256]{2,1,0:T(8,128)}), f32[32,32,256]{2,1,0:T(8,128)S(1)}, u32[]{:S(2)}, u32[]{:S(2)}) async-start(f32[32,32,256]{2,1,0:T(8,128)} %shard_map.63), calls=%async_computation.1 | async-start | bytes 2097152 | tf_op jit(solution)/shard_map/all_to_all | solution.py:58
  35.8 0.2 shard_map.61.first_ref.refs_0_
  36.0 2.8 %collective-permute-start.6 = (f32[8,128]{1,0:T(8,128)S(1)}, f32[8,128]{1,0:T(8,128)S(1)}, u32[]{:S(2)}, u32[]{:S(2)}) collective-permute-start(f32[8,128]{1,0:T(8,128)S(1)} %shard_map.61.first_ref.refs_0_), channel_id=1, source_target_pairs={{0,4},{2,6},{4,0},{6,2},{1,5},{3,7},{5,1},{7,3},{8,12},{10,14},{12... | collective-permute-start | bytes 12296 | tf_op jit(solution)/shard_map/ppermute | solution.py:54
  38.8 0.9 %collective-permute-start.5 = (f32[8,128]{1,0:T(8,128)S(1)}, f32[8,128]{1,0:T(8,128)S(1)}, u32[]{:S(2)}, u32[]{:S(2)}) collective-permute-start(f32[8,128]{1,0:T(8,128)S(1)} %shard_map.61.first_ref.refs_0_), channel_id=1, source_target_pairs={{0,6},{2,0},{4,2},{6,4},{1,7},{3,1},{5,3},{7,5},{8,14},{10,8},{12,... | collective-permute-start | bytes 12296 | tf_op jit(solution)/shard_map/ppermute | solution.py:54
  39.6 0.6 collective-permute-start.4
  40.2 0.1 collective-permute-done.6.fourth_ref.refs_3_
  40.4 1.2 %collective-permute-done.5.third_ref.refs_2_ = f32[8,128]{1,0:T(8,128)S(1)} collective-permute-done((f32[8,128]{1,0:T(8,128)S(1)}, f32[8,128]{1,0:T(8,128)S(1)}, u32[]{:S(2)}, u32[]{:S(2)}) %collective-permute-start.5) | collective-permute-done | bytes 4128 | tf_op jit(solution)/shard_map/ppermute | solution.py:54
  41.6 2.1 %collective-permute-done.4.second_ref.refs_1_ = f32[8,128]{1,0:T(8,128)S(1)} collective-permute-done((f32[8,128]{1,0:T(8,128)S(1)}, f32[8,128]{1,0:T(8,128)S(1)}, u32[]{:S(2)}, u32[]{:S(2)}) %collective-permute-start.4) | collective-permute-done | bytes 4128 | tf_op jit(solution)/shard_map/ppermute | solution.py:54
  43.7 4.5 %all-to-all-done.1.parts_ref = f32[32,32,256]{2,1,0:T(8,128)S(1)} async-done(((f32[32,32,256]{2,1,0:T(8,128)}), f32[32,32,256]{2,1,0:T(8,128)S(1)}, u32[]{:S(2)}, u32[]{:S(2)}) %all-to-all-start.1) | async-done | bytes 1048608 | tf_op jit(solution)/shard_map/all_to_all | solution.py:58
  48.2 0.1 shard_map.64.first_ref
  48.3 1.2 %collective-permute-start.11 = (f32[32,256]{1,0:T(8,128)S(1)}, f32[32,256]{1,0:T(8,128)S(1)}, u32[]{:S(2)}, u32[]{:S(2)}) collective-permute-start(f32[32,256]{1,0:T(8,128)S(1)} %shard_map.64.first_ref), channel_id=1, source_target_pairs={{0,32},{16,48},{32,0},{48,16},{1,33},{17,49},{33,1},{49,17},{2,34}... | collective-permute-start | bytes 98312 | tf_op jit(solution)/shard_map/ppermute | solution.py:54
  49.4 2.1 %collective-permute-start.10 = (f32[32,256]{1,0:T(8,128)S(1)}, f32[32,256]{1,0:T(8,128)S(1)}, u32[]{:S(2)}, u32[]{:S(2)}) collective-permute-start(f32[32,256]{1,0:T(8,128)S(1)} %shard_map.64.first_ref), channel_id=1, source_target_pairs={{0,48},{16,0},{32,16},{48,32},{1,49},{17,1},{33,17},{49,33},{2,50}... | collective-permute-start | bytes 98312 | tf_op jit(solution)/shard_map/ppermute | solution.py:54
  51.6 0.2 collective-permute-start.9
  51.8 2.9 %shard_map.62 = (f32[32,32]{1,0:T(8,128)S(1)}, f32[32,64]{1,0:T(8,128)S(1)}, f32[32,64]{1,0:T(8,128)S(1)}) custom-call(f32[8,128]{1,0:T(8,128)S(1)} %shard_map.61.first_ref.refs_0_, f32[8,128]{1,0:T(8,128)S(1)} %collective-permute-done.4.second_ref.refs_1_, f32[8,128]{1,0:T(8,128)S(1)} %collective-permute-done.5.third_ref.refs_2_, ...), custom_call_target="tpu_custom_call" | custom-call | flops 1048576 | bytes 12582912 | tf_op jit(solution)/shard_map/pallas_call | solution.py:282
  54.7 0.3 collective-permute-done.11.fourth_ref
  55.0 0.0 collective-permute-done.10.third_ref
  55.0 1.4 %collective-permute-done.9.second_ref = f32[32,256]{1,0:T(8,128)S(1)} collective-permute-done((f32[32,256]{1,0:T(8,128)S(1)}, f32[32,256]{1,0:T(8,128)S(1)}, u32[]{:S(2)}, u32[]{:S(2)}) %collective-permute-start.9) | collective-permute-done | bytes 32800 | tf_op jit(solution)/shard_map/ppermute | solution.py:54
  56.5 0.3 shard_map.65
  56.7 17.6 %all_to_all.16.blocks_ref = f32[32,32,256]{2,1,0:T(8,128)S(1)} all-to-all(f32[32,32,256]{2,1,0:T(8,128)S(1)} %shard_map.65), channel_id=1, replica_groups=mesh['x'=4,'v'=4,'w'=2,'y'=4,'c'=2] {'w','y','x'}, dimensions={0} | all-to-all | bytes 2097152 | tf_op jit(solution)/shard_map/all_to_all | solution.py:58
  74.3 0.1 shard_map.66.q_ref
  74.4 6.8 %collective-permute-start.12 = (f32[32,8192]{1,0:T(8,128)S(1)}, f32[32,8192]{1,0:T(8,128)S(1)}, u32[]{:S(2)}, u32[]{:S(2)}) collective-permute-start(f32[32,8192]{1,0:T(8,128)S(1)} %shard_map.66.q_ref), channel_id=1, source_target_pairs={{0,1},{1,0},{2,3},{3,2},{4,5},{5,4},{6,7},{7,6},{8,9},{9,8},{10,11... | collective-permute-start | bytes 3145736 | tf_op jit(solution)/shard_map/ppermute | solution.py:50
  81.2 0.1 collective-permute-start.7
  81.3 1.6 %shard_map.67 = (bf16[1,2,64,8192]{3,2,1,0:T(8,128)(2,1)}, f32[2,32,8192]{2,1,0:T(8,128)}, f32[2,32,64]{2,1,0:T(8,128)}) custom-call(s32[1]{0:T(128)} %bitcast.core_ref, f32[32,64]{1,0:T(8,128)S(1)} %get-tuple-element.28.ortho_ref, f32[32,8192]{1,0:T(8,128)S(1)} %shard_map.66.q_ref, bf16[64,8192]{1,0:T(8,128)(2,1)S(1)} %get-tuple-element.29.merged_ref), custom_call_target="tpu_custom_call" | custom-call | flops 33554432 | bytes 4194304 | tf_op jit(solution)/shard_map/pallas_call | solution.py:327
  82.9 0.6 collective-permute-done.7.ortho_ref
  83.5 0.0 collective-permute-done.12.q_ref
  83.5 1.6 %shard_map.68 = (bf16[1,2,64,8192]{3,2,1,0:T(8,128)(2,1)}, f32[2,32,8192]{2,1,0:T(8,128)}, f32[2,32,64]{2,1,0:T(8,128)}) custom-call(s32[1]{0:T(128)} %bitcast.core_ref, f32[32,64]{1,0:T(8,128)S(1)} %collective-permute-done.7.ortho_ref, f32[32,8192]{1,0:T(8,128)S(1)} %collective-permute-done.12.q_ref, ...), custom_call_target="tpu_custom_call", output_to_operand_aliasing={{0}: (4, {}), {1}: (5, {}), {2}: (6, {})} | custom-call | flops 33554432 | bytes 4194304 | tf_op jit(solution)/shard_map/pallas_call | solution.py:327
  (2 shorter events, 0.0 us)
Async XLA Ops:
  3.5 4.2 %collective-permute-start = (f32[32,64]{1,0:T(8,128)S(1)}, f32[32,64]{1,0:T(8,128)S(1)}, u32[]{:S(2)}, u32[]{:S(2)}) collective-permute-start(f32[32,64]{1,0:T(8,128)S(1)} %get-tuple-element.24), channel_id=1, source_target_pairs={{0,1},{1,0},{2,3},{3,2},{4,5},{5,4},{6,7},{7,6},{8,9},{9,8},{10,11... | collective-permute-start | bytes 24584 | tf_op jit(solution)/shard_map/ppermute | solution.py:50
  7.8 22.1 %collective-permute-start.8 = (f32[64,8192]{1,0:T(8,128)S(1)}, f32[64,8192]{1,0:T(8,128)S(1)}, u32[]{:S(2)}, u32[]{:S(2)}) collective-permute-start(f32[64,8192]{1,0:T(8,128)S(1)} %get-tuple-element.30), channel_id=1, source_target_pairs={{0,1},{1,0},{2,3},{3,2},{4,5},{5,4},{6,7},{7,6},{8,9},{9,8},{10,11... | collective-permute-start | bytes 6291464 | tf_op jit(solution)/shard_map/ppermute | solution.py:50
  8.1 4.1 %collective-permute-start.3 = (f32[32,128]{1,0:T(8,128)S(1)}, f32[32,128]{1,0:T(8,128)S(1)}, u32[]{:S(2)}, u32[]{:S(2)}) collective-permute-start(f32[32,128]{1,0:T(8,128)S(1)} %pad_maximum_fusion.first_ref), channel_id=1, source_target_pairs={{0,128},{64,192},{128,0},{192,64},{1,129},{65,193},{129,1},{193,65... | collective-permute-start | bytes 49160 | tf_op jit(solution)/shard_map/ppermute | solution.py:54
  9.2 3.1 %collective-permute-start.2 = (f32[32,128]{1,0:T(8,128)S(1)}, f32[32,128]{1,0:T(8,128)S(1)}, u32[]{:S(2)}, u32[]{:S(2)}) collective-permute-start(f32[32,128]{1,0:T(8,128)S(1)} %pad_maximum_fusion.first_ref), channel_id=1, source_target_pairs={{0,192},{64,0},{128,64},{192,128},{1,193},{65,1},{129,65},{193,129... | collective-permute-start | bytes 49160 | tf_op jit(solution)/shard_map/ppermute | solution.py:54
  10.0 3.8 %collective-permute-start.1 = (f32[32,128]{1,0:T(8,128)S(1)}, f32[32,128]{1,0:T(8,128)S(1)}, u32[]{:S(2)}, u32[]{:S(2)}) collective-permute-start(f32[32,128]{1,0:T(8,128)S(1)} %pad_maximum_fusion.first_ref), channel_id=1, source_target_pairs={{0,64},{64,128},{128,192},{192,0},{1,65},{65,129},{129,193},{193,1... | collective-permute-start | bytes 49160 | tf_op jit(solution)/shard_map/ppermute | solution.py:54
  31.2 17.0 %all-to-all-start.1 = ((f32[32,32,256]{2,1,0:T(8,128)}), f32[32,32,256]{2,1,0:T(8,128)S(1)}, u32[]{:S(2)}, u32[]{:S(2)}) async-start(f32[32,32,256]{2,1,0:T(8,128)} %shard_map.63), calls=%async_computation.1 | async-start | bytes 2097152 | tf_op jit(solution)/shard_map/all_to_all | solution.py:58
  36.0 4.4 %collective-permute-start.6 = (f32[8,128]{1,0:T(8,128)S(1)}, f32[8,128]{1,0:T(8,128)S(1)}, u32[]{:S(2)}, u32[]{:S(2)}) collective-permute-start(f32[8,128]{1,0:T(8,128)S(1)} %shard_map.61.first_ref.refs_0_), channel_id=1, source_target_pairs={{0,4},{2,6},{4,0},{6,2},{1,5},{3,7},{5,1},{7,3},{8,12},{10,14},{12... | collective-permute-start | bytes 12296 | tf_op jit(solution)/shard_map/ppermute | solution.py:54
  38.8 2.8 %collective-permute-start.5 = (f32[8,128]{1,0:T(8,128)S(1)}, f32[8,128]{1,0:T(8,128)S(1)}, u32[]{:S(2)}, u32[]{:S(2)}) collective-permute-start(f32[8,128]{1,0:T(8,128)S(1)} %shard_map.61.first_ref.refs_0_), channel_id=1, source_target_pairs={{0,6},{2,0},{4,2},{6,4},{1,7},{3,1},{5,3},{7,5},{8,14},{10,8},{12,... | collective-permute-start | bytes 12296 | tf_op jit(solution)/shard_map/ppermute | solution.py:54
  39.6 4.1 %collective-permute-start.4 = (f32[8,128]{1,0:T(8,128)S(1)}, f32[8,128]{1,0:T(8,128)S(1)}, u32[]{:S(2)}, u32[]{:S(2)}) collective-permute-start(f32[8,128]{1,0:T(8,128)S(1)} %shard_map.61.first_ref.refs_0_), channel_id=1, source_target_pairs={{0,2},{2,4},{4,6},{6,0},{1,3},{3,5},{5,7},{7,1},{8,10},{10,12},{12... | collective-permute-start | bytes 12296 | tf_op jit(solution)/shard_map/ppermute | solution.py:54
  48.3 6.8 %collective-permute-start.11 = (f32[32,256]{1,0:T(8,128)S(1)}, f32[32,256]{1,0:T(8,128)S(1)}, u32[]{:S(2)}, u32[]{:S(2)}) collective-permute-start(f32[32,256]{1,0:T(8,128)S(1)} %shard_map.64.first_ref), channel_id=1, source_target_pairs={{0,32},{16,48},{32,0},{48,16},{1,33},{17,49},{33,1},{49,17},{2,34}... | collective-permute-start | bytes 98312 | tf_op jit(solution)/shard_map/ppermute | solution.py:54
  49.4 5.6 %collective-permute-start.10 = (f32[32,256]{1,0:T(8,128)S(1)}, f32[32,256]{1,0:T(8,128)S(1)}, u32[]{:S(2)}, u32[]{:S(2)}) collective-permute-start(f32[32,256]{1,0:T(8,128)S(1)} %shard_map.64.first_ref), channel_id=1, source_target_pairs={{0,48},{16,0},{32,16},{48,32},{1,49},{17,1},{33,17},{49,33},{2,50}... | collective-permute-start | bytes 98312 | tf_op jit(solution)/shard_map/ppermute | solution.py:54
  51.6 4.9 %collective-permute-start.9 = (f32[32,256]{1,0:T(8,128)S(1)}, f32[32,256]{1,0:T(8,128)S(1)}, u32[]{:S(2)}, u32[]{:S(2)}) collective-permute-start(f32[32,256]{1,0:T(8,128)S(1)} %shard_map.64.first_ref), channel_id=1, source_target_pairs={{0,16},{16,32},{32,48},{48,0},{1,17},{17,33},{33,49},{49,1},{2,18}... | collective-permute-start | bytes 98312 | tf_op jit(solution)/shard_map/ppermute | solution.py:54
  74.4 9.1 %collective-permute-start.12 = (f32[32,8192]{1,0:T(8,128)S(1)}, f32[32,8192]{1,0:T(8,128)S(1)}, u32[]{:S(2)}, u32[]{:S(2)}) collective-permute-start(f32[32,8192]{1,0:T(8,128)S(1)} %shard_map.66.q_ref), channel_id=1, source_target_pairs={{0,1},{1,0},{2,3},{3,2},{4,5},{5,4},{6,7},{7,6},{8,9},{9,8},{10,11... | collective-permute-start | bytes 3145736 | tf_op jit(solution)/shard_map/ppermute | solution.py:50
  81.2 2.3 %collective-permute-start.7 = (f32[32,64]{1,0:T(8,128)S(1)}, f32[32,64]{1,0:T(8,128)S(1)}, u32[]{:S(2)}, u32[]{:S(2)}) collective-permute-start(f32[32,64]{1,0:T(8,128)S(1)} %get-tuple-element.27), channel_id=1, source_target_pairs={{0,1},{1,0},{2,3},{3,2},{4,5},{5,4},{6,7},{7,6},{8,9},{9,8},{10,11... | collective-permute-start | bytes 24584 | tf_op jit(solution)/shard_map/ppermute | solution.py:50

commit v11 on v10

--- a/solution.py
+++ b/solution.py
@@ -50,8 +50,8 @@
     return lax.ppermute(a, "c", [(0, 1), (1, 0)])
 
 
-def shifts(a, axis, size):
-    return [lax.ppermute(a, axis, [(i, (i + s) % size) for i in range(size)]) for s in (1, 3, 2)[: size - 1]]
+def shifts(a, axis, size, order=(1, 3, 2)):
+    return [lax.ppermute(a, axis, [(i, (i + s) % size) for i in range(size)]) for s in order[: size - 1]]
 
 
 def exchange(a, axes):
@@ -358,7 +358,7 @@
     half = exchange(right(summed, merged, received), ("w", "y", "x"))
     part = sum_parts(half, after=grams)
     inverse, ortho, ortho_theirs = factors(grams, summed)
-    parts = [part] + shifts(part, "v", NV)
+    parts = [part] + shifts(part, "v", NV, (3, 1, 2))
 
     q_own = spread(exchange(middle(parts, inverse), ("w", "y", "x")))
     q_other = swap(q_own)

time: 85.4 us -> 84.7 us (level)
  waiting for transfers between devices: 14.4 us -> 12.6 us
    ppermute x9, waiting for transfers between devices: 8.45 us -> 6.71 us  [shifts(): lax.ppermute(a, axis, [(i, (i + s) % size) for i in range(size)])]
    ppermute x9, starting transfers between devices: 10.2 us -> 11.4 us  [shifts(): lax.ppermute(a, axis, [(i, (i + s) % size) for i in range(size)])]
  transfers between devices with their start and end apart: 14 -> 14, of which waited for: 10 -> 8; matrix products, arithmetic and copies ran while one was open for 0% -> 0% of each run, Pallas kernels for 6% -> 6%
where the time goes in v11:
time: 84.7 us; the launch traced here: 84.4 us
  blocking collectives  34.1 us (40%)
  starting transfers between devices  25.9 us (31%)
  waiting for transfers between devices  12.6 us (15%)
  Pallas kernels  10.9 us (13%)
    all_to_all x2, blocking collectives, exchange(): return lax.all_to_all(a, axes, 0, 0)  34.1 us
    ppermute x9, starting transfers between devices, shifts(): lax.ppermute(a, axis, [(i, (i + s) % size) for i in range(size)])  11.4 us
    ppermute x4, starting transfers between devices, swap(): return lax.ppermute(a, 'c', [(0, 1), (1, 0)])  9.87 us
    ppermute x9, waiting for transfers between devices, shifts(): lax.ppermute(a, axis, [(i, (i + s) % size) for i in range(size)])  6.71 us
    all_to_all x1, starting transfers between devices, exchange(): return lax.all_to_all(a, axes, 0, 0)  4.59 us
    all_to_all x1, waiting for transfers between devices, exchange(): return lax.all_to_all(a, axes, 0, 0)  4.48 us
    pallas_call x2, Pallas kernels, tail(): pl.pallas_call(functools.partial(tail_kernel, bool(before)), in_specs=[IN...  3.21 us
    pallas_call x1, Pallas kernels, factors(): pl.pallas_call(factor_kernel, in_specs=[IN_VMEM] * (NY + 1), out_specs=[I...  2.89 us
  transfers between devices with their start and end apart: 14, of which 8 were waited for; matrix products, arithmetic and copies ran while one was open for 0% of the time, Pallas kernels for 6%

profile of v11, /device:TPU:1, one launch (start us, length us, event | category | flops | bytes accessed | tf_op | source)
XLA Modules:
  0.0 84.4 jit_solution(14110317954914579329)
XLA Ops:
  0.6 2.9 %shard_map.58 = (bf16[64,8192]{1,0:T(8,128)(2,1)S(1)}, bf16[64,8192]{1,0:T(8,128)(2,1)S(1)}, f32[64,8192]{1,0:T(8,128)S(1)}, f32[32,64]{1,0:T(8,128)S(1)}, f32[32,64]{1,0:T(8,128)S(1)}) custom-call(s32[1]{0:T(128)} %bitcast.core_ref, bf16[1,2,64,8192]{3,2,1,0:T(8,128)(2,1)} %grads_hbm.1, bf16[1,2,64,8192]{3,2,1,0:T(8,128)(2,1)} %errors_hbm.1, ...), custom_call_target="tpu_custom_call" | custom-call | flops 134217728 | bytes 9437184 | tf_op jit(solution)/shard_map/pallas_call | solution.py:119
  3.5 3.3 %collective-permute-start = (f32[32,64]{1,0:T(8,128)S(1)}, f32[32,64]{1,0:T(8,128)S(1)}, u32[]{:S(2)}, u32[]{:S(2)}) collective-permute-start(f32[32,64]{1,0:T(8,128)S(1)} %get-tuple-element.24), channel_id=1, source_target_pairs={{0,1},{1,0},{2,3},{3,2},{4,5},{5,4},{6,7},{7,6},{8,9},{9,8},{10,11... | collective-permute-start | bytes 24584 | tf_op jit(solution)/shard_map/ppermute | solution.py:50
  6.9 0.8 collective-permute-done
  7.7 0.1 pad_maximum_fusion.first_ref
  7.8 0.4 collective-permute-start.8
  8.1 1.0 %collective-permute-start.3 = (f32[32,128]{1,0:T(8,128)S(1)}, f32[32,128]{1,0:T(8,128)S(1)}, u32[]{:S(2)}, u32[]{:S(2)}) collective-permute-start(f32[32,128]{1,0:T(8,128)S(1)} %pad_maximum_fusion.first_ref), channel_id=1, source_target_pairs={{0,128},{64,192},{128,0},{192,64},{1,129},{65,193},{129,1},{193,65... | collective-permute-start | bytes 49160 | tf_op jit(solution)/shard_map/ppermute | solution.py:54
  9.2 0.9 %collective-permute-start.2 = (f32[32,128]{1,0:T(8,128)S(1)}, f32[32,128]{1,0:T(8,128)S(1)}, u32[]{:S(2)}, u32[]{:S(2)}) collective-permute-start(f32[32,128]{1,0:T(8,128)S(1)} %pad_maximum_fusion.first_ref), channel_id=1, source_target_pairs={{0,192},{64,0},{128,64},{192,128},{1,193},{65,1},{129,65},{193,129... | collective-permute-start | bytes 49160 | tf_op jit(solution)/shard_map/ppermute | solution.py:54
  10.0 0.6 collective-permute-start.1
  10.6 1.6 %collective-permute-done.3.fourth_ref = f32[32,128]{1,0:T(8,128)S(1)} collective-permute-done((f32[32,128]{1,0:T(8,128)S(1)}, f32[32,128]{1,0:T(8,128)S(1)}, u32[]{:S(2)}, u32[]{:S(2)}) %collective-permute-start.3) | collective-permute-done | bytes 16416 | tf_op jit(solution)/shard_map/ppermute | solution.py:54
  12.2 0.0 collective-permute-done.2.third_ref
  12.2 1.6 %collective-permute-done.1.second_ref = f32[32,128]{1,0:T(8,128)S(1)} collective-permute-done((f32[32,128]{1,0:T(8,128)S(1)}, f32[32,128]{1,0:T(8,128)S(1)}, u32[]{:S(2)}, u32[]{:S(2)}) %collective-permute-start.1) | collective-permute-done | bytes 16416 | tf_op jit(solution)/shard_map/ppermute | solution.py:54
  13.8 16.0 %all_to_all.15.parts_ref = f32[8,32,128]{2,1,0:T(8,128)S(1)} all-to-all(f32[8,32,128]{2,1,0:T(8,128)S(1)} %shard_map.59), channel_id=1, replica_groups=mesh['x'=4,'v'=4,'w'=2,'y'=4,'c'=2] {'v','w'}, dimensions={0} | all-to-all | bytes 262144 | tf_op jit(solution)/shard_map/all_to_all | solution.py:58
  29.9 0.0 collective-permute-done.8.received_ref
  29.9 1.3 %shard_map.63 = f32[32,32,256]{2,1,0:T(8,128)} custom-call(f32[32,128]{1,0:T(8,128)S(1)} %shard_map.60.summed_ref, bf16[64,8192]{1,0:T(8,128)(2,1)S(1)} %get-tuple-element.29.merged_ref, f32[64,8192]{1,0:T(8,128)S(1)} %collective-permute-done.8.received_ref), custom_call_target="tpu_custom_call" | custom-call | flops 201326592 | bytes 4194304 | tf_op jit(solution)/shard_map/pallas_call | solution.py:225
  31.2 4.6 %all-to-all-start.1 = ((f32[32,32,256]{2,1,0:T(8,128)}), f32[32,32,256]{2,1,0:T(8,128)S(1)}, u32[]{:S(2)}, u32[]{:S(2)}) async-start(f32[32,32,256]{2,1,0:T(8,128)} %shard_map.63), calls=%async_computation.1 | async-start | bytes 2097152 | tf_op jit(solution)/shard_map/all_to_all | solution.py:58
  35.8 0.2 shard_map.61.first_ref.refs_0_
  36.0 2.8 %collective-permute-start.6 = (f32[8,128]{1,0:T(8,128)S(1)}, f32[8,128]{1,0:T(8,128)S(1)}, u32[]{:S(2)}, u32[]{:S(2)}) collective-permute-start(f32[8,128]{1,0:T(8,128)S(1)} %shard_map.61.first_ref.refs_0_), channel_id=1, source_target_pairs={{0,4},{2,6},{4,0},{6,2},{1,5},{3,7},{5,1},{7,3},{8,12},{10,14},{12... | collective-permute-start | bytes 12296 | tf_op jit(solution)/shard_map/ppermute | solution.py:54
  38.8 0.9 %collective-permute-start.5 = (f32[8,128]{1,0:T(8,128)S(1)}, f32[8,128]{1,0:T(8,128)S(1)}, u32[]{:S(2)}, u32[]{:S(2)}) collective-permute-start(f32[8,128]{1,0:T(8,128)S(1)} %shard_map.61.first_ref.refs_0_), channel_id=1, source_target_pairs={{0,6},{2,0},{4,2},{6,4},{1,7},{3,1},{5,3},{7,5},{8,14},{10,8},{12,... | collective-permute-start | bytes 12296 | tf_op jit(solution)/shard_map/ppermute | solution.py:54
  39.6 0.6 collective-permute-start.4
  40.2 0.1 collective-permute-done.6.fourth_ref.refs_3_
  40.4 1.2 %collective-permute-done.5.third_ref.refs_2_ = f32[8,128]{1,0:T(8,128)S(1)} collective-permute-done((f32[8,128]{1,0:T(8,128)S(1)}, f32[8,128]{1,0:T(8,128)S(1)}, u32[]{:S(2)}, u32[]{:S(2)}) %collective-permute-start.5) | collective-permute-done | bytes 4128 | tf_op jit(solution)/shard_map/ppermute | solution.py:54
  41.6 2.1 %collective-permute-done.4.second_ref.refs_1_ = f32[8,128]{1,0:T(8,128)S(1)} collective-permute-done((f32[8,128]{1,0:T(8,128)S(1)}, f32[8,128]{1,0:T(8,128)S(1)}, u32[]{:S(2)}, u32[]{:S(2)}) %collective-permute-start.4) | collective-permute-done | bytes 4128 | tf_op jit(solution)/shard_map/ppermute | solution.py:54
  43.7 4.5 %all-to-all-done.1.parts_ref = f32[32,32,256]{2,1,0:T(8,128)S(1)} async-done(((f32[32,32,256]{2,1,0:T(8,128)}), f32[32,32,256]{2,1,0:T(8,128)S(1)}, u32[]{:S(2)}, u32[]{:S(2)}) %all-to-all-start.1) | async-done | bytes 1048608 | tf_op jit(solution)/shard_map/all_to_all | solution.py:58
  48.2 0.1 shard_map.64.first_ref
  48.3 1.2 %collective-permute-start.11 = (f32[32,256]{1,0:T(8,128)S(1)}, f32[32,256]{1,0:T(8,128)S(1)}, u32[]{:S(2)}, u32[]{:S(2)}) collective-permute-start(f32[32,256]{1,0:T(8,128)S(1)} %shard_map.64.first_ref), channel_id=1, source_target_pairs={{0,32},{16,48},{32,0},{48,16},{1,33},{17,49},{33,1},{49,17},{2,34}... | collective-permute-start | bytes 98312 | tf_op jit(solution)/shard_map/ppermute | solution.py:54
  49.4 0.8 %collective-permute-start.10 = (f32[32,256]{1,0:T(8,128)S(1)}, f32[32,256]{1,0:T(8,128)S(1)}, u32[]{:S(2)}, u32[]{:S(2)}) collective-permute-start(f32[32,256]{1,0:T(8,128)S(1)} %shard_map.64.first_ref), channel_id=1, source_target_pairs={{0,16},{16,32},{32,48},{48,0},{1,17},{17,33},{33,49},{49,1},{2,18}... | collective-permute-start | bytes 98312 | tf_op jit(solution)/shard_map/ppermute | solution.py:54
  50.3 2.7 %collective-permute-start.9 = (f32[32,256]{1,0:T(8,128)S(1)}, f32[32,256]{1,0:T(8,128)S(1)}, u32[]{:S(2)}, u32[]{:S(2)}) collective-permute-start(f32[32,256]{1,0:T(8,128)S(1)} %shard_map.64.first_ref), channel_id=1, source_target_pairs={{0,48},{16,0},{32,16},{48,32},{1,49},{17,1},{33,17},{49,33},{2,50}... | collective-permute-start | bytes 98312 | tf_op jit(solution)/shard_map/ppermute | solution.py:54
  53.0 2.9 %shard_map.62 = (f32[32,32]{1,0:T(8,128)S(1)}, f32[32,64]{1,0:T(8,128)S(1)}, f32[32,64]{1,0:T(8,128)S(1)}) custom-call(f32[8,128]{1,0:T(8,128)S(1)} %shard_map.61.first_ref.refs_0_, f32[8,128]{1,0:T(8,128)S(1)} %collective-permute-done.4.second_ref.refs_1_, f32[8,128]{1,0:T(8,128)S(1)} %collective-permute-done.5.third_ref.refs_2_, ...), custom_call_target="tpu_custom_call" | custom-call | flops 1048576 | bytes 12582912 | tf_op jit(solution)/shard_map/pallas_call | solution.py:282
  55.9 0.0 collective-permute-done.11.fourth_ref
  55.9 0.0 collective-permute-done.10.third_ref
  55.9 0.0 collective-permute-done.9.second_ref
  55.9 0.3 shard_map.65
  56.2 18.1 %all_to_all.16.blocks_ref = f32[32,32,256]{2,1,0:T(8,128)S(1)} all-to-all(f32[32,32,256]{2,1,0:T(8,128)S(1)} %shard_map.65), channel_id=1, replica_groups=mesh['x'=4,'v'=4,'w'=2,'y'=4,'c'=2] {'w','y','x'}, dimensions={0} | all-to-all | bytes 2097152 | tf_op jit(solution)/shard_map/all_to_all | solution.py:58
  74.3 0.1 shard_map.66.q_ref
  74.4 6.1 %collective-permute-start.12 = (f32[32,8192]{1,0:T(8,128)S(1)}, f32[32,8192]{1,0:T(8,128)S(1)}, u32[]{:S(2)}, u32[]{:S(2)}) collective-permute-start(f32[32,8192]{1,0:T(8,128)S(1)} %shard_map.66.q_ref), channel_id=1, source_target_pairs={{0,1},{1,0},{2,3},{3,2},{4,5},{5,4},{6,7},{7,6},{8,9},{9,8},{10,11... | collective-permute-start | bytes 3145736 | tf_op jit(solution)/shard_map/ppermute | solution.py:50
  80.5 0.1 collective-permute-start.7
  80.6 1.6 %shard_map.67 = (bf16[1,2,64,8192]{3,2,1,0:T(8,128)(2,1)}, f32[2,32,8192]{2,1,0:T(8,128)}, f32[2,32,64]{2,1,0:T(8,128)}) custom-call(s32[1]{0:T(128)} %bitcast.core_ref, f32[32,64]{1,0:T(8,128)S(1)} %get-tuple-element.28.ortho_ref, f32[32,8192]{1,0:T(8,128)S(1)} %shard_map.66.q_ref, bf16[64,8192]{1,0:T(8,128)(2,1)S(1)} %get-tuple-element.29.merged_ref), custom_call_target="tpu_custom_call" | custom-call | flops 33554432 | bytes 4194304 | tf_op jit(solution)/shard_map/pallas_call | solution.py:327
  82.2 0.6 collective-permute-done.7.ortho_ref
  82.8 0.0 collective-permute-done.12.q_ref
  82.8 1.6 %shard_map.68 = (bf16[1,2,64,8192]{3,2,1,0:T(8,128)(2,1)}, f32[2,32,8192]{2,1,0:T(8,128)}, f32[2,32,64]{2,1,0:T(8,128)}) custom-call(s32[1]{0:T(128)} %bitcast.core_ref, f32[32,64]{1,0:T(8,128)S(1)} %collective-permute-done.7.ortho_ref, f32[32,8192]{1,0:T(8,128)S(1)} %collective-permute-done.12.q_ref, ...), custom_call_target="tpu_custom_call", output_to_operand_aliasing={{0}: (4, {}), {1}: (5, {}), {2}: (6, {})} | custom-call | flops 33554432 | bytes 4194304 | tf_op jit(solution)/shard_map/pallas_call | solution.py:327
  (2 shorter events, 0.0 us)
Async XLA Ops:
  3.5 4.2 %collective-permute-start = (f32[32,64]{1,0:T(8,128)S(1)}, f32[32,64]{1,0:T(8,128)S(1)}, u32[]{:S(2)}, u32[]{:S(2)}) collective-permute-start(f32[32,64]{1,0:T(8,128)S(1)} %get-tuple-element.24), channel_id=1, source_target_pairs={{0,1},{1,0},{2,3},{3,2},{4,5},{5,4},{6,7},{7,6},{8,9},{9,8},{10,11... | collective-permute-start | bytes 24584 | tf_op jit(solution)/shard_map/ppermute | solution.py:50
  7.8 22.1 %collective-permute-start.8 = (f32[64,8192]{1,0:T(8,128)S(1)}, f32[64,8192]{1,0:T(8,128)S(1)}, u32[]{:S(2)}, u32[]{:S(2)}) collective-permute-start(f32[64,8192]{1,0:T(8,128)S(1)} %get-tuple-element.30), channel_id=1, source_target_pairs={{0,1},{1,0},{2,3},{3,2},{4,5},{5,4},{6,7},{7,6},{8,9},{9,8},{10,11... | collective-permute-start | bytes 6291464 | tf_op jit(solution)/shard_map/ppermute | solution.py:50
  8.1 4.1 %collective-permute-start.3 = (f32[32,128]{1,0:T(8,128)S(1)}, f32[32,128]{1,0:T(8,128)S(1)}, u32[]{:S(2)}, u32[]{:S(2)}) collective-permute-start(f32[32,128]{1,0:T(8,128)S(1)} %pad_maximum_fusion.first_ref), channel_id=1, source_target_pairs={{0,128},{64,192},{128,0},{192,64},{1,129},{65,193},{129,1},{193,65... | collective-permute-start | bytes 49160 | tf_op jit(solution)/shard_map/ppermute | solution.py:54
  9.2 3.1 %collective-permute-start.2 = (f32[32,128]{1,0:T(8,128)S(1)}, f32[32,128]{1,0:T(8,128)S(1)}, u32[]{:S(2)}, u32[]{:S(2)}) collective-permute-start(f32[32,128]{1,0:T(8,128)S(1)} %pad_maximum_fusion.first_ref), channel_id=1, source_target_pairs={{0,192},{64,0},{128,64},{192,128},{1,193},{65,1},{129,65},{193,129... | collective-permute-start | bytes 49160 | tf_op jit(solution)/shard_map/ppermute | solution.py:54
  10.0 3.8 %collective-permute-start.1 = (f32[32,128]{1,0:T(8,128)S(1)}, f32[32,128]{1,0:T(8,128)S(1)}, u32[]{:S(2)}, u32[]{:S(2)}) collective-permute-start(f32[32,128]{1,0:T(8,128)S(1)} %pad_maximum_fusion.first_ref), channel_id=1, source_target_pairs={{0,64},{64,128},{128,192},{192,0},{1,65},{65,129},{129,193},{193,1... | collective-permute-start | bytes 49160 | tf_op jit(solution)/shard_map/ppermute | solution.py:54
  31.2 17.0 %all-to-all-start.1 = ((f32[32,32,256]{2,1,0:T(8,128)}), f32[32,32,256]{2,1,0:T(8,128)S(1)}, u32[]{:S(2)}, u32[]{:S(2)}) async-start(f32[32,32,256]{2,1,0:T(8,128)} %shard_map.63), calls=%async_computation.1 | async-start | bytes 2097152 | tf_op jit(solution)/shard_map/all_to_all | solution.py:58
  36.0 4.4 %collective-permute-start.6 = (f32[8,128]{1,0:T(8,128)S(1)}, f32[8,128]{1,0:T(8,128)S(1)}, u32[]{:S(2)}, u32[]{:S(2)}) collective-permute-start(f32[8,128]{1,0:T(8,128)S(1)} %shard_map.61.first_ref.refs_0_), channel_id=1, source_target_pairs={{0,4},{2,6},{4,0},{6,2},{1,5},{3,7},{5,1},{7,3},{8,12},{10,14},{12... | collective-permute-start | bytes 12296 | tf_op jit(solution)/shard_map/ppermute | solution.py:54
  38.8 2.8 %collective-permute-start.5 = (f32[8,128]{1,0:T(8,128)S(1)}, f32[8,128]{1,0:T(8,128)S(1)}, u32[]{:S(2)}, u32[]{:S(2)}) collective-permute-start(f32[8,128]{1,0:T(8,128)S(1)} %shard_map.61.first_ref.refs_0_), channel_id=1, source_target_pairs={{0,6},{2,0},{4,2},{6,4},{1,7},{3,1},{5,3},{7,5},{8,14},{10,8},{12,... | collective-permute-start | bytes 12296 | tf_op jit(solution)/shard_map/ppermute | solution.py:54
  39.6 4.1 %collective-permute-start.4 = (f32[8,128]{1,0:T(8,128)S(1)}, f32[8,128]{1,0:T(8,128)S(1)}, u32[]{:S(2)}, u32[]{:S(2)}) collective-permute-start(f32[8,128]{1,0:T(8,128)S(1)} %shard_map.61.first_ref.refs_0_), channel_id=1, source_target_pairs={{0,2},{2,4},{4,6},{6,0},{1,3},{3,5},{5,7},{7,1},{8,10},{10,12},{12... | collective-permute-start | bytes 12296 | tf_op jit(solution)/shard_map/ppermute | solution.py:54
  48.3 7.6 %collective-permute-start.11 = (f32[32,256]{1,0:T(8,128)S(1)}, f32[32,256]{1,0:T(8,128)S(1)}, u32[]{:S(2)}, u32[]{:S(2)}) collective-permute-start(f32[32,256]{1,0:T(8,128)S(1)} %shard_map.64.first_ref), channel_id=1, source_target_pairs={{0,32},{16,48},{32,0},{48,16},{1,33},{17,49},{33,1},{49,17},{2,34}... | collective-permute-start | bytes 98312 | tf_op jit(solution)/shard_map/ppermute | solution.py:54
  49.4 6.5 %collective-permute-start.10 = (f32[32,256]{1,0:T(8,128)S(1)}, f32[32,256]{1,0:T(8,128)S(1)}, u32[]{:S(2)}, u32[]{:S(2)}) collective-permute-start(f32[32,256]{1,0:T(8,128)S(1)} %shard_map.64.first_ref), channel_id=1, source_target_pairs={{0,16},{16,32},{32,48},{48,0},{1,17},{17,33},{33,49},{49,1},{2,18}... | collective-permute-start | bytes 98312 | tf_op jit(solution)/shard_map/ppermute | solution.py:54
  50.3 5.6 %collective-permute-start.9 = (f32[32,256]{1,0:T(8,128)S(1)}, f32[32,256]{1,0:T(8,128)S(1)}, u32[]{:S(2)}, u32[]{:S(2)}) collective-permute-start(f32[32,256]{1,0:T(8,128)S(1)} %shard_map.64.first_ref), channel_id=1, source_target_pairs={{0,48},{16,0},{32,16},{48,32},{1,49},{17,1},{33,17},{49,33},{2,50}... | collective-permute-start | bytes 98312 | tf_op jit(solution)/shard_map/ppermute | solution.py:54
  74.4 8.4 %collective-permute-start.12 = (f32[32,8192]{1,0:T(8,128)S(1)}, f32[32,8192]{1,0:T(8,128)S(1)}, u32[]{:S(2)}, u32[]{:S(2)}) collective-permute-start(f32[32,8192]{1,0:T(8,128)S(1)} %shard_map.66.q_ref), channel_id=1, source_target_pairs={{0,1},{1,0},{2,3},{3,2},{4,5},{5,4},{6,7},{7,6},{8,9},{9,8},{10,11... | collective-permute-start | bytes 3145736 | tf_op jit(solution)/shard_map/ppermute | solution.py:50
  80.5 2.3 %collective-permute-start.7 = (f32[32,64]{1,0:T(8,128)S(1)}, f32[32,64]{1,0:T(8,128)S(1)}, u32[]{:S(2)}, u32[]{:S(2)}) collective-permute-start(f32[32,64]{1,0:T(8,128)S(1)} %get-tuple-element.27), channel_id=1, source_target_pairs={{0,1},{1,0},{2,3},{3,2},{4,5},{5,4},{6,7},{7,6},{8,9},{9,8},{10,11... | collective-permute-start | bytes 24584 | tf_op jit(solution)/shard_map/ppermute | solution.py:50

commit v12 on v11

--- a/solution.py
+++ b/solution.py
@@ -353,7 +353,7 @@
     summed = sum_parts(exchange(terms, ("v", "w")))
 
     gram = packed_gram(summed)
-    grams = [gram] + shifts(gram, "y", NY)
+    grams = [gram] + shifts(gram, "y", NY, (3, 1, 2))
 
     half = exchange(right(summed, merged, received), ("w", "y", "x"))
     part = sum_parts(half, after=grams)

time: 84.7 us -> 84.7 us (level)
  starting transfers between devices: 25.9 us -> 27.1 us
  waiting for transfers between devices: 12.6 us -> 11.4 us
    ppermute x9, waiting for transfers between devices: 6.71 us -> 4.27 us  [shifts(): lax.ppermute(a, axis, [(i, (i + s) % size) for i in range(size)])]
    all_to_all x1, waiting for transfers between devices: 4.48 us -> 5.71 us  [exchange(): return lax.all_to_all(a, axes, 0, 0)]
    ppermute x9, starting transfers between devices: 11.4 us -> 12.6 us  [shifts(): lax.ppermute(a, axis, [(i, (i + s) % size) for i in range(size)])]
  transfers between devices with their start and end apart: 14 -> 14, of which waited for: 8 -> 6; matrix products, arithmetic and copies ran while one was open for 0% -> 0% of each run, Pallas kernels for 6% -> 6%
where the time goes in v12:
time: 84.7 us; the launch traced here: 84.4 us
  blocking collectives  34.1 us (40%)
  starting transfers between devices  27.1 us (32%)
  waiting for transfers between devices  11.4 us (13%)
  Pallas kernels  10.9 us (13%)
    all_to_all x2, blocking collectives, exchange(): return lax.all_to_all(a, axes, 0, 0)  34.1 us
    ppermute x9, starting transfers between devices, shifts(): lax.ppermute(a, axis, [(i, (i + s) % size) for i in range(size)])  12.6 us
    ppermute x4, starting transfers between devices, swap(): return lax.ppermute(a, 'c', [(0, 1), (1, 0)])  9.87 us
    all_to_all x1, waiting for transfers between devices, exchange(): return lax.all_to_all(a, axes, 0, 0)  5.71 us
    all_to_all x1, starting transfers between devices, exchange(): return lax.all_to_all(a, axes, 0, 0)  4.59 us
    ppermute x9, waiting for transfers between devices, shifts(): lax.ppermute(a, axis, [(i, (i + s) % size) for i in range(size)])  4.27 us
    pallas_call x2, Pallas kernels, tail(): pl.pallas_call(functools.partial(tail_kernel, bool(before)), in_specs=[IN...  3.22 us
    pallas_call x1, Pallas kernels, factors(): pl.pallas_call(factor_kernel, in_specs=[IN_VMEM] * (NY + 1), out_specs=[I...  2.89 us
  transfers between devices with their start and end apart: 14, of which 6 were waited for; matrix products, arithmetic and copies ran while one was open for 0% of the time, Pallas kernels for 6%

profile of v12, /device:TPU:1, one launch (start us, length us, event | category | flops | bytes accessed | tf_op | source)
XLA Modules:
  0.0 84.4 jit_solution(15616589925638381887)
XLA Ops:
  0.6 2.9 %shard_map.58 = (bf16[64,8192]{1,0:T(8,128)(2,1)S(1)}, bf16[64,8192]{1,0:T(8,128)(2,1)S(1)}, f32[64,8192]{1,0:T(8,128)S(1)}, f32[32,64]{1,0:T(8,128)S(1)}, f32[32,64]{1,0:T(8,128)S(1)}) custom-call(s32[1]{0:T(128)} %bitcast.core_ref, bf16[1,2,64,8192]{3,2,1,0:T(8,128)(2,1)} %grads_hbm.1, bf16[1,2,64,8192]{3,2,1,0:T(8,128)(2,1)} %errors_hbm.1, ...), custom_call_target="tpu_custom_call" | custom-call | flops 134217728 | bytes 9437184 | tf_op jit(solution)/shard_map/pallas_call | solution.py:119
  3.5 3.3 %collective-permute-start = (f32[32,64]{1,0:T(8,128)S(1)}, f32[32,64]{1,0:T(8,128)S(1)}, u32[]{:S(2)}, u32[]{:S(2)}) collective-permute-start(f32[32,64]{1,0:T(8,128)S(1)} %get-tuple-element.24), channel_id=1, source_target_pairs={{0,1},{1,0},{2,3},{3,2},{4,5},{5,4},{6,7},{7,6},{8,9},{9,8},{10,11... | collective-permute-start | bytes 24584 | tf_op jit(solution)/shard_map/ppermute | solution.py:50
  6.9 0.8 collective-permute-done
  7.7 0.1 pad_maximum_fusion.first_ref
  7.8 0.4 collective-permute-start.8
  8.1 1.0 %collective-permute-start.3 = (f32[32,128]{1,0:T(8,128)S(1)}, f32[32,128]{1,0:T(8,128)S(1)}, u32[]{:S(2)}, u32[]{:S(2)}) collective-permute-start(f32[32,128]{1,0:T(8,128)S(1)} %pad_maximum_fusion.first_ref), channel_id=1, source_target_pairs={{0,128},{64,192},{128,0},{192,64},{1,129},{65,193},{129,1},{193,65... | collective-permute-start | bytes 49160 | tf_op jit(solution)/shard_map/ppermute | solution.py:54
  9.2 0.9 %collective-permute-start.2 = (f32[32,128]{1,0:T(8,128)S(1)}, f32[32,128]{1,0:T(8,128)S(1)}, u32[]{:S(2)}, u32[]{:S(2)}) collective-permute-start(f32[32,128]{1,0:T(8,128)S(1)} %pad_maximum_fusion.first_ref), channel_id=1, source_target_pairs={{0,192},{64,0},{128,64},{192,128},{1,193},{65,1},{129,65},{193,129... | collective-permute-start | bytes 49160 | tf_op jit(solution)/shard_map/ppermute | solution.py:54
  10.0 0.6 collective-permute-start.1
  10.6 1.6 %collective-permute-done.3.fourth_ref = f32[32,128]{1,0:T(8,128)S(1)} collective-permute-done((f32[32,128]{1,0:T(8,128)S(1)}, f32[32,128]{1,0:T(8,128)S(1)}, u32[]{:S(2)}, u32[]{:S(2)}) %collective-permute-start.3) | collective-permute-done | bytes 16416 | tf_op jit(solution)/shard_map/ppermute | solution.py:54
  12.2 0.0 collective-permute-done.2.third_ref
  12.2 1.6 %collective-permute-done.1.second_ref = f32[32,128]{1,0:T(8,128)S(1)} collective-permute-done((f32[32,128]{1,0:T(8,128)S(1)}, f32[32,128]{1,0:T(8,128)S(1)}, u32[]{:S(2)}, u32[]{:S(2)}) %collective-permute-start.1) | collective-permute-done | bytes 16416 | tf_op jit(solution)/shard_map/ppermute | solution.py:54
  13.8 16.0 %all_to_all.15.parts_ref = f32[8,32,128]{2,1,0:T(8,128)S(1)} all-to-all(f32[8,32,128]{2,1,0:T(8,128)S(1)} %shard_map.59), channel_id=1, replica_groups=mesh['x'=4,'v'=4,'w'=2,'y'=4,'c'=2] {'v','w'}, dimensions={0} | all-to-all | bytes 262144 | tf_op jit(solution)/shard_map/all_to_all | solution.py:58
  29.9 0.0 collective-permute-done.8.received_ref
  29.9 1.3 %shard_map.63 = f32[32,32,256]{2,1,0:T(8,128)} custom-call(f32[32,128]{1,0:T(8,128)S(1)} %shard_map.60.summed_ref, bf16[64,8192]{1,0:T(8,128)(2,1)S(1)} %get-tuple-element.29.merged_ref, f32[64,8192]{1,0:T(8,128)S(1)} %collective-permute-done.8.received_ref), custom_call_target="tpu_custom_call" | custom-call | flops 201326592 | bytes 4194304 | tf_op jit(solution)/shard_map/pallas_call | solution.py:225
  31.2 4.6 %all-to-all-start.1 = ((f32[32,32,256]{2,1,0:T(8,128)}), f32[32,32,256]{2,1,0:T(8,128)S(1)}, u32[]{:S(2)}, u32[]{:S(2)}) async-start(f32[32,32,256]{2,1,0:T(8,128)} %shard_map.63), calls=%async_computation.1 | async-start | bytes 2097152 | tf_op jit(solution)/shard_map/all_to_all | solution.py:58
  35.8 0.2 shard_map.61.first_ref.refs_0_
  36.0 2.8 %collective-permute-start.6 = (f32[8,128]{1,0:T(8,128)S(1)}, f32[8,128]{1,0:T(8,128)S(1)}, u32[]{:S(2)}, u32[]{:S(2)}) collective-permute-start(f32[8,128]{1,0:T(8,128)S(1)} %shard_map.61.first_ref.refs_0_), channel_id=1, source_target_pairs={{0,4},{2,6},{4,0},{6,2},{1,5},{3,7},{5,1},{7,3},{8,12},{10,14},{12... | collective-permute-start | bytes 12296 | tf_op jit(solution)/shard_map/ppermute | solution.py:54
  38.8 0.3 collective-permute-start.5
  39.0 2.4 %collective-permute-start.4 = (f32[8,128]{1,0:T(8,128)S(1)}, f32[8,128]{1,0:T(8,128)S(1)}, u32[]{:S(2)}, u32[]{:S(2)}) collective-permute-start(f32[8,128]{1,0:T(8,128)S(1)} %shard_map.61.first_ref.refs_0_), channel_id=1, source_target_pairs={{0,6},{2,0},{4,2},{6,4},{1,7},{3,1},{5,3},{7,5},{8,14},{10,8},{12,... | collective-permute-start | bytes 12296 | tf_op jit(solution)/shard_map/ppermute | solution.py:54
  41.4 0.0 collective-permute-done.6.fourth_ref.refs_3_
  41.4 1.1 %collective-permute-done.5.third_ref.refs_2_ = f32[8,128]{1,0:T(8,128)S(1)} collective-permute-done((f32[8,128]{1,0:T(8,128)S(1)}, f32[8,128]{1,0:T(8,128)S(1)}, u32[]{:S(2)}, u32[]{:S(2)}) %collective-permute-start.5) | collective-permute-done | bytes 4128 | tf_op jit(solution)/shard_map/ppermute | solution.py:54
  42.5 0.0 collective-permute-done.4.second_ref.refs_1_
  42.5 5.7 %all-to-all-done.1.parts_ref = f32[32,32,256]{2,1,0:T(8,128)S(1)} async-done(((f32[32,32,256]{2,1,0:T(8,128)}), f32[32,32,256]{2,1,0:T(8,128)S(1)}, u32[]{:S(2)}, u32[]{:S(2)}) %all-to-all-start.1) | async-done | bytes 1048608 | tf_op jit(solution)/shard_map/all_to_all | solution.py:58
  48.2 0.1 shard_map.64.first_ref
  48.3 1.2 %collective-permute-start.11 = (f32[32,256]{1,0:T(8,128)S(1)}, f32[32,256]{1,0:T(8,128)S(1)}, u32[]{:S(2)}, u32[]{:S(2)}) collective-permute-start(f32[32,256]{1,0:T(8,128)S(1)} %shard_map.64.first_ref), channel_id=1, source_target_pairs={{0,32},{16,48},{32,0},{48,16},{1,33},{17,49},{33,1},{49,17},{2,34}... | collective-permute-start | bytes 98312 | tf_op jit(solution)/shard_map/ppermute | solution.py:54
  49.4 0.8 %collective-permute-start.10 = (f32[32,256]{1,0:T(8,128)S(1)}, f32[32,256]{1,0:T(8,128)S(1)}, u32[]{:S(2)}, u32[]{:S(2)}) collective-permute-start(f32[32,256]{1,0:T(8,128)S(1)} %shard_map.64.first_ref), channel_id=1, source_target_pairs={{0,16},{16,32},{32,48},{48,0},{1,17},{17,33},{33,49},{49,1},{2,18}... | collective-permute-start | bytes 98312 | tf_op jit(solution)/shard_map/ppermute | solution.py:54
  50.3 2.7 %collective-permute-start.9 = (f32[32,256]{1,0:T(8,128)S(1)}, f32[32,256]{1,0:T(8,128)S(1)}, u32[]{:S(2)}, u32[]{:S(2)}) collective-permute-start(f32[32,256]{1,0:T(8,128)S(1)} %shard_map.64.first_ref), channel_id=1, source_target_pairs={{0,48},{16,0},{32,16},{48,32},{1,49},{17,1},{33,17},{49,33},{2,50}... | collective-permute-start | bytes 98312 | tf_op jit(solution)/shard_map/ppermute | solution.py:54
  53.0 2.9 %shard_map.62 = (f32[32,32]{1,0:T(8,128)S(1)}, f32[32,64]{1,0:T(8,128)S(1)}, f32[32,64]{1,0:T(8,128)S(1)}) custom-call(f32[8,128]{1,0:T(8,128)S(1)} %shard_map.61.first_ref.refs_0_, f32[8,128]{1,0:T(8,128)S(1)} %collective-permute-done.4.second_ref.refs_1_, f32[8,128]{1,0:T(8,128)S(1)} %collective-permute-done.5.third_ref.refs_2_, ...), custom_call_target="tpu_custom_call" | custom-call | flops 1048576 | bytes 12582912 | tf_op jit(solution)/shard_map/pallas_call | solution.py:282
  55.9 0.0 collective-permute-done.11.fourth_ref
  55.9 0.0 collective-permute-done.10.third_ref
  55.9 0.0 collective-permute-done.9.second_ref
  55.9 0.3 shard_map.65
  56.2 18.1 %all_to_all.16.blocks_ref = f32[32,32,256]{2,1,0:T(8,128)S(1)} all-to-all(f32[32,32,256]{2,1,0:T(8,128)S(1)} %shard_map.65), channel_id=1, replica_groups=mesh['x'=4,'v'=4,'w'=2,'y'=4,'c'=2] {'w','y','x'}, dimensions={0} | all-to-all | bytes 2097152 | tf_op jit(solution)/shard_map/all_to_all | solution.py:58
  74.3 0.1 shard_map.66.q_ref
  74.4 6.1 %collective-permute-start.12 = (f32[32,8192]{1,0:T(8,128)S(1)}, f32[32,8192]{1,0:T(8,128)S(1)}, u32[]{:S(2)}, u32[]{:S(2)}) collective-permute-start(f32[32,8192]{1,0:T(8,128)S(1)} %shard_map.66.q_ref), channel_id=1, source_target_pairs={{0,1},{1,0},{2,3},{3,2},{4,5},{5,4},{6,7},{7,6},{8,9},{9,8},{10,11... | collective-permute-start | bytes 3145736 | tf_op jit(solution)/shard_map/ppermute | solution.py:50
  80.5 0.1 collective-permute-start.7
  80.6 1.6 %shard_map.67 = (bf16[1,2,64,8192]{3,2,1,0:T(8,128)(2,1)}, f32[2,32,8192]{2,1,0:T(8,128)}, f32[2,32,64]{2,1,0:T(8,128)}) custom-call(s32[1]{0:T(128)} %bitcast.core_ref, f32[32,64]{1,0:T(8,128)S(1)} %get-tuple-element.28.ortho_ref, f32[32,8192]{1,0:T(8,128)S(1)} %shard_map.66.q_ref, bf16[64,8192]{1,0:T(8,128)(2,1)S(1)} %get-tuple-element.29.merged_ref), custom_call_target="tpu_custom_call" | custom-call | flops 33554432 | bytes 4194304 | tf_op jit(solution)/shard_map/pallas_call | solution.py:327
  82.2 0.6 collective-permute-done.7.ortho_ref
  82.8 0.0 collective-permute-done.12.q_ref
  82.8 1.6 %shard_map.68 = (bf16[1,2,64,8192]{3,2,1,0:T(8,128)(2,1)}, f32[2,32,8192]{2,1,0:T(8,128)}, f32[2,32,64]{2,1,0:T(8,128)}) custom-call(s32[1]{0:T(128)} %bitcast.core_ref, f32[32,64]{1,0:T(8,128)S(1)} %collective-permute-done.7.ortho_ref, f32[32,8192]{1,0:T(8,128)S(1)} %collective-permute-done.12.q_ref, ...), custom_call_target="tpu_custom_call", output_to_operand_aliasing={{0}: (4, {}), {1}: (5, {}), {2}: (6, {})} | custom-call | flops 33554432 | bytes 4194304 | tf_op jit(solution)/shard_map/pallas_call | solution.py:327
  (2 shorter events, 0.0 us)
Async XLA Ops:
  3.5 4.2 %collective-permute-start = (f32[32,64]{1,0:T(8,128)S(1)}, f32[32,64]{1,0:T(8,128)S(1)}, u32[]{:S(2)}, u32[]{:S(2)}) collective-permute-start(f32[32,64]{1,0:T(8,128)S(1)} %get-tuple-element.24), channel_id=1, source_target_pairs={{0,1},{1,0},{2,3},{3,2},{4,5},{5,4},{6,7},{7,6},{8,9},{9,8},{10,11... | collective-permute-start | bytes 24584 | tf_op jit(solution)/shard_map/ppermute | solution.py:50
  7.8 22.1 %collective-permute-start.8 = (f32[64,8192]{1,0:T(8,128)S(1)}, f32[64,8192]{1,0:T(8,128)S(1)}, u32[]{:S(2)}, u32[]{:S(2)}) collective-permute-start(f32[64,8192]{1,0:T(8,128)S(1)} %get-tuple-element.30), channel_id=1, source_target_pairs={{0,1},{1,0},{2,3},{3,2},{4,5},{5,4},{6,7},{7,6},{8,9},{9,8},{10,11... | collective-permute-start | bytes 6291464 | tf_op jit(solution)/shard_map/ppermute | solution.py:50
  8.1 4.1 %collective-permute-start.3 = (f32[32,128]{1,0:T(8,128)S(1)}, f32[32,128]{1,0:T(8,128)S(1)}, u32[]{:S(2)}, u32[]{:S(2)}) collective-permute-start(f32[32,128]{1,0:T(8,128)S(1)} %pad_maximum_fusion.first_ref), channel_id=1, source_target_pairs={{0,128},{64,192},{128,0},{192,64},{1,129},{65,193},{129,1},{193,65... | collective-permute-start | bytes 49160 | tf_op jit(solution)/shard_map/ppermute | solution.py:54
  9.2 3.1 %collective-permute-start.2 = (f32[32,128]{1,0:T(8,128)S(1)}, f32[32,128]{1,0:T(8,128)S(1)}, u32[]{:S(2)}, u32[]{:S(2)}) collective-permute-start(f32[32,128]{1,0:T(8,128)S(1)} %pad_maximum_fusion.first_ref), channel_id=1, source_target_pairs={{0,192},{64,0},{128,64},{192,128},{1,193},{65,1},{129,65},{193,129... | collective-permute-start | bytes 49160 | tf_op jit(solution)/shard_map/ppermute | solution.py:54
  10.0 3.8 %collective-permute-start.1 = (f32[32,128]{1,0:T(8,128)S(1)}, f32[32,128]{1,0:T(8,128)S(1)}, u32[]{:S(2)}, u32[]{:S(2)}) collective-permute-start(f32[32,128]{1,0:T(8,128)S(1)} %pad_maximum_fusion.first_ref), channel_id=1, source_target_pairs={{0,64},{64,128},{128,192},{192,0},{1,65},{65,129},{129,193},{193,1... | collective-permute-start | bytes 49160 | tf_op jit(solution)/shard_map/ppermute | solution.py:54
  31.2 17.0 %all-to-all-start.1 = ((f32[32,32,256]{2,1,0:T(8,128)}), f32[32,32,256]{2,1,0:T(8,128)S(1)}, u32[]{:S(2)}, u32[]{:S(2)}) async-start(f32[32,32,256]{2,1,0:T(8,128)} %shard_map.63), calls=%async_computation.1 | async-start | bytes 2097152 | tf_op jit(solution)/shard_map/all_to_all | solution.py:58
  36.0 5.4 %collective-permute-start.6 = (f32[8,128]{1,0:T(8,128)S(1)}, f32[8,128]{1,0:T(8,128)S(1)}, u32[]{:S(2)}, u32[]{:S(2)}) collective-permute-start(f32[8,128]{1,0:T(8,128)S(1)} %shard_map.61.first_ref.refs_0_), channel_id=1, source_target_pairs={{0,4},{2,6},{4,0},{6,2},{1,5},{3,7},{5,1},{7,3},{8,12},{10,14},{12... | collective-permute-start | bytes 12296 | tf_op jit(solution)/shard_map/ppermute | solution.py:54
  38.8 3.7 %collective-permute-start.5 = (f32[8,128]{1,0:T(8,128)S(1)}, f32[8,128]{1,0:T(8,128)S(1)}, u32[]{:S(2)}, u32[]{:S(2)}) collective-permute-start(f32[8,128]{1,0:T(8,128)S(1)} %shard_map.61.first_ref.refs_0_), channel_id=1, source_target_pairs={{0,2},{2,4},{4,6},{6,0},{1,3},{3,5},{5,7},{7,1},{8,10},{10,12},{12... | collective-permute-start | bytes 12296 | tf_op jit(solution)/shard_map/ppermute | solution.py:54
  39.0 3.5 %collective-permute-start.4 = (f32[8,128]{1,0:T(8,128)S(1)}, f32[8,128]{1,0:T(8,128)S(1)}, u32[]{:S(2)}, u32[]{:S(2)}) collective-permute-start(f32[8,128]{1,0:T(8,128)S(1)} %shard_map.61.first_ref.refs_0_), channel_id=1, source_target_pairs={{0,6},{2,0},{4,2},{6,4},{1,7},{3,1},{5,3},{7,5},{8,14},{10,8},{12,... | collective-permute-start | bytes 12296 | tf_op jit(solution)/shard_map/ppermute | solution.py:54
  48.3 7.6 %collective-permute-start.11 = (f32[32,256]{1,0:T(8,128)S(1)}, f32[32,256]{1,0:T(8,128)S(1)}, u32[]{:S(2)}, u32[]{:S(2)}) collective-permute-start(f32[32,256]{1,0:T(8,128)S(1)} %shard_map.64.first_ref), channel_id=1, source_target_pairs={{0,32},{16,48},{32,0},{48,16},{1,33},{17,49},{33,1},{49,17},{2,34}... | collective-permute-start | bytes 98312 | tf_op jit(solution)/shard_map/ppermute | solution.py:54
  49.4 6.5 %collective-permute-start.10 = (f32[32,256]{1,0:T(8,128)S(1)}, f32[32,256]{1,0:T(8,128)S(1)}, u32[]{:S(2)}, u32[]{:S(2)}) collective-permute-start(f32[32,256]{1,0:T(8,128)S(1)} %shard_map.64.first_ref), channel_id=1, source_target_pairs={{0,16},{16,32},{32,48},{48,0},{1,17},{17,33},{33,49},{49,1},{2,18}... | collective-permute-start | bytes 98312 | tf_op jit(solution)/shard_map/ppermute | solution.py:54
  50.3 5.6 %collective-permute-start.9 = (f32[32,256]{1,0:T(8,128)S(1)}, f32[32,256]{1,0:T(8,128)S(1)}, u32[]{:S(2)}, u32[]{:S(2)}) collective-permute-start(f32[32,256]{1,0:T(8,128)S(1)} %shard_map.64.first_ref), channel_id=1, source_target_pairs={{0,48},{16,0},{32,16},{48,32},{1,49},{17,1},{33,17},{49,33},{2,50}... | collective-permute-start | bytes 98312 | tf_op jit(solution)/shard_map/ppermute | solution.py:54
  74.4 8.4 %collective-permute-start.12 = (f32[32,8192]{1,0:T(8,128)S(1)}, f32[32,8192]{1,0:T(8,128)S(1)}, u32[]{:S(2)}, u32[]{:S(2)}) collective-permute-start(f32[32,8192]{1,0:T(8,128)S(1)} %shard_map.66.q_ref), channel_id=1, source_target_pairs={{0,1},{1,0},{2,3},{3,2},{4,5},{5,4},{6,7},{7,6},{8,9},{9,8},{10,11... | collective-permute-start | bytes 3145736 | tf_op jit(solution)/shard_map/ppermute | solution.py:50
  80.5 2.3 %collective-permute-start.7 = (f32[32,64]{1,0:T(8,128)S(1)}, f32[32,64]{1,0:T(8,128)S(1)}, u32[]{:S(2)}, u32[]{:S(2)}) collective-permute-start(f32[32,64]{1,0:T(8,128)S(1)} %get-tuple-element.27), channel_id=1, source_target_pairs={{0,1},{1,0},{2,3},{3,2},{4,5},{5,4},{6,7},{7,6},{8,9},{9,8},{10,11... | collective-permute-start | bytes 24584 | tf_op jit(solution)/shard_map/ppermute | solution.py:50
